TPU v7x, 32 devices: a whole 2x2x4 slice. The times are simulated.
32 devices in a mesh: fsdp: 4 (over x, core), dp: 8 (over z, y).
Axes of the slice: x: 2, y: 2, z: 4, core: 2. Of those that a mesh axis runs over, the one named last changes fastest.
Arguments:
- block_input: bfloat16 [8, 1024, 768], P('dp', 'fsdp'), may hold values from -6 to 6
- out_cotangent: bfloat16 [8, 1024, 768], P('dp', 'fsdp'), may hold values from -6 to 6
- doc_lengths: int32 [8, 4], P('dp'), may hold values from 1 to 1021, as said below
- norm_gain: bfloat16 [768], P('fsdp'), may hold values from 0.5 to 1.5
- in_weight: bfloat16 [768, 3352], P('fsdp'), may hold values from -0.21875 to 0.21875
- conv_weight: bfloat16 [4, 1792], P(None, 'fsdp'), may hold values from -3 to 3
- conv_bias: bfloat16 [1792], P('fsdp'), may hold values from -2 to 2
- step_bias: bfloat16 [24], P('fsdp'), may hold values from -6.5 to -2.1875
- decay_log: bfloat16 [24], P('fsdp'), may hold values from -4.5 to 1
- skip_gain: bfloat16 [24], P('fsdp'), may hold values from 0.5 to 1.5
- out_gain: bfloat16 [1536], P('fsdp'), may hold values from 0.5 to 1.5
- out_weight: bfloat16 [1536, 768], P('fsdp'), may hold values from -0.15625 to 0.15625
Outputs:
- block_output: bfloat16 [8, 1024, 768], P('dp', 'fsdp')
- input_grad: bfloat16 [8, 1024, 768], P('dp', 'fsdp')
- grad_norm_gain: float32 [768], P('fsdp')
- grad_in_weight: float32 [768, 3352], P('fsdp')
- grad_conv_weight: float32 [4, 1792], P(None, 'fsdp')
- grad_conv_bias: float32 [1792], P('fsdp')
- grad_step_bias: float32 [24], P('fsdp')
- grad_decay_log: float32 [24], P('fsdp')
- grad_skip_gain: float32 [24], P('fsdp')
- grad_out_gain: float32 [1536], P('fsdp')
- grad_out_weight: float32 [1536, 768], P('fsdp')
Inputs may be any that keep to these rules, and one draw needn't show every extreme that they name: `doc_lengths`: row q lists the lengths of the 4 documents packed, in order, into sequence q, summing to 1024: the first ends within the sequence's first 256 positions and the last two begin within its last 256 positions.
All inputs are finite; a program needn't handle non-finite values.
Results may differ from a plain program's by a relative error of at most 0.019.
Values may be sent and summed in bfloat16 or wider, within the bound.
No kernel may reach another device: no remote copies, remote signals or barrier semaphores. Data moves between devices by JAX's collectives and lax.ppermute only.
A program may use at most 128 MiB of HBM per device.

v0:
```python
import jax
import jax.numpy as jnp
from jax import lax
from jax.sharding import PartitionSpec as P

H = 24
P_SIZE = 64
N = 128
KCONV = 4
BLOCK = 256
DI = 1536
CONVCH = 1792


EPSILON = 1e-05
HIGHEST = lax.Precision.HIGHEST


def passed_along(value, axis, steps):
    count = lax.axis_size(axis)
    leading, last = (max(0, -steps), min(count, count - steps))
    return lax.ppermute(value, axis, [(source, source + steps) for source in range(leading, last)])


def entering(x, axis, join, neutral, backward):
    count = lax.axis_size(axis)
    place = lax.axis_index(axis)
    ahead = count - 1 - place if backward else place
    gathered = jax.tree.map(
        lambda a, kind: lax.all_gather(a.astype(kind), axis), x, (jnp.bfloat16, jnp.bfloat16)
    )
    state = jax.tree.map(lambda a, e: jnp.zeros_like(a) + jnp.asarray(e, a.dtype), x, neutral)

    def one(hop, state):
        source = count - 1 - hop if backward else hop
        return join(
            state,
            jax.tree.map(
                lambda a, own: lax.dynamic_index_in_dim(a, source, 0, False).astype(own.dtype),
                gathered,
                x,
            ),
        )

    return lax.fori_loop(0, ahead, one, state)


def silu_grad(value):
    sigma = jax.nn.sigmoid(value)
    return sigma * (1.0 + value * (1.0 - sigma))


def lower_tri(length):
    rows_iota = lax.broadcasted_iota(jnp.int32, (length, length), 0)
    cols_iota = lax.broadcasted_iota(jnp.int32, (length, length), 1)
    return (rows_iota >= cols_iota).astype(jnp.float32)


def block_terms(log_decay, segment, seg_before):
    length = segment.shape[0]
    lower_mask = lower_tri(length)
    cumulative = jnp.dot(lower_mask, log_decay, precision=HIGHEST)
    same_mask = lower_mask * (segment[:, None] == segment[None, :]).astype(jnp.float32)
    differences = cumulative.T[:, :, None] - cumulative.T[:, None, :]
    decay_table = jnp.exp(jnp.where(same_mask[None] > 0, differences, 0.0)) * same_mask[None]
    enter_rate = jnp.exp(cumulative) * (segment == seg_before).astype(jnp.float32)[:, None]
    tail_sum = cumulative[-1]
    same_last = (segment == segment[-1]).astype(jnp.float32)
    end_decay = jnp.exp(tail_sum[None, :] - cumulative) * same_last[:, None]
    keep_rate = jnp.exp(tail_sum) * (segment[-1] == seg_before).astype(jnp.float32)
    return (lower_mask, decay_table, enter_rate, end_decay, keep_rate)


def block_forward(fields):
    heads_full, heads_low, keys_low, query_low, step_size, log_decay, segment, seg_before = fields
    lower_mask, decay_table, enter_rate, end_decay, keep_rate = block_terms(
        log_decay, segment, seg_before
    )
    gram_matrix = jnp.dot(query_low, keys_low.T, preferred_element_type=jnp.float32)
    weights = (gram_matrix[None] * decay_table * step_size.T[:, None, :]).astype(jnp.bfloat16)
    intra_out = jnp.einsum("hts,shp->thp", weights, heads_low, preferred_element_type=jnp.float32)
    weighted = (heads_full * (end_decay * step_size)[:, :, None]).astype(jnp.bfloat16)
    local_state = jnp.einsum("shp,sn->hpn", weighted, keys_low, preferred_element_type=jnp.float32)
    return (intra_out, local_state, keep_rate, enter_rate)


def block_backward(fields, rate_values):
    (
        heads_full,
        heads_low,
        keys_low,
        query_low,
        step_size,
        log_decay,
        segment,
        seg_before,
        start_state,
        grad_ssm,
        end_grad,
    ) = fields
    lower_mask, decay_table, enter_rate, end_decay, keep_rate = block_terms(
        log_decay, segment, seg_before
    )
    gram_matrix = jnp.dot(query_low, keys_low.T, preferred_element_type=jnp.float32)
    step_row = step_size.T[:, None, :]
    weights = (gram_matrix[None] * decay_table * step_row).astype(jnp.bfloat16)
    grad_table = jnp.einsum("thp,shp->hts", grad_ssm, heads_low, preferred_element_type=jnp.float32)
    grad_heads = jnp.einsum("hts,thp->shp", weights, grad_ssm, preferred_element_type=jnp.float32)
    common = grad_table * decay_table
    grad_gram = jnp.sum(common * step_row, axis=0).astype(jnp.bfloat16)
    grad_query = jnp.dot(grad_gram, keys_low, preferred_element_type=jnp.float32)
    grad_keys = jnp.dot(grad_gram.T, query_low, preferred_element_type=jnp.float32)
    grad_diff = common * gram_matrix[None] * step_row
    grad_cumul = (jnp.sum(grad_diff, axis=2) - jnp.sum(grad_diff, axis=1)).T
    grad_step = jnp.sum(common * gram_matrix[None], axis=1).T
    start_low = start_state.astype(jnp.bfloat16)
    state_out = jnp.einsum("tn,hpn->thp", query_low, start_low, preferred_element_type=jnp.float32)
    grad_cumul = (
        grad_cumul + jnp.sum(grad_ssm.astype(jnp.float32) * state_out, axis=-1) * enter_rate
    )
    through_state = jnp.einsum(
        "thp,hpn->thn", grad_ssm, start_low, preferred_element_type=jnp.float32
    )
    grad_query = grad_query + jnp.sum(enter_rate[:, :, None] * through_state, axis=1)
    end_low = end_grad.astype(jnp.bfloat16)
    scaled_steps = end_decay * step_size
    weighted = (heads_full * scaled_steps[:, :, None]).astype(jnp.bfloat16)
    grad_weighted = jnp.einsum("hpn,sn->shp", end_low, keys_low, preferred_element_type=jnp.float32)
    grad_keys = grad_keys + jnp.einsum(
        "hpn,shp->sn", end_low, weighted, preferred_element_type=jnp.float32
    )
    grad_heads_full = grad_weighted * scaled_steps[:, :, None]
    grad_end = jnp.sum(grad_weighted * heads_full, axis=-1)
    grad_step = grad_step + grad_end * end_decay
    end_terms = grad_end * scaled_steps
    grad_tail = (
        jnp.sum(end_terms, axis=0) + jnp.sum(end_grad * start_state, axis=(1, 2)) * keep_rate
    )
    last_row = (jnp.arange(segment.shape[0]) == segment.shape[0] - 1).astype(jnp.float32)
    grad_cumul = grad_cumul - end_terms + last_row[:, None] * grad_tail[None, :]
    grad_log = jnp.dot(lower_mask.T, grad_cumul, precision=HIGHEST)
    grad_step = grad_step + grad_log * rate_values[None, :]
    grad_rate = jnp.sum(grad_log * step_size, axis=0)
    return (grad_heads + grad_heads_full, grad_keys, grad_query, grad_step, grad_rate)


def state_combine(earlier, later):
    return (earlier[0] * later[0], earlier[1] * later[0][..., None, None] + later[1])


def grad_combine(earlier, later):
    return (later[0] * earlier[0], later[1] + later[0][..., None, None] * earlier[1])


def local(
    block_input,
    out_cotangent,
    doc_lengths,
    norm_gain,
    in_weight,
    conv_weight,
    conv_bias,
    step_bias,
    decay_log,
    skip_gain,
    out_gain,
    out_weight,
):
    seq_count, tok_count, model_width = block_input.shape
    block_count = tok_count // BLOCK
    flat_blocks = seq_count * block_count
    device_index = lax.axis_index("fsdp")
    full_weights = (
        lax.all_gather(norm_gain, "fsdp", axis=0, tiled=True),
        lax.all_gather(in_weight, "fsdp", axis=0, tiled=True),
        lax.all_gather(conv_weight, "fsdp", axis=1, tiled=True),
        lax.all_gather(conv_bias, "fsdp", axis=0, tiled=True),
        lax.all_gather(step_bias, "fsdp", axis=0, tiled=True),
        lax.all_gather(decay_log, "fsdp", axis=0, tiled=True),
        lax.all_gather(skip_gain, "fsdp", axis=0, tiled=True),
        lax.all_gather(out_gain, "fsdp", axis=0, tiled=True),
        lax.all_gather(out_weight, "fsdp", axis=0, tiled=True),
    )
    positions = device_index * tok_count + jnp.arange(-(KCONV - 1), tok_count, dtype=jnp.int32)
    bounds = jnp.cumsum(doc_lengths, axis=1)[:, :-1]
    segment_ext = jnp.sum(
        (positions[None, :, None] >= bounds[:, None, :]).astype(jnp.int32), axis=2
    )
    segment_ext = jnp.where(positions[None, :] < 0, -1, segment_ext)
    segment_here = segment_ext[:, KCONV - 1 :]
    inputs = block_input.astype(jnp.float32)
    scale_in = lax.rsqrt(jnp.mean(inputs * inputs, axis=-1, keepdims=True) + EPSILON)
    normed = (inputs * scale_in * full_weights[0].astype(jnp.float32)).astype(jnp.bfloat16)
    projected = jnp.einsum(
        "std,dk->stk", normed, full_weights[1], preferred_element_type=jnp.float32
    ).astype(jnp.bfloat16)
    conv_part = projected[:, :, DI : DI + CONVCH]
    before = passed_along(conv_part[:, tok_count - (KCONV - 1) :], "fsdp", 1)
    conv_input = jnp.concatenate([before, conv_part], axis=1)
    taps_full = full_weights[2].astype(jnp.float32)
    pre_act = jnp.broadcast_to(full_weights[3].astype(jnp.float32), (seq_count, tok_count, CONVCH))
    for offset in range(KCONV):
        same_doc = (segment_ext[:, offset : offset + tok_count] == segment_here).astype(jnp.float32)
        pre_act = (
            pre_act
            + taps_full[offset]
            * conv_input[:, offset : offset + tok_count].astype(jnp.float32)
            * same_doc[:, :, None]
        )
    activated = jax.nn.silu(pre_act)
    act_low = activated.astype(jnp.bfloat16)
    heads_full = activated[:, :, :DI].reshape(seq_count, tok_count, H, P_SIZE)
    heads_low = act_low[:, :, :DI].reshape(flat_blocks, BLOCK, H, P_SIZE)
    keys_low = act_low[:, :, DI : DI + N]
    query_low = act_low[:, :, DI + N :]
    raw_step = projected[:, :, DI + CONVCH :].astype(jnp.float32)
    step_size = jax.nn.softplus(raw_step + full_weights[4].astype(jnp.float32))
    rate_values = -jnp.exp(full_weights[5].astype(jnp.float32))
    log_decay = step_size * rate_values
    prev_blocks = segment_ext[:, KCONV - 2 : KCONV - 2 + tok_count : BLOCK].reshape(flat_blocks)
    intra_out, local_state, keep_rate, enter_rate = lax.map(
        block_forward,
        (
            heads_full,
            heads_low,
            keys_low,
            query_low,
            step_size,
            log_decay,
            segment_here,
            prev_blocks,
        ),
    )
    keep_rate = keep_rate.reshape(seq_count, block_count, H)
    local_state = local_state.reshape(seq_count, block_count, H, P_SIZE, N)
    device_rate = keep_rate[:, 0]
    device_state = local_state[:, 0]
    scanned = entering(
        (device_rate, device_state),
        "fsdp",
        state_combine,
        (jnp.ones_like(device_rate), jnp.zeros_like(device_state)),
        False,
    )
    current = scanned[1]
    starts = [current]
    start_states = jnp.stack(starts, axis=1).reshape(flat_blocks, H, P_SIZE, N)
    start_low = start_states.astype(jnp.bfloat16)
    inter_out = (
        jnp.einsum("ctn,chpn->cthp", query_low, start_low, preferred_element_type=jnp.float32)
        * enter_rate[:, :, :, None]
    )
    ssm_out = intra_out + inter_out
    skip_full = full_weights[6].astype(jnp.float32)
    mixer_out = (ssm_out + skip_full[:, None] * heads_full).reshape(seq_count, tok_count, DI)
    gate_raw = projected[:, :, :DI].astype(jnp.float32)
    gate_act = jax.nn.silu(gate_raw)
    gated_out = mixer_out * gate_act
    scale_out = lax.rsqrt(jnp.mean(gated_out * gated_out, axis=-1, keepdims=True) + EPSILON)
    normed_out = (gated_out * scale_out * full_weights[7].astype(jnp.float32)).astype(jnp.bfloat16)
    result = inputs + jnp.einsum(
        "stk,kd->std", normed_out, full_weights[8], preferred_element_type=jnp.float32
    )
    block_output = result.astype(jnp.bfloat16)
    cotangent = out_cotangent.astype(jnp.float32)
    grad_normed_out = jnp.einsum(
        "std,kd->stk", out_cotangent, full_weights[8], preferred_element_type=jnp.float32
    )
    grad_out_weight = jnp.einsum(
        "stk,std->kd", normed_out, out_cotangent, preferred_element_type=jnp.float32
    )
    grad_out_gain = jnp.sum(grad_normed_out * gated_out * scale_out, axis=(0, 1))
    scaled_grad = grad_normed_out * full_weights[7].astype(jnp.float32)
    grad_gated = scale_out * (
        scaled_grad
        - gated_out
        * jnp.mean(scaled_grad * gated_out, axis=-1, keepdims=True)
        * scale_out
        * scale_out
    )
    grad_mixer = grad_gated * gate_act
    grad_gate_raw = grad_gated * mixer_out * silu_grad(gate_raw)
    grad_mixer_heads = grad_mixer.reshape(seq_count, tok_count, H, P_SIZE)
    skip_back = full_weights[6].astype(jnp.float32)
    grad_skip = jnp.sum(grad_mixer_heads * heads_full, axis=(0, 1, 3))
    grad_heads_skip = grad_mixer_heads * skip_back[:, None]
    grad_ssm = grad_mixer_heads.astype(jnp.bfloat16)
    inject = jnp.einsum(
        "cthp,ctn->chpn",
        grad_ssm.astype(jnp.float32) * enter_rate[:, :, :, None],
        query_low.astype(jnp.float32),
        precision=HIGHEST,
    )
    inject = inject.reshape(seq_count, block_count, H, P_SIZE, N)
    device_grad = inject[:, block_count - 1]
    leaving = entering(
        (device_rate, device_grad),
        "fsdp",
        grad_combine,
        (jnp.ones_like(device_rate), jnp.zeros_like(device_grad)),
        True,
    )
    current = leaving[1]
    end_list = []
    end_list.append(current)
    end_list = end_list[::-1]
    end_grads = jnp.stack(end_list, axis=1).reshape(flat_blocks, H, P_SIZE, N)
    rate_back = -jnp.exp(full_weights[5].astype(jnp.float32))

    def block_back(fields):
        return block_backward(fields, rate_back)

    grad_heads, grad_keys, grad_query, grad_step, grad_rate = lax.map(
        block_back,
        (
            heads_full,
            heads_low,
            keys_low,
            query_low,
            step_size,
            log_decay,
            segment_here,
            prev_blocks,
            start_states,
            grad_ssm,
            end_grads,
        ),
    )
    grad_heads = grad_heads + grad_heads_skip
    grad_act = jnp.concatenate(
        [grad_heads.reshape(seq_count, tok_count, DI), grad_keys, grad_query], axis=-1
    )
    grad_pre = grad_act * silu_grad(pre_act)
    step_gate = jax.nn.sigmoid(raw_step + full_weights[4].astype(jnp.float32))
    grad_raw_step = grad_step * step_gate
    grad_step_bias = jnp.sum(grad_raw_step, axis=(0, 1))
    grad_decay_log = jnp.sum(grad_rate, axis=0) * rate_back
    taps_back = full_weights[2].astype(jnp.float32)
    tap_grads = []
    grad_conv_in = jnp.zeros((seq_count, tok_count + KCONV - 1, CONVCH), jnp.float32)
    for offset in range(KCONV):
        same_doc = (segment_ext[:, offset : offset + tok_count] == segment_here).astype(jnp.float32)
        masked = grad_pre * same_doc[:, :, None]
        tap_grads.append(
            jnp.sum(
                masked * conv_input[:, offset : offset + tok_count].astype(jnp.float32), axis=(0, 1)
            )
        )
        grad_conv_in = grad_conv_in + jnp.pad(
            taps_back[offset] * masked, ((0, 0), (offset, KCONV - 1 - offset), (0, 0))
        )
    grad_taps = jnp.stack(tap_grads, axis=0)
    grad_conv_bias = jnp.sum(grad_pre, axis=(0, 1))
    returned = passed_along(grad_conv_in[:, : KCONV - 1], "fsdp", -1)
    grad_conv_part = grad_conv_in[:, KCONV - 1 :] + jnp.pad(
        returned, ((0, 0), (tok_count - (KCONV - 1), 0), (0, 0))
    )
    grad_proj = jnp.concatenate([grad_gate_raw, grad_conv_part, grad_raw_step], axis=-1).astype(
        jnp.bfloat16
    )
    grad_normed = jnp.einsum(
        "stk,dk->std", grad_proj, full_weights[1], preferred_element_type=jnp.float32
    )
    grad_in_weight = jnp.einsum(
        "std,stk->dk", normed, grad_proj, preferred_element_type=jnp.float32
    )
    grad_gain_in = jnp.sum(grad_normed * inputs * scale_in, axis=(0, 1))
    scaled_in = grad_normed * full_weights[0].astype(jnp.float32)
    grad_inputs = (
        scale_in
        * (
            scaled_in
            - inputs * jnp.mean(scaled_in * inputs, axis=-1, keepdims=True) * scale_in * scale_in
        )
        + cotangent
    )
    input_grad = grad_inputs.astype(jnp.bfloat16)
    partial_sums = (
        lax.psum_scatter(
            grad_gain_in.astype(jnp.bfloat16), "fsdp", scatter_dimension=0, tiled=True
        ).astype(jnp.float32),
        lax.psum_scatter(
            grad_in_weight.astype(jnp.bfloat16), "fsdp", scatter_dimension=0, tiled=True
        ).astype(jnp.float32),
        lax.psum_scatter(
            grad_taps.astype(jnp.bfloat16), "fsdp", scatter_dimension=1, tiled=True
        ).astype(jnp.float32),
        lax.psum_scatter(
            grad_conv_bias.astype(jnp.bfloat16), "fsdp", scatter_dimension=0, tiled=True
        ).astype(jnp.float32),
        lax.psum_scatter(
            grad_out_gain.astype(jnp.bfloat16), "fsdp", scatter_dimension=0, tiled=True
        ).astype(jnp.float32),
        lax.psum_scatter(
            grad_out_weight.astype(jnp.bfloat16), "fsdp", scatter_dimension=0, tiled=True
        ).astype(jnp.float32),
    )
    owned_parts = (
        lax.psum(partial_sums[0].astype(jnp.bfloat16), "dp").astype(jnp.float32),
        lax.psum(partial_sums[1].astype(jnp.bfloat16), "dp").astype(jnp.float32),
        lax.psum(partial_sums[2].astype(jnp.bfloat16), "dp").astype(jnp.float32),
        lax.psum(partial_sums[3].astype(jnp.bfloat16), "dp").astype(jnp.float32),
        lax.psum(partial_sums[4].astype(jnp.bfloat16), "dp").astype(jnp.float32),
        lax.psum(partial_sums[5].astype(jnp.bfloat16), "dp").astype(jnp.float32),
    )
    head_terms = jnp.stack([grad_step_bias, grad_decay_log, grad_skip], axis=0)
    head_total = lax.psum(head_terms, ("fsdp", "dp"))
    share_count = H // lax.axis_size("fsdp")
    own_heads = lax.dynamic_slice_in_dim(head_total, device_index * share_count, share_count, 1)
    return (
        block_output,
        input_grad,
        owned_parts[0],
        owned_parts[1],
        owned_parts[2],
        owned_parts[3],
        own_heads[0],
        own_heads[1],
        own_heads[2],
        owned_parts[4],
        owned_parts[5],
    )


def solution(mesh):
    return jax.shard_map(
        local,
        mesh=mesh,
        in_specs=(
            P("dp", "fsdp", None),
            P("dp", "fsdp", None),
            P("dp", None),
            P("fsdp"),
            P("fsdp", None),
            P(None, "fsdp"),
            P("fsdp"),
            P("fsdp"),
            P("fsdp"),
            P("fsdp"),
            P("fsdp"),
            P("fsdp", None),
        ),
        out_specs=(
            P("dp", "fsdp", None),
            P("dp", "fsdp", None),
            P("fsdp"),
            P("fsdp", None),
            P(None, "fsdp"),
            P("fsdp"),
            P("fsdp"),
            P("fsdp"),
            P("fsdp"),
            P("fsdp"),
            P("fsdp", None),
        ),
        check_vma=False,
    )
```

profile of v0, /device:TPU:0, one launch (start us, length us, event | category | flops | bytes accessed | tf_op | source)
XLA Modules:
  0.0 387.8 jit_solution(17671281262071877517)
XLA Ops:
  8.0 1.3 fusion.120
  11.3 0.9 dynamic-update-slice.3
  12.1 0.8 dynamic-update-slice.2
  13.0 0.8 dynamic-update-slice.4
  13.8 0.8 dynamic-update-slice.1
  14.7 0.9 dynamic-update-slice
  15.5 8.5 %all-reduce.16 = (bf16[768]{0:T(1024)(128)(2,1)S(1)}, bf16[1792]{0:T(1024)(128)(2,1)S(1)}, bf16[24]{0:T(256)(128)(2,1)S(1)}, bf16[24]{0:T(256)(128)(2,1)S(1)}, bf16[24]{0:T(256)(128)(2,1)S(1)}) all-reduce(bf16[768]{0:T(1024)(128)(2,1)S(1)} %dynamic-update-slice.1, ...), channel_id=1, replica_groups=mesh['fsdp'=4,'dp'=8] {'fsdp'}, use_global_device_ids=true, to_apply=%add.6 | all-reduce | flops 2632 | bytes 10528
  25.1 5.3 %all-gather.3 = bf16[4,448,4]{1,2,0:T(4,128)(2,1)S(1)} all-gather(bf16[1,448,4]{1,2,0:T(4,128)(2,1)} %bitcast.262), channel_id=1, replica_groups=mesh['fsdp'=4,'dp'=8] {'fsdp'}, dimensions={0}, use_global_device_ids=true | all-gather | bytes 17920 | tf_op jit(solution)/shard_map/all_gather | solution.py:176
  31.6 1.9 compare_convert_fusion.5
  33.4 19.9 %all-gather.11.cloned.1.call-done = bf16[768,3352]{1,0:T(8,128)(2,1)} async-done(((bf16[192,3352]{1,0:T(8,128)(2,1)}), bf16[768,3352]{1,0:T(8,128)(2,1)}) %all-gather.11.cloned.1.call-update) | async-done | bytes 5148688 | tf_op jit(solution)/shard_map/all_gather | solution.py:175
  53.3 4.7 %fusion.1 = bf16[1,256,3352]{1,2,0:T(8,128)(2,1)S(1)} fusion(bf16[768,3352]{1,0:T(8,128)(2,1)} %all-gather.11.cloned.1.call-done, bf16[1,256,768]{2,1,0:T(8,128)(2,1)S(1)} %copy-done.20, f32[768]{0:T(1024)S(1)} %convert_element_type.348, f32[256]{0:T(256)S(1)} %add_rsqrt_fusion.1), kind=kOutput, calls=%fused_computation.13 | convolution fusion | flops 1319704576 | bytes 7262208 | tf_op jit(solution)/shard_map/std,dk->stk/dot_general | solution.py:194
  58.7 2.2 collective-permute-start
  62.4 4.0 %fusion.116 = (bf16[1,256,1792]{1,2,0:T(8,128)(2,1)S(1)}, f32[1,256,1792]{1,2,0:T(8,128)S(1)}, f32[1,256,1792]{1,2,0:T(8,128)}) fusion(bf16[1,256,1792]{1,2,0:T(8,128)(2,1)S(1)} %slice.138, f32[1792]{0:T(1024)S(1)} %get-tuple-element.288, f32[256]{0:T(256)S(1)} %bitcast.256, bf16[1,3,1792]{1,2,0:T(8,128)(2,1)S(1)} %collective-permute-done, ...), kind=kLoop, calls=%fused_computation.221 | loop fusion | flops 13303808 | bytes 5554688 | tf_op jit(solution)/shard_map/convert_element_type | solution.py:211
  66.4 1.6 fusion.30
  68.1 0.9 copy-done.12
  69.0 1.1 convolution_convert_fusion.4
  74.3 9.7 %all-gather.5 = bf16[4,1,384]{2,1,0:T(2,128)(2,1)S(1)} all-gather(bf16[1,1,384]{2,1,0:T(2,128)(2,1)S(1)} %reshape.510), channel_id=1, replica_groups=mesh['fsdp'=4,'dp'=8] {'fsdp'}, dimensions={0}, use_global_device_ids=true | all-gather | bytes 3840 | tf_op jit(solution)/shard_map/all_gather | solution.py:181
  84.2 5.7 %all-gather.4 = bf16[4,1,24]{2,1,0:T(2,128)(2,1)} all-gather(bf16[1,1,24]{2,1,0:T(2,128)(2,1)S(1)} %bitcast.266), channel_id=2, replica_groups=mesh['fsdp'=4,'dp'=8] {'fsdp'}, dimensions={0}, use_global_device_ids=true | all-gather | bytes 240 | tf_op jit(solution)/shard_map/all_gather | solution.py:30
  90.9 5.3 %all-gather.15.cloned.1.call-done = bf16[96,64,128]{2,1,0:T(8,128)(2,1)} async-done(((bf16[24,64,128]{2,1,0:T(8,128)(2,1)}), bf16[96,64,128]{2,1,0:T(8,128)(2,1)}) %all-gather.15.cloned.1.call-update) | async-done | bytes 1572880 | tf_op jit(solution)/shard_map/all_gather | solution.py:30
  96.9 1.0 copy-done.14
  98.3 2.2 fusion.31
  100.5 2.3 multiply_reduce_fusion.7
  102.8 19.1 %all-gather.13.cloned.1.call-done = bf16[1536,768]{1,0:T(8,128)(2,1)} async-done(((bf16[384,768]{1,0:T(8,128)(2,1)}), bf16[1536,768]{1,0:T(8,128)(2,1)}) %all-gather.13.cloned.1.call-update) | async-done | bytes 2359312 | tf_op jit(solution)/shard_map/all_gather | solution.py:182
  121.8 3.5 fusion.26
  125.3 3.9 %multiply_reduce_fusion.4 = (f32[1536]{0:T(1024)}, f32[1,256,1536]{1,2,0:T(8,128)S(1)}, bf16[1,256,1536]{1,2,0:T(8,128)(2,1)}) fusion(f32[1,256,1792]{1,2,0:T(8,128)S(1)} %copy-done.6, bf16[1,256,3352]{1,2,0:T(8,128)(2,1)} %copy-done.7, f32[1,256,1536]{1,2,0:T(8,128)S(1)} %get-tuple-element.333, f32[256]{0:T(256)S(1)} %broadcast_multiply_fusion.1, ...), kind=kLoop, calls=%fused_computation.82 | loop fusion | flops 8256000 | bytes 9451520 | tf_op jit(solution)/shard_map/reduce_sum | solution.py:285
  129.3 1.2 copy-done.3
  130.6 1.6 convolution_convert_fusion.3
  132.2 2.8 multiply_reduce_fusion.5
  136.6 5.3 %multiply_reduce_fusion.1 = (f32[24,256]{1,0:T(8,128)}, f32[24,256]{1,0:T(8,128)}, f32[24,256]{1,0:T(8,128)}, bf16[256,256]{1,0:T(8,128)(2,1)S(1)}) fusion(f32[24,256]{1,0:T(8,128)S(1)} %copy-done.67, f32[256,256]{1,0:T(8,128)S(1)} %copy-done.32, f32[256,256]{1,0:T(8,128)S(1)} %copy-done.35, f32[24,256]{1,0:T(8,128)S(1)} %bitcast.246, ...), kind=kOutput, calls=%fused_computation.9 | convolution fusion | flops 218544128 | bytes 2416640 | tf_op jit(solution)/shard_map/while/body/eval_jaxpr/thp,shp->hts/dot_general | solution.py:107
  142.1 2.3 convolution_convert_fusion.2
  144.5 7.5 %all-gather.17.cloned.1.call-done = bf16[96,64,128]{2,1,0:T(8,128)(2,1)} async-done(((bf16[24,64,128]{2,1,0:T(8,128)(2,1)}), bf16[96,64,128]{2,1,0:T(8,128)(2,1)}) %all-gather.17.cloned.1.call-update) | async-done | bytes 1572880 | tf_op jit(solution)/shard_map/all_gather | solution.py:30
  152.1 5.8 %while.17 = (s32[]{:T(128)}, f32[1,24,64,128]{3,2,1,0:T(8,128)S(1)}, s32[]{:T(128)}, bf16[4,1,24,64,128]{4,3,2,1,0:T(8,128)(2,1)}, bf16[4,1,24]{2,1,0:T(2,128)(2...) while((s32[]{:T(128)}, f32[1,24,64,128]{3,2,1,0:T(8,128)S(1)}, s32[]{:T(128)}, ...), condition=%wide.region_8.9_spmd, body=%wide.region_7.8_spmd.sunk | while | flops 589854 | bytes 1966475 | solution.py:45
  152.8 1.2 convert_add_fusion.7
  154.6 1.2 convert_add_fusion.7
  156.5 1.2 convert_add_fusion.7
  157.9 3.0 multiply_reduce_fusion.6
  162.7 1.7 convolution_bitcast_fusion.1
  164.3 1.0 fusion.33
  165.5 3.7 fusion.27
  169.3 4.2 %fusion.10 = (bf16[1792]{0:T(1024)(128)(2,1)S(1)}, bf16[1792]{0:T(1024)(128)(2,1)}, bf16[1792]{0:T(1024)(128)(2,1)}, bf16[1792]{0:T(1024)(128)(2,1)S(1)}, bf16[1...) fusion(f32[256]{0:T(256)S(1)} %bitcast.254, bf16[1,256,1792]{1,2,0:T(8,128)(2,1)S(1)} %copy-done.10, ...), kind=kLoop, calls=%fused_computation.36 | loop fusion | flops 16047360 | bytes 7371776 | tf_op jit(solution)/shard_map/reduce_sum | solution.py:345
  173.6 1.3 multiply_multiply_fusion.2
  174.9 1.3 copy-done
  177.2 1.5 pad_add_fusion.1
  178.6 2.1 copy.65
  180.7 1.3 collective-permute-start.1
  182.3 6.4 %pad_add_fusion = f32[1,259,1792]{1,2,0:T(8,128)} fusion(f32[1,256,1792]{1,2,0:T(8,128)} %copy-done, f32[1,256,1792]{1,2,0:T(8,128)} %copy-done.1, f32[1,256,1792]{1,2,0:T(8,128)} %copy-done.2, f32[1,256,1792]{1,2,0:T(8,128)S(1)} %get-tuple-element.338), kind=kLoop, calls=%fused_computation.17 | loop fusion | flops 1392384 | bytes 9196544 | tf_op jit(solution)/shard_map/add | solution.py:349
  188.8 1.1 fusion.114
  189.9 1.1 copy.66
  191.0 2.5 fusion.37
  193.5 0.9 copy-done.24
  194.4 4.2 %convolution_convert_fusion = bf16[768,3352]{1,0:T(8,128)(2,1)} fusion(bf16[256,24]{0,1:T(8,128)(2,1)S(1)} %bitcast.268, bf16[256,1792]{0,1:T(8,128)(2,1)S(1)} %fusion.37, bf16[256,1536]{0,1:T(8,128)(2,1)S(1)} %bitcast.244, bf16[1,256,768]{2,1,0:T(8,128)(2,1)S(1)} %copy-done.21, f32[768]{0:T(1024)S(1)} %copy-done.70, f32[256]{0:T(256)S(1)} %copy-done.86), kind=kOutput, calls=%fused_computation.4 | convolution fusion | flops 1326569472 | bytes 7262208 | tf_op jit(solution)/shard_map/std,stk->dk/dot_general | solution.py:364
  200.8 1.0 copy.79
  201.9 3.4 fusion.32
  205.5 46.0 %reduce-scatter.6.cloned.1.call-done = bf16[192,3352]{1,0:T(8,128)(2,1)} async-done(((bf16[768,3352]{1,0:T(8,128)(2,1)}), bf16[192,3352]{1,0:T(8,128)(2,1)}) %reduce-scatter.6.cloned.1.call-update) | async-done | bytes 1287184 | tf_op jit(solution)/shard_map/reduce_scatter | solution.py:382
  251.5 0.9 fusion.94
  252.5 39.8 %psum.53 = f32[3,24]{1,0:T(4,128)S(1)} all-reduce(f32[3,24]{1,0:T(4,128)S(1)} %pad_maximum_fusion.5), channel_id=1, replica_groups=mesh['fsdp'=4,'dp'=8] {'fsdp','dp'}, use_global_device_ids=true, to_apply=%region_37.38 | all-reduce | flops 72 | bytes 576 | tf_op jit(solution)/shard_map/psum | solution.py:407
  292.9 4.6 %fusion.50 = (bf16[768]{0:T(1024)(128)(2,1)S(1)}, f32[256]{0:T(256)S(1)}, f32[256,768]{1,0:T(8,128)S(1)}) fusion(bf16[1,256,768]{2,1,0:T(8,128)(2,1)S(1)} %copy-done.21, f32[256]{0:T(256)S(1)} %copy-done.86, f32[768]{0:T(1024)S(1)} %copy-done.70, bf16[768,3352]{1,0:T(8,128)(2,1)} %all-gather.11.cloned.1.call-done, bf16[256,24]{0,1:T(8,128)(2,1)S(1)} %bitcast.269, ...), kind=kOutput, calls=%fused_computation.116 | convolution fusion | flops 1324583936 | bytes 8051200 | tf_op jit(solution)/shard_map/stk,dk->std/dot_general | solution.py:361
  297.5 11.7 %all-reduce.15 = (bf16[768]{0:T(1024)(128)(2,1)S(1)}, bf16[1792]{0:T(1024)(128)(2,1)S(1)}, bf16[1536]{0:T(1024)(128)(2,1)S(1)}) all-reduce(bf16[768]{0:T(1024)(128)(2,1)S(1)} %get-tuple-element.285, bf16[1792]{0:T(1024)(128)(2,1)S(1)} %get-tuple-element.283, ...), channel_id=5, replica_groups=mesh['fsdp'=4,'dp'=8] {'fsdp'}, use_global_device_ids=true, to_apply=%region_20.21.clone | all-reduce | flops 4096 | bytes 16384
  309.4 1.1 fusion.48
  310.5 1.0 copy.80
  311.5 20.6 %all-reduce.13 = (bf16[192]{0:T(256)(128)(2,1)S(1)}, bf16[4,448]{1,0:T(4,128)(2,1)S(1)}, bf16[448]{0:T(512)(128)(2,1)S(1)}, bf16[384]{0:T(512)(128)(2,1)S(1)}) all-reduce(bf16[192]{0:T(256)(128)(2,1)S(1)} %dynamic-slice.6, bf16[4,448]{1,0:T(4,128)(2,1)S(1)} %copy.80, ...), channel_id=1, replica_groups=mesh['fsdp'=4,'dp'=8] {'dp'}, use_global_device_ids=true, to_apply=%region_21.22 | all-reduce | flops 2816 | bytes 11264 | tf_op jit(solution)/shard_map/psum | solution.py:399
  334.5 42.4 %all-reduce.19.cloned.1.call-done = (bf16[192,3352]{1,0:T(8,128)(2,1)}, bf16[384,768]{1,0:T(8,128)(2,1)}) async-done(((bf16[192,3352]{1,0:T(8,128)(2,1)}, bf16[384,768]{1,0:T(8,128)(2,1)}), (bf16[192,3352]{1,0:T(8,128)(2,1)}, bf16[384,768]{1,0:T(8,128)(2,1)})) %all-reduce.19.cloned.1.call-update) | async-done | bytes 1877008 | tf_op jit(solution)/shard_map/psum | solution.py:400
  376.8 3.1 convert_element_type.390
  379.9 1.1 convert_element_type.397
  (288 shorter events, 20.8 us)
Async XLA Ops:
  7.2 24.0 %copy-start.20 = (bf16[1,256,768]{2,1,0:T(8,128)(2,1)S(1)}, bf16[1,256,768]{2,1,0:T(8,128)(2,1)}, u32[]{:S(2)}) copy-start(bf16[1,256,768]{2,1,0:T(8,128)(2,1)} %param.16) | copy-start | bytes 1179652
  7.2 46.1 %all-gather.11.cloned.1.call-start = ((), (), s32[]{:S(2)}) async-start(), calls=%async_computation.3 | async-start | bytes 6635520 | tf_op jit(solution)/shard_map/all_gather | solution.py:175
  7.9 88.2 %all-gather.15.cloned.1.call-start = ((), (), s32[]{:S(2)}) async-start(), calls=%async_computation.7 | async-start | bytes 1966080 | tf_op jit(solution)/shard_map/all_gather | solution.py:30
  24.0 7.4 %copy-start.91 = (bf16[24]{0:T(256)(128)(2,1)}, bf16[24]{0:T(256)(128)(2,1)S(1)}, u32[]{:S(2)}) copy-start(bf16[24]{0:T(256)(128)(2,1)S(1)} %get-tuple-element.322) | copy-start | bytes 148
  24.0 34.0 %copy-start.69 = (f32[768]{0:T(1024)}, f32[768]{0:T(1024)S(1)}, u32[]{:S(2)}) copy-start(f32[768]{0:T(1024)S(1)} %convert_element_type.348) | copy-start | bytes 9220
  24.0 65.9 %copy-start.81 = (f32[24]{0:T(128)}, f32[24]{0:T(128)S(1)}, u32[]{:S(2)}) copy-start(f32[24]{0:T(128)S(1)} %convert_element_type.360) | copy-start | bytes 292
  31.2 31.1 %copy-start.51 = (f32[1792]{0:T(1024)}, f32[1792]{0:T(1024)S(1)}, u32[]{:S(2)}) copy-start(f32[1792]{0:T(1024)S(1)} %get-tuple-element.288) | copy-start | bytes 21508
  31.2 31.1 %copy-start.53 = (f32[1792]{0:T(1024)}, f32[1792]{0:T(1024)S(1)}, u32[]{:S(2)}) copy-start(f32[1792]{0:T(1024)S(1)} %get-tuple-element.289) | copy-start | bytes 21508
  31.2 31.1 %copy-start.55 = (f32[1792]{0:T(1024)}, f32[1792]{0:T(1024)S(1)}, u32[]{:S(2)}) copy-start(f32[1792]{0:T(1024)S(1)} %get-tuple-element.290) | copy-start | bytes 21508
  31.4 26.8 %copy-start.93 = (f32[24]{0:T(128)}, f32[24]{0:T(128)S(1)}, u32[]{:S(2)}) copy-start(f32[24]{0:T(128)S(1)} %exponential_negate_fusion) | copy-start | bytes 292
  31.4 26.6 %copy-start.85 = (f32[256]{0:T(256)}, f32[256]{0:T(256)S(1)}, u32[]{:S(2)}) copy-start(f32[256]{0:T(256)S(1)} %add_rsqrt_fusion.1) | copy-start | bytes 3076
  31.5 30.8 %copy-start.75 = (f32[1,256]{1,0:T(1,128)}, f32[1,256]{1,0:T(1,128)S(1)}, u32[]{:S(2)}) copy-start(f32[1,256]{1,0:T(1,128)S(1)} %get-tuple-element.351) | copy-start | bytes 3076
  31.5 30.8 %copy-start.77 = (f32[1,256]{1,0:T(1,128)}, f32[1,256]{1,0:T(1,128)S(1)}, u32[]{:S(2)}) copy-start(f32[1,256]{1,0:T(1,128)S(1)} %get-tuple-element.352) | copy-start | bytes 3076
  31.5 30.8 %copy-start.79 = (f32[1,256]{1,0:T(1,128)}, f32[1,256]{1,0:T(1,128)S(1)}, u32[]{:S(2)}) copy-start(f32[1,256]{1,0:T(1,128)S(1)} %get-tuple-element.353) | copy-start | bytes 3076
  33.4 27.5 %copy-start.83 = (f32[256]{0:T(256)}, f32[256]{0:T(256)S(1)}, u32[]{:S(2)}) copy-start(f32[256]{0:T(256)S(1)} %get-tuple-element.355) | copy-start | bytes 3076
  58.0 31.9 %copy-start.7 = (bf16[1,256,3352]{1,2,0:T(8,128)(2,1)}, bf16[1,256,3352]{1,2,0:T(8,128)(2,1)S(1)}, u32[]{:S(2)}) copy-start(bf16[1,256,3352]{1,2,0:T(8,128)(2,1)S(1)} %fusion.1) | copy-start | bytes 5148676
  58.5 25.5 %copy-start.41 = (f32[256,24]{0,1:T(8,128)}, f32[256,24]{0,1:T(8,128)S(1)}, u32[]{:S(2)}) copy-start(f32[256,24]{0,1:T(8,128)S(1)} %fusion.64) | copy-start | bytes 73732
  58.7 7.6 %copy-start.87 = (f32[24]{0:T(128)}, f32[24]{0:T(128)S(1)}, u32[]{:S(2)}) copy-start(f32[24]{0:T(128)S(1)} %slice_reduce_fusion) | copy-start | bytes 292
  58.7 3.6 collective-permute-start
  61.5 4.9 %copy-start.37 = (f32[256,24]{0,1:T(8,128)}, f32[256,24]{0,1:T(8,128)S(1)}, u32[]{:S(2)}) copy-start(f32[256,24]{0,1:T(8,128)S(1)} %get-tuple-element.345) | copy-start | bytes 73732
  61.6 4.8 %copy-start.9 = (bf16[1,256,1792]{1,2,0:T(8,128)(2,1)}, bf16[1,256,1792]{1,2,0:T(8,128)(2,1)S(1)}, u32[]{:S(2)}) copy-start(bf16[1,256,1792]{1,2,0:T(8,128)(2,1)S(1)} %slice.138) | copy-start | bytes 2752516
  62.3 4.1 %copy-start.22 = (bf16[1,3,1792]{1,2,0:T(8,128)(2,1)}, bf16[1,3,1792]{1,2,0:T(8,128)(2,1)S(1)}, u32[]{:S(2)}) copy-start(bf16[1,3,1792]{1,2,0:T(8,128)(2,1)S(1)} %collective-permute-done) | copy-start | bytes 32260
  66.4 75.5 %copy-start.17 = (bf16[1,256,1792]{1,2,0:T(8,128)(2,1)}, bf16[1,256,1792]{1,2,0:T(8,128)(2,1)S(1)}, u32[]{:S(2)}) copy-start(bf16[1,256,1792]{1,2,0:T(8,128)(2,1)S(1)} %get-tuple-element.334) | copy-start | bytes 2752516
  68.1 6.1 %copy-start.90 = (bf16[384]{0:T(512)(128)(2,1)S(1)}, bf16[384]{0:T(512)(128)(2,1)}, u32[]{:S(2)}) copy-start(bf16[384]{0:T(512)(128)(2,1)} %param.26) | copy-start | bytes 2308
  70.1 51.7 %all-gather.13.cloned.1.call-start = ((), (), s32[]{:S(2)}) async-start(), calls=%async_computation.4 | async-start | bytes 2949120 | tf_op jit(solution)/shard_map/all_gather | solution.py:182
  70.9 81.1 %all-gather.17.cloned.1.call-start = ((), (), s32[]{:S(2)}) async-start(), calls=%async_computation.8 | async-start | bytes 1966080 | tf_op jit(solution)/shard_map/all_gather | solution.py:30
  90.7 6.2 %copy-start.26 = (bf16[1,256,1536]{1,2,0:T(8,128)(2,1)}, bf16[1,256,1536]{1,2,0:T(8,128)(2,1)S(1)}, u32[]{:S(2)}) copy-start(bf16[1,256,1536]{1,2,0:T(8,128)(2,1)S(1)} %slice.150) | copy-start | bytes 2359300
  90.9 6.0 %copy-start.31 = (f32[256,256]{1,0:T(8,128)}, f32[256,256]{1,0:T(8,128)S(1)}, u32[]{:S(2)}) copy-start(f32[256,256]{1,0:T(8,128)S(1)} %fusion.76) | copy-start | bytes 786436
  102.7 22.6 %copy-start.61 = (f32[256]{0:T(256)}, f32[256]{0:T(256)S(1)}, u32[]{:S(2)}) copy-start(f32[256]{0:T(256)S(1)} %add_rsqrt_fusion) | copy-start | bytes 3076
  125.3 5.1 %copy-start.49 = (f32[256,24]{0,1:T(8,128)S(1)}, f32[256,24]{0,1:T(8,128)}, u32[]{:S(2)}) copy-start(f32[256,24]{0,1:T(8,128)} %get-tuple-element.344) | copy-start | bytes 73732
  132.2 73.3 %reduce-scatter.8.cloned.1.call-start = ((), (), s32[]{:S(2)}) async-start(), calls=%async_computation.6 | async-start | bytes 2949120 | tf_op jit(solution)/shard_map/reduce_scatter | solution.py:394
  135.0 6.9 %copy-start.28 = (bf16[256,24,64]{0,2,1:T(8,128)(2,1)}, bf16[256,24,64]{0,2,1:T(8,128)(2,1)S(1)}, u32[]{:S(2)}) copy-start(bf16[256,24,64]{0,2,1:T(8,128)(2,1)S(1)} %get-tuple-element.331) | copy-start | bytes 2359300
  136.6 5.5 %copy-start.18 = (bf16[1,256,768]{2,1,0:T(8,128)(2,1)S(1)}, bf16[1,256,768]{2,1,0:T(8,128)(2,1)}, u32[]{:S(2)}) copy-start(bf16[1,256,768]{2,1,0:T(8,128)(2,1)} %param.17) | copy-start | bytes 1179652
  136.6 5.5 %copy-start.62 = (f32[256]{0:T(256)S(1)}, f32[256]{0:T(256)}, u32[]{:S(2)}) copy-start(f32[256]{0:T(256)} %copy-done.61) | copy-start | bytes 3076
  144.4 107.1 %reduce-scatter.6.cloned.1.call-start = ((), (), s32[]{:S(2)}) async-start(), calls=%async_computation.5 | async-start | bytes 6635520 | tf_op jit(solution)/shard_map/reduce_scatter | solution.py:382
  165.4 3.8 copy-start.8
  165.4 3.8 copy-start.10
  165.4 3.8 copy-start.11
  165.4 3.8 copy-start.23
  169.3 4.3 %copy-start.52 = (f32[1792]{0:T(1024)S(1)}, f32[1792]{0:T(1024)}, u32[]{:S(2)}) copy-start(f32[1792]{0:T(1024)} %copy-done.51) | copy-start | bytes 21508
  169.3 4.3 %copy-start.54 = (f32[1792]{0:T(1024)S(1)}, f32[1792]{0:T(1024)}, u32[]{:S(2)}) copy-start(f32[1792]{0:T(1024)} %copy-done.53) | copy-start | bytes 21508
  169.3 4.3 %copy-start.56 = (f32[1792]{0:T(1024)S(1)}, f32[1792]{0:T(1024)}, u32[]{:S(2)}) copy-start(f32[1792]{0:T(1024)} %copy-done.55) | copy-start | bytes 21508
  177.2 4.8 %copy-start.45 = (f32[256,24]{0,1:T(8,128)S(1)}, f32[256,24]{0,1:T(8,128)}, u32[]{:S(2)}) copy-start(f32[256,24]{0,1:T(8,128)} %copy-done.41) | copy-start | bytes 73732
  177.2 4.8 %copy-start.59 = (f32[1,24]{0,1:T(8,128)S(1)}, f32[1,24]{0,1:T(8,128)}, u32[]{:S(2)}) copy-start(f32[1,24]{0,1:T(8,128)} %copy.68) | copy-start | bytes 292
  177.2 4.9 %copy-start.60 = (f32[1,24]{0,1:T(8,128)S(1)}, f32[1,24]{0,1:T(8,128)}, u32[]{:S(2)}) copy-start(f32[1,24]{0,1:T(8,128)} %copy.67) | copy-start | bytes 292
  180.7 9.1 %collective-permute-start.1 = (f32[1,3,1792]{2,0,1:T(1,128)}, f32[1,3,1792]{2,0,1:T(1,128)}, u32[]{:S(2)}, u32[]{:S(2)}) collective-permute-start(f32[1,3,1792]{2,0,1:T(1,128)} %copy.65), channel_id=1, source_target_pairs={{8,0},{16,8},{24,16},{9,1},{17,9},{25,17},{10,2},{18,10},{26,18},{... | collective-permute-start | bytes 64520 | tf_op jit(solution)/shard_map/ppermute | solution.py:22
  182.2 6.5 %copy-start.40 = (f32[256,24]{0,1:T(8,128)S(1)}, f32[256,24]{0,1:T(8,128)}, u32[]{:S(2)}) copy-start(f32[256,24]{0,1:T(8,128)} %copy-done.37) | copy-start | bytes 73732
  182.2 6.5 %copy-start.47 = (f32[256,24]{0,1:T(8,128)S(1)}, f32[256,24]{0,1:T(8,128)}, u32[]{:S(2)}) copy-start(f32[256,24]{0,1:T(8,128)} %copy-done.46) | copy-start | bytes 73732
  182.2 6.5 %copy-start.50 = (f32[256,24]{0,1:T(8,128)S(1)}, f32[256,24]{0,1:T(8,128)}, u32[]{:S(2)}) copy-start(f32[256,24]{0,1:T(8,128)} %get-tuple-element.344) | copy-start | bytes 73732
  182.2 6.5 %copy-start.65 = (f32[256,24]{0,1:T(8,128)S(1)}, f32[256,24]{0,1:T(8,128)}, u32[]{:S(2)}) copy-start(f32[256,24]{0,1:T(8,128)} %get-tuple-element.330) | copy-start | bytes 73732
  182.3 6.5 %copy-start.82 = (f32[24]{0:T(128)S(1)}, f32[24]{0:T(128)}, u32[]{:S(2)}) copy-start(f32[24]{0:T(128)} %copy-done.81) | copy-start | bytes 292
  182.3 6.5 %copy-start.84 = (f32[256]{0:T(256)S(1)}, f32[256]{0:T(256)}, u32[]{:S(2)}) copy-start(f32[256]{0:T(256)} %copy-done.83) | copy-start | bytes 3076
  182.3 6.5 %copy-start.88 = (f32[24]{0:T(128)S(1)}, f32[24]{0:T(128)}, u32[]{:S(2)}) copy-start(f32[24]{0:T(128)} %copy-done.87) | copy-start | bytes 292
  182.3 6.5 %copy-start.89 = (f32[256]{0:T(256)S(1)}, f32[256]{0:T(256)}, u32[]{:S(2)}) copy-start(f32[256]{0:T(256)} %get-tuple-element.363) | copy-start | bytes 3076
  182.3 6.5 %copy-start.94 = (f32[24]{0:T(128)S(1)}, f32[24]{0:T(128)}, u32[]{:S(2)}) copy-start(f32[24]{0:T(128)} %copy-done.93) | copy-start | bytes 292
  182.3 6.5 %copy-start.97 = (f32[24,256]{1,0:T(8,128)S(1)}, f32[24,256]{1,0:T(8,128)}, u32[]{:S(2)}) copy-start(f32[24,256]{1,0:T(8,128)} %get-tuple-element.274) | copy-start | bytes 73732
  182.3 6.5 %copy-start.98 = (f32[24,256]{1,0:T(8,128)S(1)}, f32[24,256]{1,0:T(8,128)}, u32[]{:S(2)}) copy-start(f32[24,256]{1,0:T(8,128)} %get-tuple-element.275) | copy-start | bytes 73732
  182.3 6.5 %copy-start.99 = (f32[24,256]{1,0:T(8,128)S(1)}, f32[24,256]{1,0:T(8,128)}, u32[]{:S(2)}) copy-start(f32[24,256]{1,0:T(8,128)} %get-tuple-element.276) | copy-start | bytes 73732
  198.7 111.8 %reduce-scatter.10.cloned.1.call-start = ((), (), s32[]{:S(2)}) async-start(), calls=%async_computation.9 | async-start | bytes 573440
  201.8 175.0 %all-reduce.19.cloned.1.call-start = ((), (), s32[]{:S(2)}) async-start(), calls=%async_computation.10 | async-start | bytes 3833856 | tf_op jit(solution)/shard_map/psum | solution.py:400
  205.3 47.1 %copy-start.92 = (bf16[24]{0:T(256)(128)(2,1)S(1)}, bf16[24]{0:T(256)(128)(2,1)}, u32[]{:S(2)}) copy-start(bf16[24]{0:T(256)(128)(2,1)} %copy-done.91) | copy-start | bytes 148
  205.3 87.6 %copy-start.25 = (bf16[256,1792]{0,1:T(8,128)(2,1)S(1)}, bf16[256,1792]{0,1:T(8,128)(2,1)}, u32[]{:S(2)}) copy-start(bf16[256,1792]{0,1:T(8,128)(2,1)} %copy-done.24) | copy-start | bytes 2752516
  292.9 4.6 %copy-start.71 = (bf16[1536]{0:T(1024)(128)(2,1)S(1)}, bf16[1536]{0:T(1024)(128)(2,1)}, u32[]{:S(2)}) copy-start(bf16[1536]{0:T(1024)(128)(2,1)} %get-tuple-element.281) | copy-start | bytes 9220
  292.9 16.6 %copy-start.19 = (bf16[1,256,768]{2,1,0:T(8,128)(2,1)S(1)}, bf16[1,256,768]{2,1,0:T(8,128)(2,1)}, u32[]{:S(2)}) copy-start(bf16[1,256,768]{2,1,0:T(8,128)(2,1)} %param.17) | copy-start | bytes 1179652
  (46 other events, 112.5 us)
Sparse Core Ops, SparseCore 0:
  9.6 43.6 all-gather.10
  70.2 25.8 all-gather.14
  97.7 24.0 all-gather.12
  132.3 19.6 all-gather.16
  155.0 33.2 reduce-scatter.7
  198.8 52.6 reduce-scatter.5
  254.0 21.1 reduce-scatter.9
  278.9 97.9 all-reduce.18
where the time goes:
time: 389 us; the launch traced here: 388 us
  waiting for transfers between devices  142 us (37%)
  blocking collectives  101 us (26%)
  other arithmetic  51.9 us (13%)
  matrix products  44.8 us (12%)
  local copies, waits for them, and re-layouts  22.6 us (6%)
  between operations  20.6 us (5%)
    reduce_scatter x1, waiting for transfers between devices, local(): lax.psum_scatter(grad_in_weight.astype(jnp.bfloat16), 'fsdp', scatter_dim...  46 us
    psum x1, waiting for transfers between devices, local(): lax.psum(partial_sums[1].astype(jnp.bfloat16), 'dp').astype(jnp.float32)  42.4 us
    psum x1, blocking collectives, local(): head_total = lax.psum(head_terms, ('fsdp', 'dp'))  39.8 us
    psum x1, blocking collectives, local(): lax.psum(partial_sums[0].astype(jnp.bfloat16), 'dp').astype(jnp.float32)  20.6 us
    unnamed x2, blocking collectives  20.2 us
    all_gather x1, waiting for transfers between devices, local(): lax.all_gather(in_weight, 'fsdp', axis=0, tiled=True)  19.9 us
    all_gather x1, waiting for transfers between devices, local(): lax.all_gather(out_weight, 'fsdp', axis=0, tiled=True)  19.1 us
    unnamed x217, local copies, waits for them, and re-layouts  15.9 us
  transfers between devices with their start and end apart: 10, of which 7 were waited for; matrix products, arithmetic and copies ran while one was open for 22% of the time, Pallas kernels for 0%

commit v1 on v0

v1 whole, which is shorter than its diff:
```python
import functools

import jax
import jax.numpy as jnp
from jax import lax
from jax.experimental import pallas as pl
from jax.experimental.pallas import tpu as pltpu
from jax.sharding import PartitionSpec as P

H = 24
PS = 64
N = 128
KCONV = 4
BLOCK = 256
DI = 1536
CONVCH = 1792
EPS = 1e-05
BF = jnp.bfloat16
F32 = jnp.float32
ANY = pl.ANY
VMEM_LIMIT = 56 * 1024 * 1024


def dot(a, b):
    return lax.dot_general(a, b, (((1,), (0,)), ((), ())), preferred_element_type=F32)


def dot_nt(a, b):
    return lax.dot_general(a, b, (((1,), (1,)), ((), ())), preferred_element_type=F32)


def dot_tn(a, b):
    return lax.dot_general(a, b, (((0,), (0,)), ((), ())), preferred_element_type=F32)


def pieces(value, count):
    out = []
    for _ in range(count):
        part = value.astype(BF)
        out.append(part)
        value = value - part.astype(F32)
    return out


def sigmoid(value):
    return 0.5 * jnp.tanh(0.5 * value) + 0.5


def iota(shape, dim):
    return lax.broadcasted_iota(jnp.int32, shape, dim)


def segments(bounds, position):
    seg = functools.reduce(
        lambda total, bound: total + jnp.where(position >= bound, 1, 0),
        bounds,
        jnp.zeros_like(position),
    )
    return jnp.where(position < 0, -1, seg)


def expand(table, pairs):
    low = iota((table.shape[0], 128), 1) < PS
    return jnp.concatenate(
        [
            jnp.where(low, table[:, 2 * p : 2 * p + 1], table[:, 2 * p + 1 : 2 * p + 2])
            for p in range(pairs)
        ],
        axis=1,
    )


def head_select(lanes):
    return (iota((lanes, 128), 0) // PS == iota((lanes, 128), 1)).astype(BF)


def head_sum(value):
    select = head_select(value.shape[1])
    return sum(dot(part, select) for part in pieces(value, 2))


def head_rows(row, lanes):
    mine = iota((lanes, 128), 0) // PS == iota((lanes, 128), 1)
    return jnp.sum(jnp.where(mine, row, 0.0), axis=1, keepdims=True)


def load_blocks(refs, dest, me, rows, sem):
    copies = [
        pltpu.make_async_copy(
            ref, dest.at[pl.ds(pl.multiple_of((me ^ k) * rows, 16), rows)], sem.at[k]
        )
        for k, ref in enumerate(refs)
    ]
    for copy in copies:
        copy.start()
    return copies


def conv_forward(cext, taps, bounds, start, width):
    col = start + iota((BLOCK, 1), 0)
    seg = segments(bounds, col)
    masks, pre = [], taps[KCONV : KCONV + 1, :]
    for k in range(KCONV):
        back = KCONV - 1 - k
        same = jnp.where(segments(bounds, col - back) == seg, 1.0, 0.0)
        masks.append(same)
        pre = pre + taps[k : k + 1, :] * (cext[pl.ds(8 - back, BLOCK), :] * same)
    return pre, masks


def scan_terms(raw, heads, bounds, start):
    z = raw + heads[0:1, :]
    step = jnp.maximum(z, 0.0) + jnp.log1p(jnp.exp(-jnp.abs(z)))
    rate = -jnp.exp(heads[1:2, :])
    log_decay = step * rate
    tri = (iota((BLOCK, BLOCK), 0) >= iota((BLOCK, BLOCK), 1)).astype(BF)
    cum = sum(dot(tri, part) for part in pieces(log_decay, 3))
    col = segments(bounds, start + iota((BLOCK, 1), 0))
    row = segments(bounds, start + iota((1, BLOCK), 1))
    before = segments(bounds, start - 1)
    last = segments(bounds, start + BLOCK - 1)
    below = iota((BLOCK, BLOCK), 0) >= iota((BLOCK, BLOCK), 1)
    bias = jnp.where(below, jnp.where(col == row, 0.0, -1e30), -1e30)
    tail = cum[BLOCK - 1 : BLOCK, :]
    enter = jnp.where(col == before, jnp.exp(cum), 0.0)
    end = jnp.where(col == last, jnp.exp(tail - cum), 0.0)
    keep = jnp.where(last == before, jnp.exp(tail), 0.0)
    return z, step, rate, cum, bias, enter, end, keep


def forward_kernel(n, heads, scal, *refs):
    xs, ws = refs[:n], refs[n : 2 * n]
    gain, taps, hp, skip = refs[2 * n : 2 * n + 4]
    normed_o, conv_o, raw_o, mixer_o, start_o = refs[2 * n + 4 : 2 * n + 9]
    xv, wv, cext, state, sem_x, sem_w = refs[2 * n + 9 :]
    lanes = heads * PS
    width = lanes + 2 * N
    b = pl.program_id(0)
    bounds = [scal[i] for i in range(2, scal.shape[0])]
    start = b * BLOCK

    @pl.when(b == 0)
    def _():
        me = scal[0]
        copies = load_blocks(xs, xv, me, BLOCK, sem_x)
        copies += load_blocks(ws, wv, me, ws[0].shape[0], sem_w)
        cext[0:8, :] = jnp.zeros((8, width), F32)
        state[...] = jnp.zeros_like(state)
        for copy in copies:
            copy.wait()

    x = xv[pl.ds(pl.multiple_of(start, BLOCK), BLOCK), :].astype(F32)
    scale = lax.rsqrt(jnp.mean(x * x, axis=1, keepdims=True) + EPS)
    normed = (x * scale * gain[...]).astype(BF)
    normed_o[...] = normed
    proj = dot(normed, wv[...]).astype(BF)
    conv_o[...] = proj[:, :width]
    raw = proj[:, width:].astype(F32)
    raw_o[...] = raw
    cext[8:, :] = proj[:, :width].astype(F32)
    pre, _ = conv_forward(cext, taps, bounds, start, width)
    cext[0:8, :] = cext[BLOCK:, :]
    act = pre * sigmoid(pre)
    low = act.astype(BF)
    full = act[:, :lanes]
    keys, query = low[:, lanes : lanes + N], low[:, lanes + N :]
    _, step, _, cum, bias, enter, end, keep = scan_terms(raw, hp, bounds, start)
    cum_t, step_t = cum.T, step.T
    gram = dot_nt(query, keys)
    start_state = state[...]
    start_o[0] = start_state
    inter = dot_nt(query, start_state.astype(BF)) * expand(enter, heads // 2)
    weighted = (full * expand(end * step, heads // 2)).astype(BF)
    state[...] = head_rows(keep, lanes) * start_state + dot_tn(weighted, keys)
    rest = inter + skip[...] * full
    first = iota((BLOCK, 2 * PS), 1) < PS
    for p in range(heads // 2):
        at = slice(2 * PS * p, 2 * PS * (p + 1))
        pair = low[:, at]
        halves = (jnp.where(first, pair, 0), jnp.where(first, 0, pair))
        for t in range(2):
            rows, cols = slice(128 * t, 128 * (t + 1)), slice(0, 128 * (t + 1))
            total = rest[rows, at]
            for i in range(2):
                h = 2 * p + i
                decay = jnp.exp(cum[rows, h : h + 1] - cum_t[h : h + 1, cols] + bias[rows, cols])
                weights = (gram[rows, cols] * decay * step_t[h : h + 1, cols]).astype(BF)
                total = total + dot(weights, halves[i][cols, :])
            mixer_o[rows, at] = total


def gate_kernel(n, scal, *refs):
    gs, ws = refs[:n], refs[n : 2 * n]
    normed, mixer, wo, gain = refs[2 * n : 2 * n + 4]
    raw_o, gno_o, stat_o = refs[2 * n + 4 : 2 * n + 7]
    gv, wv, sem_g, sem_w = refs[2 * n + 7 :]
    b = pl.program_id(0)

    @pl.when(b == 0)
    def _():
        me = scal[0]
        copies = load_blocks(gs, gv, me, BLOCK, sem_g)
        copies += load_blocks(ws, wv, me, ws[0].shape[0], sem_w)
        for copy in copies:
            copy.wait()

    raw = dot(normed[...], wv[...]).astype(BF)
    raw_o[...] = raw
    gate = raw.astype(F32)
    gated = mixer[...] * (gate * sigmoid(gate))
    g = gv[pl.ds(pl.multiple_of(b * BLOCK, BLOCK), BLOCK), :]
    gno = dot_nt(g, wo[...])
    gno_o[...] = gno
    first = jnp.sum(gated * gated, axis=1, keepdims=True)
    second = jnp.sum(gno * gain[...] * gated, axis=1, keepdims=True)
    lane = iota((BLOCK, 128), 1)
    both = jnp.where(lane == 0, first, jnp.where(lane == 1, second, 0.0))
    stat_o[...] = both.T[0:8, :]


def output_kernel(n, nd, inner, scal, *refs):
    gs = refs[:n]
    stats = refs[n : 2 * n]
    normed, mixer, raw, gno, wo, gain = refs[2 * n : 2 * n + 6]
    out_o, gssm_o, ggr_o, dwo_o, dwg_o = refs[2 * n + 6 : 2 * n + 11]
    gv, acc_o, acc_g, sem_g = refs[2 * n + 11 :]
    b = pl.program_id(0)

    @pl.when(b == 0)
    def _():
        copies = load_blocks(gs, gv, scal[0], BLOCK, sem_g)
        acc_o[...] = jnp.zeros_like(acc_o)
        acc_g[...] = jnp.zeros_like(acc_g)
        for copy in copies:
            copy.wait()

    stat = functools.reduce(lambda a, c: a + c, [s[...] for s in stats])
    stat = jnp.concatenate([stat, jnp.zeros((120, BLOCK), F32)], axis=0).T
    scale = lax.rsqrt(stat[:, 0:1] * (1.0 / inner) + EPS)
    mean = stat[:, 1:2] * (1.0 / inner)
    mix = mixer[...]
    gate = raw[...].astype(F32)
    sig = sigmoid(gate)
    act = gate * sig
    gated = mix * act
    normed_out = (gated * scale * gain[...]).astype(BF)
    g = gv[pl.ds(pl.multiple_of(b * BLOCK, BLOCK), BLOCK), :]
    out_o[0] = dot(normed_out, wo[...]).astype(BF)
    acc_o[...] += dot_tn(normed_out, g)
    grad_gated = scale * (gno[...] * gain[...] - gated * (mean * scale * scale))
    grad_raw = (grad_gated * mix * (sig * (1.0 + gate * (1.0 - sig)))).astype(BF)
    ggr_o[...] = grad_raw
    gssm_o[...] = (grad_gated * act).astype(BF)
    acc_g[...] += dot_tn(normed[...], grad_raw)

    @pl.when(b == pl.num_programs(0) - 1)
    def _():
        store_shares(acc_g, dwg_o, n, nd, scal)
        share = acc_o.shape[0] // nd
        for d in range(nd):
            dwo_o[d ^ scal[1] if nd > 1 else d] = acc_o[d * share : (d + 1) * share, :].astype(BF)


def store_shares(acc, out, n, nd, scal):
    rows = acc.shape[0] // n
    share = rows // nd
    for j in range(n):
        for d in range(nd):
            at = j * rows + d * share
            out[j ^ scal[0], d ^ scal[1] if nd > 1 else d] = acc[at : at + share, :].astype(BF)


def scan_kernel(n, nd, heads, scal, *refs):
    ws, wgs = refs[:n], refs[n : 2 * n]
    normed, conv, conv_before, raw, starts, gssm, ggr, taps, hp, skip = refs[2 * n : 2 * n + 10]
    gn_o, dw_o, small_o = refs[2 * n + 10 : 2 * n + 13]
    wv, wgv, cext, gext, end_grad, acc, ggram, ght, sem_w, sem_g = refs[2 * n + 13 :]
    lanes = heads * PS
    width = lanes + 2 * N
    i = pl.program_id(0)
    b = pl.num_programs(0) - 1 - i
    bounds = [scal[k] for k in range(2, scal.shape[0])]
    start = b * BLOCK
    pairs = heads // 2

    @pl.when(i == 0)
    def _():
        copies = load_blocks(ws, wv, scal[0], ws[0].shape[0], sem_w)
        copies += load_blocks(wgs, wgv, scal[0], wgs[0].shape[0], sem_g)
        gext[BLOCK:, :] = jnp.zeros((8, width), F32)
        end_grad[...] = jnp.zeros_like(end_grad)
        acc[...] = jnp.zeros_like(acc)
        small_o[...] = jnp.zeros_like(small_o)
        for copy in copies:
            copy.wait()

    halo = conv_before[8:16, :].astype(F32)
    cext[0:8, :] = jnp.where(b > 0, halo, 0.0)
    cext[8:, :] = conv[...].astype(F32)
    pre, masks = conv_forward(cext, taps, bounds, start, width)
    sig = sigmoid(pre)
    act = pre * sig
    low = act.astype(BF)
    full = act[:, :lanes]
    keys, query = low[:, lanes : lanes + N], low[:, lanes + N :]
    z, step, rate, cum, bias, enter, end, keep = scan_terms(raw[...], hp, bounds, start)
    cum_t, step_t, enter_t = cum.T, step.T, enter.T
    gram = dot_nt(query, keys)
    grad = gssm[...]
    grad_f = grad.astype(F32)
    grad_t = grad_f.T.astype(BF)
    first = iota((BLOCK, 2 * PS), 1) < PS
    lane = iota((128, 128), 1)
    row_totals = [jnp.zeros((128, 128), F32), jnp.zeros((128, 128), F32)]
    col_totals = []
    ggram[...] = jnp.zeros_like(ggram)
    for p in range(pairs):
        at = slice(2 * PS * p, 2 * PS * (p + 1))
        pair = low[:, at]
        halves = (jnp.where(first, pair, 0), jnp.where(first, 0, pair))
        for k in range(2):
            h = 2 * p + k
            own = slice(PS * h, PS * (h + 1))
            cols_total = None
            for t in range(2):
                rows, cols = slice(128 * t, 128 * (t + 1)), slice(0, 128 * (t + 1))
                decay = jnp.exp(cum[rows, h : h + 1] - cum_t[h : h + 1, cols] + bias[rows, cols])
                table = dot_nt(grad[rows, at], halves[k][cols, :])
                gram_here = gram[rows, cols]
                step_row = step_t[h : h + 1, cols]
                weights = (gram_here * decay * step_row).astype(BF)
                common = table * decay
                stepped = common * step_row
                ggram[rows, cols] += stepped
                col = jnp.sum(common * gram_here, axis=0, keepdims=True)
                total = jnp.sum(stepped * gram_here, axis=1, keepdims=True)
                row_totals[t] = jnp.where(lane == h, total, row_totals[t])
                part = dot(grad_t[own, rows], weights)
                if t == 0:
                    ght[own, 0:128] = part
                    cols_total = col
                else:
                    ght[own, 0:128] += part[:, 0:128]
                    ght[own, 128:256] = part[:, 128:256]
                    cols_total = col + jnp.concatenate(
                        [cols_total, jnp.zeros((1, 128), F32)], axis=1
                    )
            col_totals.append(cols_total)
    col_totals.append(jnp.zeros((128 - heads, BLOCK), F32))
    grad_step = jnp.concatenate(col_totals, axis=0).T
    grad_cum = jnp.concatenate(row_totals, axis=0) - step * grad_step
    gg = ggram[...].astype(BF)
    start_state = starts[0]
    start_low = start_state.astype(BF)
    grad_cum += head_sum(grad_f * dot_nt(query, start_low)) * enter
    entered = (grad_f * expand(enter, pairs)).astype(BF)
    grad_query = dot(gg, keys) + dot(entered, start_low)
    later = end_grad[...]
    end_low = later.astype(BF)
    scaled = end * step
    scaled_wide = expand(scaled, pairs)
    weighted = (full * scaled_wide).astype(BF)
    grad_weighted = dot_nt(keys, end_low)
    grad_keys = dot_tn(gg, query) + dot(weighted, end_low)
    grad_end = head_sum(grad_weighted * full)
    grad_step += grad_end * end
    end_terms = grad_end * scaled
    ones = jnp.ones((8, N), BF)
    held = sum(dot_nt(ones, part) for part in pieces(later * start_state, 2))
    grad_tail = jnp.sum(end_terms, axis=0, keepdims=True) + head_sum(held)[0:1, :] * keep
    final = iota((BLOCK, 1), 0) == BLOCK - 1
    grad_cum = grad_cum - end_terms + jnp.where(final, grad_tail, 0.0)
    upper = (iota((BLOCK, BLOCK), 0) <= iota((BLOCK, BLOCK), 1)).astype(BF)
    grad_log = sum(dot(upper, part) for part in pieces(grad_cum, 3))
    grad_step += grad_log * rate
    grad_rate = jnp.sum(grad_log * step, axis=0, keepdims=True)
    grad_heads = ght[...].T + grad_weighted * scaled_wide + grad_f * skip[...]
    grad_skip = jnp.sum(grad_f * full, axis=0, keepdims=True)
    grad_act = jnp.concatenate([grad_heads, grad_keys, grad_query], axis=1)
    grad_pre = grad_act * (sig * (1.0 + pre * (1.0 - sig)))
    gext[0:BLOCK, :] = grad_pre
    position = start + iota((BLOCK, 1), 0)
    seg = segments(bounds, position)
    grad_conv = jnp.zeros((BLOCK, width), F32)
    for k in range(KCONV):
        back = KCONV - 1 - k
        taken = cext[pl.ds(8 - back, BLOCK), :] * masks[k]
        small_o[k : k + 1, 0:width] += jnp.sum(grad_pre * taken, axis=0, keepdims=True)
        same = jnp.where(segments(bounds, position + back) == seg, 1.0, 0.0)
        grad_conv += taps[k : k + 1, :] * (gext[pl.ds(back, BLOCK), :] * same)
    small_o[4:5, 0:width] += jnp.sum(grad_pre, axis=0, keepdims=True)
    gext[BLOCK:, :] = gext[0:8, :]
    grad_raw = grad_step * sigmoid(z)
    small_o[0:1, width : width + 128] += jnp.sum(grad_raw, axis=0, keepdims=True)
    small_o[1:2, width : width + 128] += grad_rate * rate
    small_o[2:3, width : width + 128] += head_sum(jnp.broadcast_to(grad_skip, (8, lanes)))[0:1, :]
    here = normed[...]
    raw_low = grad_raw.astype(BF)
    small_o[:, width + 128 :] += dot_tn(raw_low, here)[0:8, :]
    conv_low = grad_conv.astype(BF)
    acc[...] += dot_tn(here, conv_low)
    gn = dot_nt(jnp.concatenate([conv_low, raw_low], axis=1), wv[...]) + dot_nt(ggr[...], wgv[...])
    gn_o[0] = gn.astype(BF)
    geared = jnp.concatenate(
        [grad_t[PS * h : PS * (h + 1), :].astype(F32) * enter_t[h : h + 1, :] for h in range(heads)],
        axis=0,
    ).astype(BF)
    end_grad[...] = head_rows(keep, lanes) * later + dot(geared, query)

    @pl.when(i == pl.num_programs(0) - 1)
    def _():
        store_shares(acc, dw_o, n, nd, scal)


def weights_kernel(n, own_heads, scal, gate, conv, step, weight, gain, out, gain_out):
    own = own_heads * PS
    me = scal[0]
    gate_v, conv_v = gate[0].astype(F32), conv[0].astype(F32)
    lanes = gate_v.shape[1] // n
    for q in range(n):

        @pl.when(me == q)
        def _(q=q):
            for k in range(n):
                at = (q ^ k) * own
                out[:, at : at + own] = gate_v[:, k * lanes : k * lanes + own]
                out[:, DI + at : DI + at + own] = conv_v[:, k * lanes : k * lanes + own]

    out[:, 2 * DI : 2 * DI + 2 * N] = conv_v[:, n * lanes :]
    out[:, 2 * DI + 2 * N :] = step[...]
    dots = jnp.sum(out[...] * weight[...].astype(F32), axis=1, keepdims=True)
    gain_out[...] = dots / gain[...]


def out_weight_kernel(scal, share, weight, gain, out, gain_out):
    value = share[0].astype(F32)
    out[...] = value
    gain_out[...] = jnp.sum(value * weight[...].astype(F32), axis=1, keepdims=True) / gain[...]


def xor(value, axis, k):
    return lax.ppermute(value, axis, [(s, s ^ k) for s in range(lax.axis_size(axis))])


def gather_xor(value, axis):
    out = [value]
    for k in range(1, lax.axis_size(axis)):
        out.append(xor(value, axis, k) if k % 2 == 0 or k == 1 else xor(out[k - 1], axis, 1))
    return out


def by_owner(parts, me):
    stacked = jnp.stack(parts)
    return [lax.dynamic_index_in_dim(stacked, me ^ j, 0, False) for j in range(len(parts))]


def stages(count):
    out, low = [], 0
    bits = count.bit_length() - 1
    while low < bits:
        take = 1 if low == 0 else min(2, bits - low)
        out.append((low, take))
        low += take
    return out


def scatter_dp(value, dim):
    total = value
    for low, take in stages(value.shape[dim]):
        radix = 1 << take
        shape = total.shape
        total = total.reshape(shape[:dim] + (shape[dim] // radix, radix) + shape[dim + 1 :])
        index = lambda m: (slice(None),) * (dim + 1) + (m,)
        recv = [xor(total[index(m)], "dp", m << low) for m in range(1, radix)]
        mine = total[index(0)].astype(F32)
        for r in recv:
            mine = mine + r.astype(F32)
        total = mine.astype(BF)
    return total.reshape(total.shape[:dim] + total.shape[dim + 1 :])


def gather_dp(value):
    count = lax.axis_size("dp")
    out = value[None]
    for low, take in reversed(stages(count)):
        out = jnp.concatenate([out] + [xor(out, "dp", m << low) for m in range(1, 1 << take)], 0)
    order = [0]
    for low, take in reversed(stages(count)):
        order = [o | (m << low) for m in range(1 << take) for o in order]
    return out, order


def call(kernel, name, grid, scal, in_specs, args, out_specs, out_shape, scratch, flops, bytes_):
    return pl.pallas_call(
        kernel,
        grid_spec=pltpu.PrefetchScalarGridSpec(
            num_scalar_prefetch=1,
            grid=grid,
            in_specs=in_specs,
            out_specs=out_specs,
            scratch_shapes=scratch,
        ),
        out_shape=out_shape,
        name=name,
        compiler_params=pltpu.CompilerParams(vmem_limit_bytes=VMEM_LIMIT),
        cost_estimate=pl.CostEstimate(flops=flops, bytes_accessed=bytes_, transcendentals=0),
    )(scal, *args)


def local(
    block_input,
    out_cotangent,
    doc_lengths,
    norm_gain,
    in_weight,
    conv_weight,
    conv_bias,
    step_bias,
    decay_log,
    skip_gain,
    out_gain,
    out_weight,
):
    n, ndp = lax.axis_size("fsdp"), lax.axis_size("dp")
    me, dpi = lax.axis_index("fsdp"), lax.axis_index("dp")
    _, toks, model = block_input.shape
    length = toks * n
    nb = length // BLOCK
    own_heads = H // n
    heads = own_heads + own_heads % 2
    own, lanes = own_heads * PS, heads * PS
    width = lanes + 2 * N
    rows = model // n
    share = rows // ndp
    nd = ndp if share % 8 == 0 else 1
    x_own, g_own = block_input[0], out_cotangent[0]
    bounds = jnp.cumsum(doc_lengths[0])[:-1].astype(jnp.int32)
    scal = jnp.concatenate([jnp.stack([me, dpi]).astype(jnp.int32), bounds])

    small = jnp.concatenate([norm_gain, conv_bias, conv_weight.reshape(-1)])
    small = jnp.pad(small, (0, -small.shape[0] % 1024)).reshape(-1, 128)
    xs = gather_xor(x_own, "fsdp")
    smalls = by_owner(
        [small] + [xor(small, "fsdp", k) for k in range(1, n)], me
    )
    flat = jnp.stack(smalls).reshape(n, -1)
    chans = CONVCH // n
    gain_full = flat[:, :rows].reshape(1, model).astype(F32)
    conv_full = jnp.concatenate(
        [
            flat[:, rows + chans : rows + chans * (1 + KCONV)]
            .reshape(n, KCONV, chans)
            .transpose(1, 0, 2)
            .reshape(KCONV, CONVCH),
            flat[:, rows : rows + chans].reshape(1, CONVCH),
        ],
        axis=0,
    ).astype(F32)
    conv_heads = lax.dynamic_slice_in_dim(conv_full, me * own, own, 1)
    taps = jnp.concatenate(
        [jnp.pad(conv_heads, ((0, 0), (0, lanes - own))), conv_full[:, DI:]], axis=1
    )
    taps = jnp.pad(taps, ((0, 3), (0, 0)))
    hp = jnp.stack([step_bias, decay_log]).astype(F32)
    hp = jnp.pad(hp, ((0, 6), (0, 128 - own_heads)))
    skip = jnp.pad(jnp.repeat(skip_gain.astype(F32), PS), (0, lanes - own)).reshape(1, lanes)

    def columns(first, size, padded):
        part = in_weight[:, first : first + n * size].reshape(rows, n, size).transpose(1, 0, 2)
        return jnp.pad(part, ((0, 0), (0, 0), (0, padded - size)))

    shared = jnp.broadcast_to(in_weight[None, :, 2 * DI : 2 * DI + 2 * N], (n, rows, 2 * N))
    conv_cols = jnp.concatenate(
        [columns(DI, own, lanes), shared, columns(2 * DI + 2 * N, own_heads, 128)], axis=2
    )
    gate_cols = columns(0, own, lanes)

    def exchange(stacked):
        mine = [lax.dynamic_index_in_dim(stacked, me ^ k, 0, False) for k in range(n)]
        return [mine[0]] + [xor(mine[k], "fsdp", k) for k in range(1, n)]

    ws = exchange(conv_cols)
    wgs = exchange(gate_cols)
    gs = gather_xor(g_own, "fsdp")

    any_spec = pl.BlockSpec(memory_space=ANY)

    def whole(*shape):
        return pl.BlockSpec(shape, lambda b, s: (0,) * len(shape))

    def tokens(cols):
        return pl.BlockSpec((BLOCK, cols), lambda b, s: (b, 0))

    shape = jax.ShapeDtypeStruct
    normed, conv_in, raw_step, mixer, starts = call(
        functools.partial(forward_kernel, n, heads),
        "forward",
        (nb,),
        scal,
        [any_spec] * (2 * n) + [whole(1, model), whole(8, width), whole(8, 128), whole(1, lanes)],
        (*xs, *ws, gain_full, taps, hp, skip),
        [
            tokens(model),
            tokens(width),
            tokens(128),
            tokens(lanes),
            pl.BlockSpec((1, lanes, N), lambda b, s: (b, 0, 0)),
        ],
        [
            shape((length, model), BF),
            shape((length, width), BF),
            shape((length, 128), F32),
            shape((length, lanes), F32),
            shape((nb, lanes, N), F32),
        ],
        [
            pltpu.VMEM((length, model), BF),
            pltpu.VMEM((model, width + 128), BF),
            pltpu.VMEM((8 + BLOCK, width), F32),
            pltpu.VMEM((lanes, N), F32),
            pltpu.SemaphoreType.DMA((n,)),
            pltpu.SemaphoreType.DMA((n,)),
        ],
        9 * 10**9,
        10**7,
    )

    out_w = jnp.pad(out_weight, ((0, lanes - own), (0, 0)))
    out_g = jnp.pad(out_gain.astype(F32), (0, lanes - own)).reshape(1, lanes)
    raw_gate, gno, stat = call(
        functools.partial(gate_kernel, n),
        "gate",
        (nb,),
        scal,
        [any_spec] * (2 * n)
        + [tokens(model), tokens(lanes), whole(lanes, model), whole(1, lanes)],
        (*gs, *wgs, normed, mixer, out_w, out_g),
        [tokens(lanes), tokens(lanes), pl.BlockSpec((8, BLOCK), lambda b, s: (0, b))],
        [
            shape((length, lanes), BF),
            shape((length, lanes), F32),
            shape((8, length), F32),
        ],
        [
            pltpu.VMEM((length, model), BF),
            pltpu.VMEM((model, lanes), BF),
            pltpu.SemaphoreType.DMA((n,)),
            pltpu.SemaphoreType.DMA((n,)),
        ],
        2 * 10**9,
        10**7,
    )
    stats = [stat] + [xor(stat, "fsdp", k) for k in range(1, n)]

    out_part, gssm, ggr, dwo, dwg = call(
        functools.partial(output_kernel, n, nd, DI),
        "output",
        (nb,),
        scal,
        [any_spec] * n
        + [pl.BlockSpec((8, BLOCK), lambda b, s: (0, b))] * n
        + [tokens(model), tokens(lanes), tokens(lanes), tokens(lanes)]
        + [whole(lanes, model), whole(1, lanes)],
        (*gs, *stats, normed, mixer, raw_gate, gno, out_w, out_g),
        [
            pl.BlockSpec((1, BLOCK, model), lambda b, s: (b ^ s[0], 0, 0)),
            tokens(lanes),
            tokens(lanes),
            whole(nd, lanes // nd, model),
            whole(n, nd, rows // nd, lanes),
        ],
        [
            shape((nb, BLOCK, model), BF),
            shape((length, lanes), BF),
            shape((length, lanes), BF),
            shape((nd, lanes // nd, model), BF),
            shape((n, nd, rows // nd, lanes), BF),
        ],
        [
            pltpu.VMEM((length, model), BF),
            pltpu.VMEM((lanes, model), F32),
            pltpu.VMEM((model, lanes), F32),
            pltpu.SemaphoreType.DMA((n,)),
        ],
        3 * 10**9,
        10**7,
    )

    def token_sum(parts):
        paired = parts.reshape(n // 2, 2, BLOCK, model)
        other = xor(paired[:, 1], "fsdp", 1)
        both = (paired[:, 0].astype(F32) + other.astype(F32)).astype(BF)
        total = both[0].astype(F32)
        for k in range(2, n, 2):
            total = total + xor(both[k // 2], "fsdp", k).astype(F32)
        return total

    def row_sum(shares):
        mine = scatter_dp(shares, 1) if nd > 1 else shares[:, 0]
        return [mine[0]] + [xor(mine[k], "fsdp", k) for k in range(1, n)]

    def spread(value):
        if nd == 1:
            return lax.psum(value.astype(BF), "dp")[None]
        out, order = gather_dp(value.astype(BF))
        return out

    order = gather_order(ndp) if nd > 1 else [0]

    gate_share = spread(jnp.concatenate(row_sum(dwg), axis=1))
    wo_share = spread(scatter_dp(dwo, 0) if nd > 1 else dwo[0])
    result = x_own.astype(F32) + token_sum(out_part)
    block_output = result.astype(BF)[None]

    back = lambda b: nb - 1 - b

    def tokens_back(cols):
        return pl.BlockSpec((BLOCK, cols), lambda b, s: (back(b), 0))

    gn_part, dw, small_grads = call(
        functools.partial(scan_kernel, n, nd, heads),
        "scan_back",
        (nb,),
        scal,
        [any_spec] * (2 * n)
        + [
            tokens_back(model),
            tokens_back(width),
            pl.BlockSpec((16, width), lambda b, s: (jnp.maximum(back(b) * (BLOCK // 16) - 1, 0), 0)),
            tokens_back(128),
            pl.BlockSpec((1, lanes, N), lambda b, s: (back(b), 0, 0)),
            tokens_back(lanes),
            tokens_back(lanes),
            whole(8, width),
            whole(8, 128),
            whole(1, lanes),
        ],
        (*ws, *wgs, normed, conv_in, conv_in, raw_step, starts, gssm, ggr, taps, hp, skip),
        [
            pl.BlockSpec((1, BLOCK, model), lambda b, s: (back(b) ^ s[0], 0, 0)),
            whole(n, nd, rows // nd, width),
            whole(8, width + 128 + model),
        ],
        [
            shape((nb, BLOCK, model), BF),
            shape((n, nd, rows // nd, width), BF),
            shape((8, width + 128 + model), F32),
        ],
        [
            pltpu.VMEM((model, width + 128), BF),
            pltpu.VMEM((model, lanes), BF),
            pltpu.VMEM((8 + BLOCK, width), F32),
            pltpu.VMEM((BLOCK + 8, width), F32),
            pltpu.VMEM((lanes, N), F32),
            pltpu.VMEM((model, width), F32),
            pltpu.VMEM((BLOCK, BLOCK), F32),
            pltpu.VMEM((lanes, BLOCK), F32),
            pltpu.SemaphoreType.DMA((n,)),
            pltpu.SemaphoreType.DMA((n,)),
        ],
        12 * 10**9,
        10**7,
    )

    conv_parts = row_sum(dw)
    shared_sum = conv_parts[0][:, lanes:].astype(F32)
    for part in conv_parts[1:]:
        shared_sum = shared_sum + part[:, lanes:].astype(F32)
    conv_share = spread(
        jnp.concatenate([part[:, :lanes] for part in conv_parts] + [shared_sum.astype(BF)], axis=1)
    )

    total_in = token_sum(gn_part)
    inputs = x_own.astype(F32)
    scale_in = lax.rsqrt(jnp.mean(inputs * inputs, axis=-1, keepdims=True) + EPS)
    gained = total_in * gain_full
    input_grad = scale_in * (
        gained - inputs * jnp.mean(gained * inputs, axis=-1, keepdims=True) * scale_in * scale_in
    ) + g_own.astype(F32)
    input_grad = input_grad.astype(BF)[None]

    if nd > 1:
        for low, take in stages(ndp):
            small_grads = small_grads + sum(
                xor(small_grads, "dp", m << low) for m in range(1, 1 << take)
            )
    else:
        small_grads = lax.psum(small_grads, "dp")
    parts = [small_grads] + [xor(small_grads, "fsdp", k) for k in range(1, n)]
    ordered = by_owner(parts, me)
    conv_grads = jnp.concatenate(
        [part[:5, :own] for part in ordered] + [sum(part[:5, lanes:width] for part in parts)], axis=1
    )
    conv_grads = lax.dynamic_slice_in_dim(conv_grads, me * chans, chans, 1)
    head_grads = small_grads[:3, width : width + own_heads]
    step_rows = jnp.concatenate([part[:own_heads, width + 128 :] for part in ordered], axis=0)
    step_cols = lax.dynamic_slice_in_dim(step_rows, me * rows, rows, 1).T

    def place(e, s):
        return functools.reduce(lambda a, c: jnp.where(e == c[0], c[1], a), list(enumerate(order)), 0) ^ (
            s[1] if nd > 1 else 0
        )

    part_rows = rows // nd
    grad_in, grad_gain = call(
        functools.partial(weights_kernel, n, own_heads),
        "in_weight_grad",
        (nd,),
        scal,
        [
            pl.BlockSpec((1, part_rows, n * lanes), lambda e, s: (e, 0, 0)),
            pl.BlockSpec((1, part_rows, n * lanes + 2 * N), lambda e, s: (e, 0, 0)),
            pl.BlockSpec((part_rows, H), lambda e, s: (place(e, s), 0)),
            pl.BlockSpec((part_rows, in_weight.shape[1]), lambda e, s: (place(e, s), 0)),
            pl.BlockSpec((part_rows, 1), lambda e, s: (place(e, s), 0)),
        ],
        (gate_share, conv_share, step_cols, in_weight, norm_gain.astype(F32).reshape(rows, 1)),
        [
            pl.BlockSpec((part_rows, in_weight.shape[1]), lambda e, s: (place(e, s), 0)),
            pl.BlockSpec((part_rows, 1), lambda e, s: (place(e, s), 0)),
        ],
        [shape(in_weight.shape, F32), shape((rows, 1), F32)],
        [],
        10**6,
        6 * 10**6,
    )
    own_rows = lanes // nd
    grad_out, grad_out_gain = call(
        out_weight_kernel,
        "out_weight_grad",
        (nd,),
        scal,
        [
            pl.BlockSpec((1, own_rows, model), lambda e, s: (e, 0, 0)),
            pl.BlockSpec((own_rows, model), lambda e, s: (place(e, s), 0)),
            pl.BlockSpec((own_rows, 1), lambda e, s: (place(e, s), 0)),
        ],
        (wo_share, out_w, jnp.pad(out_gain.astype(F32), (0, lanes - own), constant_values=1.0).reshape(lanes, 1)),
        [
            pl.BlockSpec((own_rows, model), lambda e, s: (place(e, s), 0)),
            pl.BlockSpec((own_rows, 1), lambda e, s: (place(e, s), 0)),
        ],
        [shape((lanes, model), F32), shape((lanes, 1), F32)],
        [],
        10**6,
        3 * 10**6,
    )
    return (
        block_output,
        input_grad,
        grad_gain.reshape(rows),
        grad_in,
        conv_grads[:KCONV],
        conv_grads[KCONV],
        head_grads[0],
        head_grads[1],
        head_grads[2],
        grad_out_gain[:own].reshape(own),
        grad_out[:own],
    )


def gather_order(count):
    order = [0]
    for low, take in reversed(stages(count)):
        order = [o | (m << low) for m in range(1 << take) for o in order]
    return order


def solution(mesh):
    return jax.shard_map(
        local,
        mesh=mesh,
        in_specs=(
            P("dp", "fsdp", None),
            P("dp", "fsdp", None),
            P("dp", None),
            P("fsdp"),
            P("fsdp", None),
            P(None, "fsdp"),
            P("fsdp"),
            P("fsdp"),
            P("fsdp"),
            P("fsdp"),
            P("fsdp"),
            P("fsdp", None),
        ),
        out_specs=(
            P("dp", "fsdp", None),
            P("dp", "fsdp", None),
            P("fsdp"),
            P("fsdp", None),
            P(None, "fsdp"),
            P("fsdp"),
            P("fsdp"),
            P("fsdp"),
            P("fsdp"),
            P("fsdp"),
            P("fsdp", None),
        ),
        check_vma=False,
    )
```

time: 389 us -> 239 us (0.61)
  blocking collectives: 101 us -> 0 us
  waiting for transfers between devices: 142 us -> 60.4 us
  Pallas kernels: 0 us -> 72 us
  starting transfers between devices: 3.79 us -> 60.9 us
  matrix products: 44.8 us -> 0 us
  other arithmetic: 51.9 us -> 12.9 us
  between operations: 20.6 us -> 1.38 us
  local copies, waits for them, and re-layouts: 22.6 us -> 30.1 us
    pallas_call x0 -> x6, Pallas kernels: none -> 72 us  [call(): pl.pallas_call(kernel, grid_spec=pltpu.PrefetchScalarGridSpec(num_scalar_...]
    psum x2 -> x0, blocking collectives: 60.4 us -> none  [the longest x1 39.8 us: local(): head_total = lax.psum(head_terms, ('fsdp', 'dp'))]
    ppermute x2 -> x59, waiting for transfers between devices: 0.7 us -> 60.4 us  [xor(): lax.ppermute(value, axis, [(s, s ^ k) for s in range(lax.axis_size(axis))])]
    ppermute x2 -> x59, starting transfers between devices: 3.47 us -> 60.9 us  [xor(): lax.ppermute(value, axis, [(s, s ^ k) for s in range(lax.axis_size(axis))])]
    all_gather x4 -> x0, waiting for transfers between devices: 51.8 us -> none  [the longest x1 19.9 us: local(): lax.all_gather(in_weight, 'fsdp', axis=0, tiled=True)]
    reduce_scatter x2 -> x0, waiting for transfers between devices: 46 us -> none  [the longest x1 46 us: local(): lax.psum_scatter(grad_in_weight.astype(jnp.bfloat16), 'fsdp', scatter_dim...]
    dot_general x20 -> x0, matrix products: 44.8 us -> none  [the longest x1 5.29 us: block_backward(): jnp.einsum('thp,shp->hts', grad_ssm, heads_low, preferred_element_type=jn...]
    psum x1 -> x0, waiting for transfers between devices: 42.4 us -> none  [local(): lax.psum(partial_sums[1].astype(jnp.bfloat16), 'dp').astype(jnp.float32)]
  transfers between devices with their start and end apart: 10 -> 59, of which waited for: 7 -> 28; matrix products, arithmetic and copies ran while one was open for 22% -> 15% of each run, Pallas kernels for 0% -> 12%
where the time goes in v1:
time: 239 us; the launch traced here: 238 us
  Pallas kernels  72 us (30%)
  starting transfers between devices  60.9 us (25%)
  waiting for transfers between devices  60.4 us (25%)
  local copies, waits for them, and re-layouts  30.1 us (13%)
  other arithmetic  12.9 us (5%)
    pallas_call x6, Pallas kernels, call(): pl.pallas_call(kernel, grid_spec=pltpu.PrefetchScalarGridSpec(num_scalar_...  72 us
    ppermute x59, starting transfers between devices, xor(): lax.ppermute(value, axis, [(s, s ^ k) for s in range(lax.axis_size(axis))])  60.9 us
    ppermute x59, waiting for transfers between devices, xor(): lax.ppermute(value, axis, [(s, s ^ k) for s in range(lax.axis_size(axis))])  60.4 us
    unnamed x91, local copies, waits for them, and re-layouts  10.5 us
  transfers between devices with their start and end apart: 59, of which 28 were waited for; matrix products, arithmetic and copies ran while one was open for 15% of the time, Pallas kernels for 12%

profile of v1, /device:TPU:0, one launch (start us, length us, event | category | flops | bytes accessed | tf_op | source)
XLA Modules:
  0.0 237.7 jit_solution(3398186714490498018)
XLA Ops:
  1.2 2.6 %collective-permute-start.7 = (bf16[256,768]{1,0:T(8,128)(2,1)}, bf16[256,768]{1,0:T(8,128)(2,1)S(1)}, u32[]{:S(2)}, u32[]{:S(2)}) collective-permute-start(bf16[256,768]{1,0:T(8,128)(2,1)} %bitcast.235), channel_id=1, source_target_pairs={{0,16},{8,24},{16,0},{24,8},{1,17},{9,25},{17,1},{25,9},{2,18},{10... | collective-permute-start | bytes 1179656 | tf_op jit(solution)/shard_map/ppermute | solution.py:442
  4.5 1.4 concatenate.50
  6.0 1.7 collective-permute-start.13
  7.9 1.3 fusion.44
  11.1 1.2 constant_dynamic-slice_fusion.6
  16.3 1.1 collective-permute-start.11
  20.7 5.3 %collective-permute-done.10.refs_6_.refs_2_ = bf16[192,768]{1,0:T(8,128)(2,1)} collective-permute-done((bf16[192,768]{1,0:T(8,128)(2,1)S(1)}, bf16[192,768]{1,0:T(8,128)(2,1)}, u32[]{:S(2)}, u32[]{:S(2)}) %collective-permute-start.10) | collective-permute-done | bytes 294944 | tf_op jit(solution)/shard_map/ppermute | solution.py:442
  26.0 4.5 %collective-permute-done.11.refs_7_.refs_3_ = bf16[192,768]{1,0:T(8,128)(2,1)} collective-permute-done((bf16[192,768]{1,0:T(8,128)(2,1)S(1)}, bf16[192,768]{1,0:T(8,128)(2,1)}, u32[]{:S(2)}, u32[]{:S(2)}) %collective-permute-start.11) | collective-permute-done | bytes 294944 | tf_op jit(solution)/shard_map/ppermute | solution.py:442
  30.5 1.6 collective-permute-start.3
  32.5 8.2 %collective-permute-done.1.refs_2_ = bf16[256,768]{1,0:T(8,128)(2,1)S(1)} collective-permute-done((bf16[256,768]{1,0:T(8,128)(2,1)S(1)}, bf16[256,768]{1,0:T(8,128)(2,1)S(1)}, u32[]{:S(2)}, u32[]{:S(2)}) %collective-permute-start.1) | collective-permute-done | bytes 393248 | tf_op jit(solution)/shard_map/ppermute | solution.py:442
  41.1 14.7 %forward.1 = (bf16[1024,768]{1,0:T(8,128)(2,1)}, bf16[1024,640]{1,0:T(8,128)(2,1)}, f32[1024,128]{1,0:T(8,128)}, f32[1024,384]{1,0:T(8,128)}, f32[4,384,128]{2,1,0:T(8,128)}) custom-call(s32[5]{0:T(128)} %pad_add_fusion.scal, bf16[256,768]{1,0:T(8,128)(2,1)} %bitcast.236, bf16[256,768]{1,0:T(8,128)(2,1)} %copy-done.19, bf16[256,768]{1,0:T(8,128)(2,1)} %copy-done.20, ...), custom_call_target="tpu_custom_call" | custom-call | flops 8999999488 | bytes 10000000 | tf_op jit(solution)/shard_map/forward/pallas_call | solution.py:494
  56.9 7.7 %gate.1 = (bf16[1024,384]{1,0:T(8,128)(2,1)}, f32[1024,384]{1,0:T(8,128)}, f32[8,1024]{1,0:T(8,128)}) custom-call(s32[5]{0:T(128)} %pad_add_fusion.scal, bf16[256,768]{1,0:T(8,128)(2,1)} %bitcast.247, bf16[256,768]{1,0:T(8,128)(2,1)} %copy-done.22, bf16[256,768]{1,0:T(8,128)(2,1)} %copy-done.21, bf16[256,768]{1,0:T(8,128)(2,1)} %copy-done.23, ...), custom_call_target="tpu_custom_call" | custom-call | flops 2000000000 | bytes 10000000 | tf_op jit(solution)/shard_map/gate/pallas_call | solution.py:494
  64.8 1.6 collective-permute-start.16
  69.0 1.1 collective-permute-done.17.refs_7_
  70.6 10.2 %output.1 = (bf16[4,256,768]{2,1,0:T(8,128)(2,1)}, bf16[1024,384]{1,0:T(8,128)(2,1)}, bf16[1024,384]{1,0:T(8,128)(2,1)}, bf16[8,48,768]{2,1,0:T(8,128)(2,1)}, bf16[4,8,24,384]{3,2,1,0:T(8,128)(2,1)}) custom-call(s32[5]{0:T(128)} %pad_add_fusion.scal, bf16[256,768]{1,0:T(8,128)(2,1)} %bitcast.248, bf16[256,768]{1,0:T(8,128)(2,1)} %copy-done.22, ...), custom_call_target="tpu_custom_call" | custom-call | flops 3000000000 | bytes 10000000 | tf_op jit(solution)/shard_map/output/pallas_call | solution.py:494
  80.8 26.2 %scan_back.1 = (bf16[4,256,768]{2,1,0:T(8,128)(2,1)}, bf16[4,8,24,640]{3,2,1,0:T(8,128)(2,1)}, f32[8,1536]{1,0:T(8,128)}) custom-call(s32[5]{0:T(128)} %pad_add_fusion.scal, bf16[192,768]{1,0:T(8,128)(2,1)} %get-tuple-element.82.refs_4_.refs_0_, bf16[192,768]{1,0:T(8,128)(2,1)} %copy-done.24, bf16[192,768]{1,0:T(8,128)(2,1)} %collective-permute-done.10.refs_6_.refs_2_, ...), custom_call_target="tpu_custom_call" | custom-call | flops 12000000000 | bytes 10000000 | tf_op jit(solution)/shard_map/scan_back/pallas_call | solution.py:494
  107.1 2.2 slice_bitcast_fusion
  110.9 1.6 collective-permute-start.44
  112.5 2.5 %collective-permute-done.44 = f32[8,1536]{1,0:T(8,128)S(1)} collective-permute-done((f32[8,1536]{1,0:T(8,128)S(1)}, f32[8,1536]{1,0:T(8,128)S(1)}, u32[]{:S(2)}, u32[]{:S(2)}) %collective-permute-start.44) | collective-permute-done | bytes 49184 | tf_op jit(solution)/shard_map/ppermute | solution.py:442
  115.0 3.7 %collective-permute-start.47 = (f32[8,1536]{1,0:T(8,128)S(1)}, f32[8,1536]{1,0:T(8,128)S(1)}, u32[]{:S(2)}, u32[]{:S(2)}) collective-permute-start(f32[8,1536]{1,0:T(8,128)S(1)} %add.164), channel_id=1, source_target_pairs={{0,6},{1,7},{2,4},{3,5},{4,2},{5,3},{6,0},{7,1},{8,14},{9,15},{10,... | collective-permute-start | bytes 147464 | tf_op jit(solution)/shard_map/ppermute | solution.py:442
  121.8 1.0 collective-permute-done.45
  123.8 1.0 collective-permute-start.49
  126.1 1.1 collective-permute-done.50
  127.3 1.5 collective-permute-start.22
  128.8 1.1 collective-permute-start.51
  133.5 3.9 %collective-permute-done.22 = bf16[4,4,24,384]{3,2,0,1:T(8,128)(2,1)S(1)} collective-permute-done((bf16[4,4,24,384]{3,2,0,1:T(8,128)(2,1)}, bf16[4,4,24,384]{3,2,0,1:T(8,128)(2,1)S(1)}, u32[]{:S(2)}, u32[]{:S(2)}) %collective-permute-start.22) | collective-permute-done | bytes 294944 | tf_op jit(solution)/shard_map/ppermute | solution.py:442
  137.5 2.2 collective-permute-start.25
  139.7 1.4 collective-permute-start.24
  142.0 2.0 collective-permute-start.23
  144.0 1.0 fusion.21
  146.8 2.7 %collective-permute-start.52 = (bf16[1,48,768]{2,1,0:T(8,128)(2,1)S(1)}, bf16[1,48,768]{2,1,0:T(8,128)(2,1)S(1)}, u32[]{:S(2)}, u32[]{:S(2)}) collective-permute-start(bf16[1,48,768]{2,1,0:T(8,128)(2,1)S(1)} %get-tuple-element.96), channel_id=1, source_target_pairs={{0,2},{1,3},{2,0},{3,1},{4,6},{5,7},{6,4},{7,5},{8,10},{9,11},{10,... | collective-permute-start | bytes 221192 | tf_op jit(solution)/shard_map/ppermute | solution.py:442
  149.6 1.8 collective-permute-done.54
  151.4 1.4 collective-permute-done.53
  152.8 1.8 collective-permute-start.27
  154.7 1.6 collective-permute-start.33
  156.6 2.2 collective-permute-start.56
  158.8 3.0 %collective-permute-done.55 = bf16[1,48,768]{2,1,0:T(8,128)(2,1)S(1)} collective-permute-done((bf16[1,48,768]{2,1,0:T(8,128)(2,1)S(1)}, bf16[1,48,768]{2,1,0:T(8,128)(2,1)S(1)}, u32[]{:S(2)}, u32[]{:S(2)}) %collective-permute-start.55) | collective-permute-done | bytes 73760 | tf_op jit(solution)/shard_map/ppermute | solution.py:442
  161.9 1.8 collective-permute-start.57
  164.0 4.2 %collective-permute-done.57 = bf16[1,48,768]{2,1,0:T(8,128)(2,1)S(1)} collective-permute-done((bf16[1,48,768]{2,1,0:T(8,128)(2,1)S(1)}, bf16[1,48,768]{2,1,0:T(8,128)(2,1)S(1)}, u32[]{:S(2)}, u32[]{:S(2)}) %collective-permute-start.57) | collective-permute-done | bytes 73760 | tf_op jit(solution)/shard_map/ppermute | solution.py:442
  169.0 1.9 collective-permute-start.31
  170.9 2.6 %collective-permute-done.30 = bf16[1,24,1536]{2,1,0:T(8,128)(2,1)S(1)} collective-permute-done((bf16[1,24,1536]{2,1,0:T(8,128)(2,1)S(1)}, bf16[1,24,1536]{2,1,0:T(8,128)(2,1)S(1)}, u32[]{:S(2)}, u32[]{:S(2)}) %collective-permute-start.30) | collective-permute-done | bytes 73760 | tf_op jit(solution)/shard_map/ppermute | solution.py:442
  173.5 1.7 collective-permute-done.31
  175.4 2.0 collective-permute-start.36
  177.5 2.6 %collective-permute-start.35 = (bf16[4,1,24,640]{3,2,0,1:T(8,128)(2,1)S(1)}, bf16[4,1,24,640]{3,2,0,1:T(8,128)(2,1)S(1)}, u32[]{:S(2)}, u32[]{:S(2)}) collective-permute-start(bf16[4,1,24,640]{3,2,0,1:T(8,128)(2,1)S(1)} %get-tuple-element.93), channel_id=1, source_target_pairs={{0,4},{1,5},{2,6},{3,7},{4,0},{5,1},{6,2},{7,3},{8,12},{9,13},{10,... | collective-permute-start | bytes 368648 | tf_op jit(solution)/shard_map/ppermute | solution.py:442
  180.6 1.7 collective-permute-done.36
  182.3 3.9 %collective-permute-done.35 = bf16[4,1,24,640]{3,2,0,1:T(8,128)(2,1)S(1)} collective-permute-done((bf16[4,1,24,640]{3,2,0,1:T(8,128)(2,1)S(1)}, bf16[4,1,24,640]{3,2,0,1:T(8,128)(2,1)S(1)}, u32[]{:S(2)}, u32[]{:S(2)}) %collective-permute-start.35) | collective-permute-done | bytes 122912 | tf_op jit(solution)/shard_map/ppermute | solution.py:442
  187.2 1.0 collective-permute-start.39
  188.2 2.2 collective-permute-done.38
  190.8 3.2 %collective-permute-start.41 = (bf16[1,24,1792]{2,1,0:T(8,128)(2,1)S(1)}, bf16[1,24,1792]{2,1,0:T(8,128)(2,1)S(1)}, u32[]{:S(2)}, u32[]{:S(2)}) collective-permute-start(bf16[1,24,1792]{2,1,0:T(8,128)(2,1)S(1)} %bitcast.243), channel_id=1, source_target_pairs={{0,4},{1,5},{2,6},{3,7},{4,0},{5,1},{6,2},{7,3},{8,12},{9,13},{10,... | collective-permute-start | bytes 258056 | tf_op jit(solution)/shard_map/ppermute | solution.py:442
  194.1 1.1 collective-permute-start.42
  196.6 2.2 collective-permute-start.58
  198.8 2.3 collective-permute-done.41
  201.1 2.5 %collective-permute-start.32 = (bf16[4,24,1536]{2,1,0:T(8,128)(2,1)S(1)}, bf16[4,24,1536]{2,1,0:T(8,128)(2,1)}, u32[]{:S(2)}, u32[]{:S(2)}) collective-permute-start(bf16[4,24,1536]{2,1,0:T(8,128)(2,1)S(1)} %pad_maximum_fusion.1), channel_id=1, source_target_pairs={{0,1},{1,0},{2,3},{3,2},{4,5},{5,4},{6,7},{7,6},{8,9},{9,8},{10,11... | collective-permute-start | bytes 884744 | tf_op jit(solution)/shard_map/ppermute | solution.py:442
  207.6 6.1 %out_weight_grad.1 = (f32[384,768]{1,0:T(8,128)}, f32[384,1]{1,0:T(8,128)}) custom-call(s32[5]{0:T(128)} %pad_add_fusion.scal, bf16[8,48,768]{2,1,0:T(8,128)(2,1)} %copy-done.3, bf16[384,768]{1,0:T(8,128)(2,1)} %weight.3, f32[384,1]{1,0:T(8,128)} %reshape.253.gain), custom_call_target="tpu_custom_call" | custom-call | flops 1000000 | bytes 3000000 | tf_op jit(solution)/shard_map/out_weight_grad/pallas_call | solution.py:494
  213.7 1.7 reduce.1
  215.3 1.0 constant_dynamic-update-slice_fusion.gate
  217.2 1.6 fusion.1
  220.3 1.3 fusion.2
  221.7 1.3 collective-permute-start.19
  223.0 1.7 constant_dynamic-update-slice_fusion.10.conv
  224.7 7.0 %in_weight_grad.1 = (f32[192,3352]{1,0:T(8,128)}, f32[192,1]{1,0:T(8,128)}) custom-call(s32[5]{0:T(128)} %pad_add_fusion.scal, bf16[8,24,1536]{2,1,0:T(8,128)(2,1)} %copy-done.6, bf16[8,24,1792]{2,1,0:T(8,128)(2,1)} %constant_dynamic-update-slice_fusion.10.conv, f32[192,24]{1,0:T(8,128)} %bitcast.246, bf16[192,3352]{1,0:T(8,128)(2,1)} %weight.2, ...), custom_call_target="tpu_custom_call" | custom-call | flops 1000000 | bytes 6000000 | tf_op jit(solution)/shard_map/in_weight_grad/pallas_call | solution.py:494
  231.7 1.6 reduce
  233.6 2.8 %collective-permute-done.19 = bf16[256,768]{1,0:T(8,128)(2,1)S(1)} collective-permute-done((bf16[256,768]{1,0:T(8,128)(2,1)S(1)}, bf16[256,768]{1,0:T(8,128)(2,1)S(1)}, u32[]{:S(2)}, u32[]{:S(2)}) %collective-permute-start.19) | collective-permute-done | bytes 393248 | tf_op jit(solution)/shard_map/ppermute | solution.py:442
  236.4 1.3 fusion.18
  (240 shorter events, 40.8 us)
Async XLA Ops:
  0.7 31.5 %collective-permute-start.6 = (bf16[256,768]{1,0:T(8,128)(2,1)}, bf16[256,768]{1,0:T(8,128)(2,1)S(1)}, u32[]{:S(2)}, u32[]{:S(2)}) collective-permute-start(bf16[256,768]{1,0:T(8,128)(2,1)} %bitcast.234), channel_id=1, source_target_pairs={{0,8},{8,0},{16,24},{24,16},{1,9},{9,1},{17,25},{25,17},{2,10},{10... | collective-permute-start | bytes 1179656 | tf_op jit(solution)/shard_map/ppermute | solution.py:442
  1.2 18.1 %collective-permute-start.7 = (bf16[256,768]{1,0:T(8,128)(2,1)}, bf16[256,768]{1,0:T(8,128)(2,1)S(1)}, u32[]{:S(2)}, u32[]{:S(2)}) collective-permute-start(bf16[256,768]{1,0:T(8,128)(2,1)} %bitcast.235), channel_id=1, source_target_pairs={{0,16},{8,24},{16,0},{24,8},{1,17},{9,25},{17,1},{25,9},{2,18},{10... | collective-permute-start | bytes 1179656 | tf_op jit(solution)/shard_map/ppermute | solution.py:442
  6.0 9.6 %collective-permute-start.14 = (bf16[24,128]{1,0:T(8,128)(2,1)S(1)}, bf16[24,128]{1,0:T(8,128)(2,1)S(1)}, u32[]{:S(2)}, u32[]{:S(2)}) collective-permute-start(bf16[24,128]{1,0:T(8,128)(2,1)S(1)} %get-tuple-element.122), channel_id=1, source_target_pairs={{0,24},{8,16},{16,8},{24,0},{1,25},{9,17},{17,9},{25,1},{2,26},{10... | collective-permute-start | bytes 18440 | tf_op jit(solution)/shard_map/ppermute | solution.py:442
  6.0 10.0 %collective-permute-start.13 = (bf16[24,128]{1,0:T(8,128)(2,1)S(1)}, bf16[24,128]{1,0:T(8,128)(2,1)S(1)}, u32[]{:S(2)}, u32[]{:S(2)}) collective-permute-start(bf16[24,128]{1,0:T(8,128)(2,1)S(1)} %get-tuple-element.122), channel_id=1, source_target_pairs={{0,16},{8,24},{16,0},{24,8},{1,17},{9,25},{17,1},{25,9},{2,18},{10... | collective-permute-start | bytes 18440 | tf_op jit(solution)/shard_map/ppermute | solution.py:442
  7.8 8.5 %collective-permute-start.12 = (bf16[24,128]{1,0:T(8,128)(2,1)S(1)}, bf16[24,128]{1,0:T(8,128)(2,1)S(1)}, u32[]{:S(2)}, u32[]{:S(2)}) collective-permute-start(bf16[24,128]{1,0:T(8,128)(2,1)S(1)} %get-tuple-element.122), channel_id=1, source_target_pairs={{0,8},{8,0},{16,24},{24,16},{1,9},{9,1},{17,25},{25,17},{2,10},{10... | collective-permute-start | bytes 18440 | tf_op jit(solution)/shard_map/ppermute | solution.py:442
  15.6 2.3 collective-permute-start.9
  16.0 10.0 %collective-permute-start.10 = (bf16[192,768]{1,0:T(8,128)(2,1)S(1)}, bf16[192,768]{1,0:T(8,128)(2,1)}, u32[]{:S(2)}, u32[]{:S(2)}) collective-permute-start(bf16[192,768]{1,0:T(8,128)(2,1)S(1)} %get-tuple-element.80), channel_id=1, source_target_pairs={{0,16},{8,24},{16,0},{24,8},{1,17},{9,25},{17,1},{25,9},{2,18},{10... | collective-permute-start | bytes 884744 | tf_op jit(solution)/shard_map/ppermute | solution.py:442
  16.3 14.2 %collective-permute-start.11 = (bf16[192,768]{1,0:T(8,128)(2,1)S(1)}, bf16[192,768]{1,0:T(8,128)(2,1)}, u32[]{:S(2)}, u32[]{:S(2)}) collective-permute-start(bf16[192,768]{1,0:T(8,128)(2,1)S(1)} %get-tuple-element.79), channel_id=1, source_target_pairs={{0,24},{8,16},{16,8},{24,0},{1,25},{9,17},{17,9},{25,1},{2,26},{10... | collective-permute-start | bytes 884744 | tf_op jit(solution)/shard_map/ppermute | solution.py:442
  18.6 22.0 %collective-permute-start.1 = (bf16[256,768]{1,0:T(8,128)(2,1)S(1)}, bf16[256,768]{1,0:T(8,128)(2,1)S(1)}, u32[]{:S(2)}, u32[]{:S(2)}) collective-permute-start(bf16[256,768]{1,0:T(8,128)(2,1)S(1)} %bitcast.249), channel_id=1, source_target_pairs={{0,16},{8,24},{16,0},{24,8},{1,17},{9,25},{17,1},{25,9},{2,18},{10... | collective-permute-start | bytes 1179656 | tf_op jit(solution)/shard_map/ppermute | solution.py:442
  19.3 21.8 %copy-start.20 = (bf16[256,768]{1,0:T(8,128)(2,1)}, bf16[256,768]{1,0:T(8,128)(2,1)S(1)}, u32[]{:S(2)}) copy-start(bf16[256,768]{1,0:T(8,128)(2,1)S(1)} %collective-permute-done.7.refs_2_) | copy-start | bytes 1179652
  19.3 21.4 %collective-permute-start.8 = (bf16[256,768]{1,0:T(8,128)(2,1)S(1)}, bf16[256,768]{1,0:T(8,128)(2,1)}, u32[]{:S(2)}, u32[]{:S(2)}) collective-permute-start(bf16[256,768]{1,0:T(8,128)(2,1)S(1)} %collective-permute-done.7.refs_2_), channel_id=1, source_target_pairs={{0,8},{8,0},{16,24},{24,16},{1,9},{9,1},{17,25},{25,17},{2,10},{10... | collective-permute-start | bytes 1179656 | tf_op jit(solution)/shard_map/ppermute | solution.py:442
  26.0 29.9 %collective-permute-start = (bf16[256,768]{1,0:T(8,128)(2,1)S(1)}, bf16[256,768]{1,0:T(8,128)(2,1)S(1)}, u32[]{:S(2)}, u32[]{:S(2)}) collective-permute-start(bf16[256,768]{1,0:T(8,128)(2,1)S(1)} %bitcast.250), channel_id=1, source_target_pairs={{0,8},{8,0},{16,24},{24,16},{1,9},{9,1},{17,25},{25,17},{2,10},{10... | collective-permute-start | bytes 1179656 | tf_op jit(solution)/shard_map/ppermute | solution.py:442
  30.5 25.3 %collective-permute-start.3 = (bf16[192,384]{1,0:T(8,128)(2,1)S(1)}, bf16[192,384]{1,0:T(8,128)(2,1)S(1)}, u32[]{:S(2)}, u32[]{:S(2)}) collective-permute-start(bf16[192,384]{1,0:T(8,128)(2,1)S(1)} %bitcast.256), channel_id=1, source_target_pairs={{0,8},{8,0},{16,24},{24,16},{1,9},{9,1},{17,25},{25,17},{2,10},{10... | collective-permute-start | bytes 442376 | tf_op jit(solution)/shard_map/ppermute | solution.py:442
  32.1 23.7 %collective-permute-start.4 = (bf16[192,384]{1,0:T(8,128)(2,1)S(1)}, bf16[192,384]{1,0:T(8,128)(2,1)S(1)}, u32[]{:S(2)}, u32[]{:S(2)}) collective-permute-start(bf16[192,384]{1,0:T(8,128)(2,1)S(1)} %bitcast.255), channel_id=1, source_target_pairs={{0,16},{8,24},{16,0},{24,8},{1,17},{9,25},{17,1},{25,9},{2,18},{10... | collective-permute-start | bytes 442376 | tf_op jit(solution)/shard_map/ppermute | solution.py:442
  40.6 15.2 %copy-start.21 = (bf16[256,768]{1,0:T(8,128)(2,1)}, bf16[256,768]{1,0:T(8,128)(2,1)S(1)}, u32[]{:S(2)}) copy-start(bf16[256,768]{1,0:T(8,128)(2,1)S(1)} %collective-permute-done.1.refs_2_) | copy-start | bytes 1179652
  40.6 15.2 %collective-permute-start.5 = (bf16[192,384]{1,0:T(8,128)(2,1)S(1)}, bf16[192,384]{1,0:T(8,128)(2,1)S(1)}, u32[]{:S(2)}, u32[]{:S(2)}) collective-permute-start(bf16[192,384]{1,0:T(8,128)(2,1)S(1)} %bitcast.254), channel_id=1, source_target_pairs={{0,24},{8,16},{16,8},{24,0},{1,25},{9,17},{17,9},{25,1},{2,26},{10... | collective-permute-start | bytes 442376 | tf_op jit(solution)/shard_map/ppermute | solution.py:442
  40.7 15.3 %collective-permute-start.2 = (bf16[256,768]{1,0:T(8,128)(2,1)S(1)}, bf16[256,768]{1,0:T(8,128)(2,1)S(1)}, u32[]{:S(2)}, u32[]{:S(2)}) collective-permute-start(bf16[256,768]{1,0:T(8,128)(2,1)S(1)} %collective-permute-done.1.refs_2_), channel_id=1, source_target_pairs={{0,8},{8,0},{16,24},{24,16},{1,9},{9,1},{17,25},{25,17},{2,10},{10... | collective-permute-start | bytes 1179656 | tf_op jit(solution)/shard_map/ppermute | solution.py:442
  64.6 3.6 %collective-permute-start.15 = (f32[8,1024]{1,0:T(8,128)}, f32[8,1024]{1,0:T(8,128)S(1)}, u32[]{:S(2)}, u32[]{:S(2)}) collective-permute-start(f32[8,1024]{1,0:T(8,128)} %get-tuple-element.33.refs_4_), channel_id=1, source_target_pairs={{0,8},{8,0},{16,24},{24,16},{1,9},{9,1},{17,25},{25,17},{2,10},{10... | collective-permute-start | bytes 98312 | tf_op jit(solution)/shard_map/ppermute | solution.py:442
  64.8 4.1 %collective-permute-start.16 = (f32[8,1024]{1,0:T(8,128)}, f32[8,1024]{1,0:T(8,128)S(1)}, u32[]{:S(2)}, u32[]{:S(2)}) collective-permute-start(f32[8,1024]{1,0:T(8,128)} %get-tuple-element.33.refs_4_), channel_id=1, source_target_pairs={{0,16},{8,24},{16,0},{24,8},{1,17},{9,25},{17,1},{25,9},{2,18},{10... | collective-permute-start | bytes 98312 | tf_op jit(solution)/shard_map/ppermute | solution.py:442
  66.5 3.6 %collective-permute-start.17 = (f32[8,1024]{1,0:T(8,128)}, f32[8,1024]{1,0:T(8,128)S(1)}, u32[]{:S(2)}, u32[]{:S(2)}) collective-permute-start(f32[8,1024]{1,0:T(8,128)} %get-tuple-element.33.refs_4_), channel_id=1, source_target_pairs={{0,24},{8,16},{16,8},{24,0},{1,25},{9,17},{17,9},{25,1},{2,26},{10... | collective-permute-start | bytes 98312 | tf_op jit(solution)/shard_map/ppermute | solution.py:442
  109.3 107.9 %collective-permute-start.20 = (bf16[2,256,768]{2,1,0:T(8,128)(2,1)}, bf16[2,256,768]{2,1,0:T(8,128)(2,1)}, u32[]{:S(2)}, u32[]{:S(2)}) collective-permute-start(bf16[2,256,768]{2,1,0:T(8,128)(2,1)} %slice_bitcast_fusion), channel_id=1, source_target_pairs={{0,8},{8,0},{16,24},{24,16},{1,9},{9,1},{17,25},{25,17},{2,10},{10... | collective-permute-start | bytes 2359304 | tf_op jit(solution)/shard_map/ppermute | solution.py:442
  110.4 109.9 %collective-permute-start.18 = (bf16[2,256,768]{2,1,0:T(8,128)(2,1)}, bf16[2,256,768]{2,1,0:T(8,128)(2,1)}, u32[]{:S(2)}, u32[]{:S(2)}) collective-permute-start(bf16[2,256,768]{2,1,0:T(8,128)(2,1)} %slice_bitcast_fusion.2), channel_id=1, source_target_pairs={{0,8},{8,0},{16,24},{24,16},{1,9},{9,1},{17,25},{25,17},{2,10},{10... | collective-permute-start | bytes 2359304 | tf_op jit(solution)/shard_map/ppermute | solution.py:442
  110.9 4.2 %collective-permute-start.44 = (f32[8,1536]{1,0:T(8,128)S(1)}, f32[8,1536]{1,0:T(8,128)S(1)}, u32[]{:S(2)}, u32[]{:S(2)}) collective-permute-start(f32[8,1536]{1,0:T(8,128)S(1)} %copy-done.13), channel_id=1, source_target_pairs={{0,1},{1,0},{2,3},{3,2},{4,5},{5,4},{6,7},{7,6},{8,9},{9,8},{10,11... | collective-permute-start | bytes 147464 | tf_op jit(solution)/shard_map/ppermute | solution.py:442
  115.0 6.8 %collective-permute-start.47 = (f32[8,1536]{1,0:T(8,128)S(1)}, f32[8,1536]{1,0:T(8,128)S(1)}, u32[]{:S(2)}, u32[]{:S(2)}) collective-permute-start(f32[8,1536]{1,0:T(8,128)S(1)} %add.164), channel_id=1, source_target_pairs={{0,6},{1,7},{2,4},{3,5},{4,2},{5,3},{6,0},{7,1},{8,14},{9,15},{10,... | collective-permute-start | bytes 147464 | tf_op jit(solution)/shard_map/ppermute | solution.py:442
  118.7 4.1 %collective-permute-start.45 = (f32[8,1536]{1,0:T(8,128)S(1)}, f32[8,1536]{1,0:T(8,128)S(1)}, u32[]{:S(2)}, u32[]{:S(2)}) collective-permute-start(f32[8,1536]{1,0:T(8,128)S(1)} %add.164), channel_id=1, source_target_pairs={{0,2},{1,3},{2,0},{3,1},{4,6},{5,7},{6,4},{7,5},{8,10},{9,11},{10,... | collective-permute-start | bytes 147464 | tf_op jit(solution)/shard_map/ppermute | solution.py:442
  118.7 5.0 %collective-permute-start.46 = (f32[8,1536]{1,0:T(8,128)S(1)}, f32[8,1536]{1,0:T(8,128)S(1)}, u32[]{:S(2)}, u32[]{:S(2)}) collective-permute-start(f32[8,1536]{1,0:T(8,128)S(1)} %add.164), channel_id=1, source_target_pairs={{0,4},{1,5},{2,6},{3,7},{4,0},{5,1},{6,2},{7,3},{8,12},{9,13},{10,... | collective-permute-start | bytes 147464 | tf_op jit(solution)/shard_map/ppermute | solution.py:442
  123.7 3.6 %collective-permute-start.50 = (f32[8,1536]{1,0:T(8,128)S(1)}, f32[8,1536]{1,0:T(8,128)S(1)}, u32[]{:S(2)}, u32[]{:S(2)}) collective-permute-start(f32[8,1536]{1,0:T(8,128)S(1)} %add_add_fusion), channel_id=1, source_target_pairs={{0,24},{8,16},{16,8},{24,0},{1,25},{9,17},{17,9},{25,1},{2,26},{10... | collective-permute-start | bytes 147464 | tf_op jit(solution)/shard_map/ppermute | solution.py:442
  123.8 5.0 %collective-permute-start.49 = (f32[8,1536]{1,0:T(8,128)S(1)}, f32[8,1536]{1,0:T(8,128)S(1)}, u32[]{:S(2)}, u32[]{:S(2)}) collective-permute-start(f32[8,1536]{1,0:T(8,128)S(1)} %add_add_fusion), channel_id=1, source_target_pairs={{0,16},{8,24},{16,0},{24,8},{1,17},{9,25},{17,1},{25,9},{2,18},{10... | collective-permute-start | bytes 147464 | tf_op jit(solution)/shard_map/ppermute | solution.py:442
  124.7 5.2 %collective-permute-start.48 = (f32[8,1536]{1,0:T(8,128)S(1)}, f32[8,1536]{1,0:T(8,128)S(1)}, u32[]{:S(2)}, u32[]{:S(2)}) collective-permute-start(f32[8,1536]{1,0:T(8,128)S(1)} %add_add_fusion), channel_id=1, source_target_pairs={{0,8},{8,0},{16,24},{24,16},{1,9},{9,1},{17,25},{25,17},{2,10},{10... | collective-permute-start | bytes 147464 | tf_op jit(solution)/shard_map/ppermute | solution.py:442
  127.3 10.2 %collective-permute-start.22 = (bf16[4,4,24,384]{3,2,0,1:T(8,128)(2,1)}, bf16[4,4,24,384]{3,2,0,1:T(8,128)(2,1)S(1)}, u32[]{:S(2)}, u32[]{:S(2)}) collective-permute-start(bf16[4,4,24,384]{3,2,0,1:T(8,128)(2,1)} %bitcast.221), channel_id=1, source_target_pairs={{0,1},{1,0},{2,3},{3,2},{4,5},{5,4},{6,7},{7,6},{8,9},{9,8},{10,11... | collective-permute-start | bytes 884744 | tf_op jit(solution)/shard_map/ppermute | solution.py:442
  128.8 13.2 %collective-permute-start.51 = (bf16[4,48,768]{2,1,0:T(8,128)(2,1)}, bf16[4,48,768]{2,1,0:T(8,128)(2,1)S(1)}, u32[]{:S(2)}, u32[]{:S(2)}) collective-permute-start(bf16[4,48,768]{2,1,0:T(8,128)(2,1)} %slice_bitcast_fusion.8), channel_id=1, source_target_pairs={{0,1},{1,0},{2,3},{3,2},{4,5},{5,4},{6,7},{7,6},{8,9},{9,8},{10,11... | collective-permute-start | bytes 884744 | tf_op jit(solution)/shard_map/ppermute | solution.py:442
  137.5 17.2 %copy-start.9 = (bf16[4,4,1,24,640]{4,3,0,1,2:T(8,128)(2,1)S(1)}, bf16[4,4,1,24,640]{4,3,0,1,2:T(8,128)(2,1)}, u32[]{:S(2)}) copy-start(bf16[4,4,1,24,640]{4,3,0,1,2:T(8,128)(2,1)} %copy.119) | copy-start | bytes 1474564
  137.5 7.5 %collective-permute-start.25 = (bf16[4,1,24,384]{3,2,1,0:T(8,128)(2,1)S(1)}, bf16[4,1,24,384]{3,2,1,0:T(8,128)(2,1)S(1)}, u32[]{:S(2)}, u32[]{:S(2)}) collective-permute-start(bf16[4,1,24,384]{3,2,1,0:T(8,128)(2,1)S(1)} %get-tuple-element.100), channel_id=1, source_target_pairs={{0,6},{1,7},{2,4},{3,5},{4,2},{5,3},{6,0},{7,1},{8,14},{9,15},{10,... | collective-permute-start | bytes 221192 | tf_op jit(solution)/shard_map/ppermute | solution.py:442
  139.7 6.3 %collective-permute-start.24 = (bf16[4,1,24,384]{3,2,0,1:T(8,128)(2,1)S(1)}, bf16[4,1,24,384]{3,2,0,1:T(8,128)(2,1)S(1)}, u32[]{:S(2)}, u32[]{:S(2)}) collective-permute-start(bf16[4,1,24,384]{3,2,0,1:T(8,128)(2,1)S(1)} %get-tuple-element.101), channel_id=1, source_target_pairs={{0,4},{1,5},{2,6},{3,7},{4,0},{5,1},{6,2},{7,3},{8,12},{9,13},{10,... | collective-permute-start | bytes 221192 | tf_op jit(solution)/shard_map/ppermute | solution.py:442
  142.0 4.9 %collective-permute-start.23 = (bf16[4,1,24,384]{3,2,0,1:T(8,128)(2,1)S(1)}, bf16[4,1,24,384]{3,2,0,1:T(8,128)(2,1)S(1)}, u32[]{:S(2)}, u32[]{:S(2)}) collective-permute-start(bf16[4,1,24,384]{3,2,0,1:T(8,128)(2,1)S(1)} %get-tuple-element.99), channel_id=1, source_target_pairs={{0,2},{1,3},{2,0},{3,1},{4,6},{5,7},{6,4},{7,5},{8,10},{9,11},{10,... | collective-permute-start | bytes 221192 | tf_op jit(solution)/shard_map/ppermute | solution.py:442
  145.1 6.3 %collective-permute-start.54 = (bf16[1,48,768]{2,1,0:T(8,128)(2,1)S(1)}, bf16[1,48,768]{2,1,0:T(8,128)(2,1)S(1)}, u32[]{:S(2)}, u32[]{:S(2)}) collective-permute-start(bf16[1,48,768]{2,1,0:T(8,128)(2,1)S(1)} %get-tuple-element.97), channel_id=1, source_target_pairs={{0,6},{1,7},{2,4},{3,5},{4,2},{5,3},{6,0},{7,1},{8,14},{9,15},{10,... | collective-permute-start | bytes 221192 | tf_op jit(solution)/shard_map/ppermute | solution.py:442
  146.0 6.8 %collective-permute-start.53 = (bf16[1,48,768]{2,1,0:T(8,128)(2,1)S(1)}, bf16[1,48,768]{2,1,0:T(8,128)(2,1)S(1)}, u32[]{:S(2)}, u32[]{:S(2)}) collective-permute-start(bf16[1,48,768]{2,1,0:T(8,128)(2,1)S(1)} %get-tuple-element.98), channel_id=1, source_target_pairs={{0,4},{1,5},{2,6},{3,7},{4,0},{5,1},{6,2},{7,3},{8,12},{9,13},{10,... | collective-permute-start | bytes 221192 | tf_op jit(solution)/shard_map/ppermute | solution.py:442
  146.8 7.8 %collective-permute-start.52 = (bf16[1,48,768]{2,1,0:T(8,128)(2,1)S(1)}, bf16[1,48,768]{2,1,0:T(8,128)(2,1)S(1)}, u32[]{:S(2)}, u32[]{:S(2)}) collective-permute-start(bf16[1,48,768]{2,1,0:T(8,128)(2,1)S(1)} %get-tuple-element.96), channel_id=1, source_target_pairs={{0,2},{1,3},{2,0},{3,1},{4,6},{5,7},{6,4},{7,5},{8,10},{9,11},{10,... | collective-permute-start | bytes 221192 | tf_op jit(solution)/shard_map/ppermute | solution.py:442
  151.4 3.2 %collective-permute-start.28 = (bf16[24,384]{1,0:T(8,128)(2,1)S(1)}, bf16[24,384]{1,0:T(8,128)(2,1)S(1)}, u32[]{:S(2)}, u32[]{:S(2)}) collective-permute-start(bf16[24,384]{1,0:T(8,128)(2,1)S(1)} %get-tuple-element.111), channel_id=1, source_target_pairs={{0,24},{8,16},{16,8},{24,0},{1,25},{9,17},{17,9},{25,1},{2,26},{10... | collective-permute-start | bytes 55304 | tf_op jit(solution)/shard_map/ppermute | solution.py:442
  152.8 3.8 %collective-permute-start.27 = (bf16[24,384]{1,0:T(8,128)(2,1)S(1)}, bf16[24,384]{1,0:T(8,128)(2,1)S(1)}, u32[]{:S(2)}, u32[]{:S(2)}) collective-permute-start(bf16[24,384]{1,0:T(8,128)(2,1)S(1)} %get-tuple-element.112), channel_id=1, source_target_pairs={{0,16},{8,24},{16,0},{24,8},{1,17},{9,25},{17,1},{25,9},{2,18},{10... | collective-permute-start | bytes 55304 | tf_op jit(solution)/shard_map/ppermute | solution.py:442
  154.6 2.0 collective-permute-start.26
  154.7 20.6 %collective-permute-start.33 = (bf16[4,4,24,640]{3,2,0,1:T(8,128)(2,1)S(1)}, bf16[4,4,24,640]{3,2,0,1:T(8,128)(2,1)S(1)}, u32[]{:S(2)}, u32[]{:S(2)}) collective-permute-start(bf16[4,4,24,640]{3,2,0,1:T(8,128)(2,1)S(1)} %bitcast.241), channel_id=1, source_target_pairs={{0,1},{1,0},{2,3},{3,2},{4,5},{5,4},{6,7},{7,6},{8,9},{9,8},{10,11... | collective-permute-start | bytes 1474568 | tf_op jit(solution)/shard_map/ppermute | solution.py:442
  156.6 5.3 %collective-permute-start.55 = (bf16[1,48,768]{2,1,0:T(8,128)(2,1)S(1)}, bf16[1,48,768]{2,1,0:T(8,128)(2,1)S(1)}, u32[]{:S(2)}, u32[]{:S(2)}) collective-permute-start(bf16[1,48,768]{2,1,0:T(8,128)(2,1)S(1)} %get-tuple-element.76), channel_id=1, source_target_pairs={{0,2},{1,3},{2,0},{3,1},{4,6},{5,7},{6,4},{7,5},{8,10},{9,11},{10,... | collective-permute-start | bytes 221192 | tf_op jit(solution)/shard_map/ppermute | solution.py:442
  156.6 7.1 %collective-permute-start.56 = (bf16[1,48,768]{2,1,0:T(8,128)(2,1)S(1)}, bf16[1,48,768]{2,1,0:T(8,128)(2,1)S(1)}, u32[]{:S(2)}, u32[]{:S(2)}) collective-permute-start(bf16[1,48,768]{2,1,0:T(8,128)(2,1)S(1)} %get-tuple-element.76), channel_id=1, source_target_pairs={{0,4},{1,5},{2,6},{3,7},{4,0},{5,1},{6,2},{7,3},{8,12},{9,13},{10,... | collective-permute-start | bytes 221192 | tf_op jit(solution)/shard_map/ppermute | solution.py:442
  161.9 6.4 %collective-permute-start.57 = (bf16[1,48,768]{2,1,0:T(8,128)(2,1)S(1)}, bf16[1,48,768]{2,1,0:T(8,128)(2,1)S(1)}, u32[]{:S(2)}, u32[]{:S(2)}) collective-permute-start(bf16[1,48,768]{2,1,0:T(8,128)(2,1)S(1)} %get-tuple-element.76), channel_id=1, source_target_pairs={{0,6},{1,7},{2,4},{3,5},{4,2},{5,3},{6,0},{7,1},{8,14},{9,15},{10,... | collective-permute-start | bytes 221192 | tf_op jit(solution)/shard_map/ppermute | solution.py:442
  163.7 5.2 %collective-permute-start.29 = (bf16[1,24,1536]{2,1,0:T(8,128)(2,1)S(1)}, bf16[1,24,1536]{2,1,0:T(8,128)(2,1)S(1)}, u32[]{:S(2)}, u32[]{:S(2)}) collective-permute-start(bf16[1,24,1536]{2,1,0:T(8,128)(2,1)S(1)} %maximum_bitcast_fusion), channel_id=1, source_target_pairs={{0,2},{1,3},{2,0},{3,1},{4,6},{5,7},{6,4},{7,5},{8,10},{9,11},{10,... | collective-permute-start | bytes 221192 | tf_op jit(solution)/shard_map/ppermute | solution.py:442
  168.2 5.3 %collective-permute-start.30 = (bf16[1,24,1536]{2,1,0:T(8,128)(2,1)S(1)}, bf16[1,24,1536]{2,1,0:T(8,128)(2,1)S(1)}, u32[]{:S(2)}, u32[]{:S(2)}) collective-permute-start(bf16[1,24,1536]{2,1,0:T(8,128)(2,1)S(1)} %maximum_bitcast_fusion), channel_id=1, source_target_pairs={{0,4},{1,5},{2,6},{3,7},{4,0},{5,1},{6,2},{7,3},{8,12},{9,13},{10,... | collective-permute-start | bytes 221192 | tf_op jit(solution)/shard_map/ppermute | solution.py:442
  169.0 6.3 %collective-permute-start.31 = (bf16[1,24,1536]{2,1,0:T(8,128)(2,1)S(1)}, bf16[1,24,1536]{2,1,0:T(8,128)(2,1)S(1)}, u32[]{:S(2)}, u32[]{:S(2)}) collective-permute-start(bf16[1,24,1536]{2,1,0:T(8,128)(2,1)S(1)} %maximum_bitcast_fusion), channel_id=1, source_target_pairs={{0,6},{1,7},{2,4},{3,5},{4,2},{5,3},{6,0},{7,1},{8,14},{9,15},{10,... | collective-permute-start | bytes 221192 | tf_op jit(solution)/shard_map/ppermute | solution.py:442
  175.4 6.8 %collective-permute-start.36 = (bf16[4,1,24,640]{3,2,1,0:T(8,128)(2,1)S(1)}, bf16[4,1,24,640]{3,2,1,0:T(8,128)(2,1)S(1)}, u32[]{:S(2)}, u32[]{:S(2)}) collective-permute-start(bf16[4,1,24,640]{3,2,1,0:T(8,128)(2,1)S(1)} %get-tuple-element.92), channel_id=1, source_target_pairs={{0,6},{1,7},{2,4},{3,5},{4,2},{5,3},{6,0},{7,1},{8,14},{9,15},{10,... | collective-permute-start | bytes 368648 | tf_op jit(solution)/shard_map/ppermute | solution.py:442
  177.5 8.7 %collective-permute-start.35 = (bf16[4,1,24,640]{3,2,0,1:T(8,128)(2,1)S(1)}, bf16[4,1,24,640]{3,2,0,1:T(8,128)(2,1)S(1)}, u32[]{:S(2)}, u32[]{:S(2)}) collective-permute-start(bf16[4,1,24,640]{3,2,0,1:T(8,128)(2,1)S(1)} %get-tuple-element.93), channel_id=1, source_target_pairs={{0,4},{1,5},{2,6},{3,7},{4,0},{5,1},{6,2},{7,3},{8,12},{9,13},{10,... | collective-permute-start | bytes 368648 | tf_op jit(solution)/shard_map/ppermute | solution.py:442
  180.1 6.0 %collective-permute-start.34 = (bf16[4,1,24,640]{3,2,0,1:T(8,128)(2,1)S(1)}, bf16[4,1,24,640]{3,2,0,1:T(8,128)(2,1)S(1)}, u32[]{:S(2)}, u32[]{:S(2)}) collective-permute-start(bf16[4,1,24,640]{3,2,0,1:T(8,128)(2,1)S(1)} %get-tuple-element.91), channel_id=1, source_target_pairs={{0,2},{1,3},{2,0},{3,1},{4,6},{5,7},{6,4},{7,5},{8,10},{9,11},{10,... | collective-permute-start | bytes 368648 | tf_op jit(solution)/shard_map/ppermute | solution.py:442
  180.6 25.7 %copy-start.4 = (bf16[8,24,1536]{2,1,0:T(8,128)(2,1)}, bf16[8,24,1536]{2,1,0:T(8,128)(2,1)S(1)}, u32[]{:S(2)}) copy-start(bf16[8,24,1536]{2,1,0:T(8,128)(2,1)S(1)} %constant_dynamic-update-slice_fusion.1) | copy-start | bytes 1769476
  186.2 1.9 collective-permute-start.37
  186.3 4.0 %collective-permute-start.38 = (bf16[24,640]{1,0:T(8,128)(2,1)S(1)}, bf16[24,640]{1,0:T(8,128)(2,1)S(1)}, u32[]{:S(2)}, u32[]{:S(2)}) collective-permute-start(bf16[24,640]{1,0:T(8,128)(2,1)S(1)} %get-tuple-element.107), channel_id=1, source_target_pairs={{0,16},{8,24},{16,0},{24,8},{1,17},{9,25},{17,1},{25,9},{2,18},{10... | collective-permute-start | bytes 92168 | tf_op jit(solution)/shard_map/ppermute | solution.py:442
  187.2 3.5 %collective-permute-start.39 = (bf16[24,640]{1,0:T(8,128)(2,1)S(1)}, bf16[24,640]{1,0:T(8,128)(2,1)S(1)}, u32[]{:S(2)}, u32[]{:S(2)}) collective-permute-start(bf16[24,640]{1,0:T(8,128)(2,1)S(1)} %get-tuple-element.106), channel_id=1, source_target_pairs={{0,24},{8,16},{16,8},{24,0},{1,25},{9,17},{17,9},{25,1},{2,26},{10... | collective-permute-start | bytes 92168 | tf_op jit(solution)/shard_map/ppermute | solution.py:442
  190.7 5.8 %collective-permute-start.40 = (bf16[1,24,1792]{2,1,0:T(8,128)(2,1)S(1)}, bf16[1,24,1792]{2,1,0:T(8,128)(2,1)S(1)}, u32[]{:S(2)}, u32[]{:S(2)}) collective-permute-start(bf16[1,24,1792]{2,1,0:T(8,128)(2,1)S(1)} %bitcast.242), channel_id=1, source_target_pairs={{0,2},{1,3},{2,0},{3,1},{4,6},{5,7},{6,4},{7,5},{8,10},{9,11},{10,... | collective-permute-start | bytes 258056 | tf_op jit(solution)/shard_map/ppermute | solution.py:442
  190.8 10.3 %collective-permute-start.41 = (bf16[1,24,1792]{2,1,0:T(8,128)(2,1)S(1)}, bf16[1,24,1792]{2,1,0:T(8,128)(2,1)S(1)}, u32[]{:S(2)}, u32[]{:S(2)}) collective-permute-start(bf16[1,24,1792]{2,1,0:T(8,128)(2,1)S(1)} %bitcast.243), channel_id=1, source_target_pairs={{0,4},{1,5},{2,6},{3,7},{4,0},{5,1},{6,2},{7,3},{8,12},{9,13},{10,... | collective-permute-start | bytes 258056 | tf_op jit(solution)/shard_map/ppermute | solution.py:442
  194.1 9.5 %collective-permute-start.42 = (bf16[1,24,1792]{2,1,0:T(8,128)(2,1)S(1)}, bf16[1,24,1792]{2,1,0:T(8,128)(2,1)S(1)}, u32[]{:S(2)}, u32[]{:S(2)}) collective-permute-start(bf16[1,24,1792]{2,1,0:T(8,128)(2,1)S(1)} %bitcast.244), channel_id=1, source_target_pairs={{0,6},{1,7},{2,4},{3,5},{4,2},{5,3},{6,0},{7,1},{8,14},{9,15},{10,... | collective-permute-start | bytes 258056 | tf_op jit(solution)/shard_map/ppermute | solution.py:442
  196.6 10.2 %collective-permute-start.58 = (bf16[4,48,768]{2,1,0:T(8,128)(2,1)S(1)}, bf16[4,48,768]{2,1,0:T(8,128)(2,1)S(1)}, u32[]{:S(2)}, u32[]{:S(2)}) collective-permute-start(bf16[4,48,768]{2,1,0:T(8,128)(2,1)S(1)} %pad_maximum_fusion.2), channel_id=1, source_target_pairs={{0,1},{1,0},{2,3},{3,2},{4,5},{5,4},{6,7},{7,6},{8,9},{9,8},{10,11... | collective-permute-start | bytes 884744 | tf_op jit(solution)/shard_map/ppermute | solution.py:442
  201.1 14.2 %collective-permute-start.32 = (bf16[4,24,1536]{2,1,0:T(8,128)(2,1)S(1)}, bf16[4,24,1536]{2,1,0:T(8,128)(2,1)}, u32[]{:S(2)}, u32[]{:S(2)}) collective-permute-start(bf16[4,24,1536]{2,1,0:T(8,128)(2,1)S(1)} %pad_maximum_fusion.1), channel_id=1, source_target_pairs={{0,1},{1,0},{2,3},{3,2},{4,5},{5,4},{6,7},{7,6},{8,9},{9,8},{10,11... | collective-permute-start | bytes 884744 | tf_op jit(solution)/shard_map/ppermute | solution.py:442
  204.4 18.6 %collective-permute-start.43 = (bf16[4,24,1792]{2,1,0:T(8,128)(2,1)}, bf16[4,24,1792]{2,1,0:T(8,128)(2,1)}, u32[]{:S(2)}, u32[]{:S(2)}) collective-permute-start(bf16[4,24,1792]{2,1,0:T(8,128)(2,1)} %pad_maximum_fusion), channel_id=1, source_target_pairs={{0,1},{1,0},{2,3},{3,2},{4,5},{5,4},{6,7},{7,6},{8,9},{9,8},{10,11... | collective-permute-start | bytes 1032200 | tf_op jit(solution)/shard_map/ppermute | solution.py:442
  219.5 13.8 %collective-permute-start.21 = (bf16[256,768]{1,0:T(8,128)(2,1)}, bf16[256,768]{1,0:T(8,128)(2,1)S(1)}, u32[]{:S(2)}, u32[]{:S(2)}) collective-permute-start(bf16[256,768]{1,0:T(8,128)(2,1)} %slice_bitcast_fusion.4), channel_id=1, source_target_pairs={{0,16},{8,24},{16,0},{24,8},{1,17},{9,25},{17,1},{25,9},{2,18},{10... | collective-permute-start | bytes 1179656 | tf_op jit(solution)/shard_map/ppermute | solution.py:442
  221.7 14.8 %collective-permute-start.19 = (bf16[256,768]{1,0:T(8,128)(2,1)S(1)}, bf16[256,768]{1,0:T(8,128)(2,1)S(1)}, u32[]{:S(2)}, u32[]{:S(2)}) collective-permute-start(bf16[256,768]{1,0:T(8,128)(2,1)S(1)} %slice_bitcast_fusion.6), channel_id=1, source_target_pairs={{0,16},{8,24},{16,0},{24,8},{1,17},{9,25},{17,1},{25,9},{2,18},{10... | collective-permute-start | bytes 1179656 | tf_op jit(solution)/shard_map/ppermute | solution.py:442
  224.7 11.7 %copy-start.11 = (bf16[1,256,768]{2,1,0:T(8,128)(2,1)S(1)}, bf16[1,256,768]{2,1,0:T(8,128)(2,1)}, u32[]{:S(2)}) copy-start(bf16[1,256,768]{2,1,0:T(8,128)(2,1)} %param.13) | copy-start | bytes 1179652
  (29 other events, 99.6 us)

commit v2 on v1

v2 whole, which is shorter than its diff:
```python
import functools

import jax
import jax.numpy as jnp
from jax import lax
from jax.experimental import pallas as pl
from jax.experimental.pallas import tpu as pltpu
from jax.sharding import PartitionSpec as P

H = 24
PS = 64
N = 128
KCONV = 4
BLOCK = 256
DI = 1536
CONVCH = 1792
EPS = 1e-05
BF = jnp.bfloat16
F32 = jnp.float32
ANY = pltpu.HBM
VMEM_LIMIT = 24 * 1024 * 1024


def dot(a, b):
    return lax.dot_general(a, b, (((1,), (0,)), ((), ())), preferred_element_type=F32)


def dot_nt(a, b):
    return lax.dot_general(a, b, (((1,), (1,)), ((), ())), preferred_element_type=F32)


def dot_tn(a, b):
    return lax.dot_general(a, b, (((0,), (0,)), ((), ())), preferred_element_type=F32)


def pieces(value, count):
    out = []
    for _ in range(count):
        part = value.astype(BF)
        out.append(part)
        value = value - part.astype(F32)
    return out


def sigmoid(value):
    return 0.5 * jnp.tanh(0.5 * value) + 0.5


def iota(shape, dim):
    return lax.broadcasted_iota(jnp.int32, shape, dim)


def document_start(bounds, position):
    return functools.reduce(
        lambda start, bound: jnp.where(position >= bound, bound, start),
        bounds,
        jnp.zeros_like(position),
    )


def document_end(bounds, position):
    return functools.reduce(
        lambda end, bound: jnp.where(position < bound, bound, end),
        reversed(bounds),
        jnp.full_like(position, 1 << 30),
    )


def expand(table, pairs):
    low = iota((table.shape[0], 128), 1) < PS
    return jnp.concatenate(
        [
            jnp.where(low, table[:, 2 * p : 2 * p + 1], table[:, 2 * p + 1 : 2 * p + 2])
            for p in range(pairs)
        ],
        axis=1,
    )


def head_select(lanes):
    return (iota((lanes, 128), 0) // PS == iota((lanes, 128), 1)).astype(BF)


def head_sum(value):
    select = head_select(value.shape[1])
    return sum(dot(part, select) for part in pieces(value, 2))


def head_rows(row, lanes):
    mine = iota((lanes, 128), 0) // PS == iota((lanes, 128), 1)
    return jnp.sum(jnp.where(mine, row, 0.0), axis=1, keepdims=True)


def load_blocks(refs, dest, me, rows, sem, col=None):
    copies = []
    for k, ref in enumerate(refs):
        at = pl.ds(pl.multiple_of((me ^ k) * rows, 16), rows)
        to = dest.at[at] if col is None else dest.at[at, pl.ds(col[0], col[2])]
        ref = ref if col is None else ref.at[:, pl.ds(col[1], col[2])]
        copies.append(pltpu.make_async_copy(ref, to, sem.at[k]))
    for copy in copies:
        copy.start()
    return copies


def wait_block(ref, dest, me, b, sem):
    at = pl.ds(pl.multiple_of(b * BLOCK, BLOCK), BLOCK)
    pltpu.make_async_copy(ref, dest.at[at], sem.at[b ^ me]).wait()
    return dest[at, :]


def conv_forward(cext, taps, bounds, start):
    position = start + iota((BLOCK, 1), 0)
    depth = position - document_start(bounds, position)
    masks, pre = [], taps[KCONV : KCONV + 1, :]
    for k in range(KCONV):
        back = KCONV - 1 - k
        taken = cext[pl.ds(8 - back, BLOCK), :]
        if back:
            masks.append(jnp.where(depth >= back, 1.0, 0.0))
            taken = taken * masks[-1]
        pre = pre + taps[k : k + 1, :] * taken
    return pre, masks + [None]


def scan_terms(raw, heads, bounds, start):
    z = raw + heads[0:1, :]
    step = jnp.maximum(z, 0.0) + jnp.log1p(jnp.exp(-jnp.abs(z)))
    rate = -jnp.exp(heads[1:2, :])
    log_decay = step * rate
    tri = (iota((BLOCK, BLOCK), 0) >= iota((BLOCK, BLOCK), 1)).astype(BF)
    cum = sum(dot(tri, part) for part in pieces(log_decay, 3))
    position = start + iota((BLOCK, 1), 0)
    first = document_start(bounds, position)
    last_first = document_start(bounds, start + BLOCK - 1)
    other = start + iota((BLOCK, BLOCK), 1)
    bias = jnp.where((other <= position) & (other >= first), 0.0, -1e30)
    tail = cum[BLOCK - 1 : BLOCK, :]
    enter = jnp.where(first < start, jnp.exp(cum), 0.0)
    end = jnp.where(position >= last_first, jnp.exp(tail - cum), 0.0)
    keep = jnp.where(last_first < start, jnp.exp(tail), 0.0)
    return z, step, rate, cum, bias, enter, end, keep


def forward_kernel(n, heads, own_heads, scal, *refs):
    xs, ws, wks = refs[:n], refs[n : 2 * n], refs[2 * n : 3 * n]
    gain, taps, hp, skip = refs[3 * n : 3 * n + 4]
    normed_o, normed_t_o, conv_o, convk_o, raw_o, mixer_o, start_o = refs[3 * n + 4 : 3 * n + 11]
    xv, wv, cext, state, sem_x, sem_w, sem_k = refs[3 * n + 11 :]
    lanes = heads * PS
    width = lanes + 2 * N
    b = pl.program_id(0)
    bounds = [scal[i] for i in range(2, scal.shape[0])]
    start = b * BLOCK

    @pl.when(b == 0)
    def _():
        me = scal[0]
        load_blocks(xs, xv, me, BLOCK, sem_x)
        copies = load_blocks(ws, wv, me, ws[0].shape[0], sem_w, (0, 0, lanes))
        copies += load_blocks(wks, wv, me, ws[0].shape[0], sem_k, (lanes, 0, 2 * N + 128))
        cext[0:8, :] = jnp.zeros((8, width), F32)
        state[...] = jnp.zeros_like(state)
        for copy in copies:
            copy.wait()

    x = wait_block(xs[0], xv, scal[0], b, sem_x).astype(F32)
    scale = lax.rsqrt(jnp.mean(x * x, axis=1, keepdims=True) + EPS)
    normed = (x * scale * gain[...]).astype(BF)
    normed_o[...] = normed
    normed_t_o[...] = normed.T
    proj = dot(normed, wv[...]).astype(BF)
    conv_o[...] = proj[:, :lanes]
    convk_o[...] = proj[:, lanes:width]
    raw = pltpu.roll(proj[:, width:].astype(F32), 128 - scal[0] * own_heads, 1)
    raw_o[...] = raw
    cext[8:, :] = proj[:, :width].astype(F32)
    pre, _ = conv_forward(cext, taps, bounds, start)
    cext[0:8, :] = cext[BLOCK:, :]
    act = pre * sigmoid(pre)
    low = act.astype(BF)
    full = act[:, :lanes]
    keys, query = low[:, lanes : lanes + N], low[:, lanes + N :]
    _, step, _, cum, bias, enter, end, keep = scan_terms(raw, hp, bounds, start)
    cum_t, step_t = cum.T, step.T
    gram = dot_nt(query, keys)
    start_state = state[...]
    start_o[0] = start_state
    inter = dot_nt(query, start_state.astype(BF)) * expand(enter, heads // 2)
    weighted = (full * expand(end * step, heads // 2)).astype(BF)
    state[...] = head_rows(keep, lanes) * start_state + dot_tn(weighted, keys)
    rest = inter + skip[...] * full
    first = iota((BLOCK, 2 * PS), 1) < PS
    for p in range(heads // 2):
        at = slice(2 * PS * p, 2 * PS * (p + 1))
        pair = low[:, at]
        halves = (jnp.where(first, pair, 0), jnp.where(first, 0, pair))
        for t in range(2):
            rows, cols = slice(128 * t, 128 * (t + 1)), slice(0, 128 * (t + 1))
            total = rest[rows, at]
            for i in range(2):
                h = 2 * p + i
                decay = jnp.exp(cum[rows, h : h + 1] - cum_t[h : h + 1, cols] + bias[rows, cols])
                weights = (gram[rows, cols] * decay * step_t[h : h + 1, cols]).astype(BF)
                total = total + dot(weights, halves[i][cols, :])
            mixer_o[rows, at] = total


def gate_kernel(n, scal, *refs):
    gs, ws = refs[:n], refs[n : 2 * n]
    normed, mixer, wo, gain = refs[2 * n : 2 * n + 4]
    raw_o, gno_o, stat_o = refs[2 * n + 4 : 2 * n + 7]
    gv, wv, sem_g, sem_w = refs[2 * n + 7 :]
    b = pl.program_id(0)

    @pl.when(b == 0)
    def _():
        me = scal[0]
        load_blocks(gs, gv, me, BLOCK, sem_g)
        lanes = wv.shape[1]
        for copy in load_blocks(ws, wv, me, ws[0].shape[0], sem_w, (0, lanes, lanes)):
            copy.wait()

    raw = dot(normed[...], wv[...]).astype(BF)
    raw_o[...] = raw
    gate = raw.astype(F32)
    gated = mixer[...] * (gate * sigmoid(gate))
    g = wait_block(gs[0], gv, scal[0], b, sem_g)
    gno = dot_nt(g, wo[...])
    gno_o[...] = gno
    first = jnp.sum(gated * gated, axis=1, keepdims=True)
    second = jnp.sum(gno * gain[...] * gated, axis=1, keepdims=True)
    lane = iota((BLOCK, 128), 1)
    both = jnp.where(lane == 0, first, jnp.where(lane == 1, second, 0.0))
    stat_o[...] = both.T[0:8, :]


def output_kernel(n, nd, inner, scal, *refs):
    gs = refs[:n]
    stats = refs[n : 2 * n]
    normed_t, mixer, raw, gno, wo, gain = refs[2 * n : 2 * n + 6]
    out_o, gssm_o, ggr_o, early_o = refs[2 * n + 6 : 2 * n + 10]
    gv, acc_o, acc_g, sem_g = refs[2 * n + 10 :]
    b = pl.program_id(0)

    @pl.when(b == 0)
    def _():
        load_blocks(gs, gv, scal[0], BLOCK, sem_g)
        acc_o[...] = jnp.zeros_like(acc_o)
        acc_g[...] = jnp.zeros_like(acc_g)

    stat = functools.reduce(lambda a, c: a + c, [s[...] for s in stats])
    stat = jnp.concatenate([stat, jnp.zeros((120, BLOCK), F32)], axis=0).T
    scale = lax.rsqrt(stat[:, 0:1] * (1.0 / inner) + EPS)
    mean = stat[:, 1:2] * (1.0 / inner)
    mix = mixer[...]
    gate = raw[...].astype(F32)
    sig = sigmoid(gate)
    act = gate * sig
    gated = mix * act
    normed_out = (gated * scale * gain[...]).astype(BF)
    g = wait_block(gs[0], gv, scal[0], b, sem_g)
    out_o[0] = dot(normed_out, wo[...]).astype(BF)
    acc_o[...] += dot_tn(normed_out, g)
    grad_gated = scale * (gno[...] * gain[...] - gated * (mean * scale * scale))
    grad_raw = (grad_gated * mix * (sig * (1.0 + gate * (1.0 - sig)))).astype(BF)
    ggr_o[...] = grad_raw
    gssm_o[...] = (grad_gated * act).astype(BF)
    acc_g[...] += dot(normed_t[...], grad_raw)

    @pl.when(b == pl.num_programs(0) - 1)
    def _():
        share, lanes, model = acc_o.shape[0] // nd, acc_g.shape[1], acc_o.shape[1]
        rows = model // n
        part, side = rows // nd, max(1, model // lanes)
        for d in range(nd):
            to = d ^ scal[1] if nd > 1 else d
            early_o[to, 0:share, :] = acc_o[d * share : (d + 1) * share, :].astype(BF)
            for j in range(n):
                k = j ^ scal[0]
                first = pl.multiple_of(share + k // side * part, 8)
                value = acc_g[j * rows + d * part : j * rows + (d + 1) * part, :].astype(BF)
                for c in range(side):

                    @pl.when(k % side == c)
                    def _(c=c, value=value, first=first, to=to):
                        early_o[to, pl.ds(first, part), c * lanes : (c + 1) * lanes] = value


def store_shares(acc, out, n, nd, scal):
    rows = acc.shape[0] // n
    share = rows // nd
    for j in range(n):
        for d in range(nd):
            at = j * rows + d * share
            out[j ^ scal[0], d ^ scal[1] if nd > 1 else d] = acc[at : at + share, :].astype(BF)


def scan_kernel(n, nd, heads, own_heads, scal, *refs):
    normed_t, conv, conv_before, convk, convk_before, raw, starts, gssm, taps, hp, skip = refs[:11]
    proj_o, dw_o, small_o = refs[11:14]
    cext, gext, end_grad, acc, ggram, ght = refs[14:]
    lanes = heads * PS
    width = lanes + 2 * N
    i = pl.program_id(0)
    b = pl.num_programs(0) - 1 - i
    bounds = [scal[k] for k in range(2, scal.shape[0])]
    start = b * BLOCK
    pairs = heads // 2

    @pl.when(i == 0)
    def _():
        gext[BLOCK:, :] = jnp.zeros((8, width), F32)
        end_grad[...] = jnp.zeros_like(end_grad)
        acc[...] = jnp.zeros_like(acc)
        small_o[...] = jnp.zeros_like(small_o)

    for source, halo, at in ((conv, conv_before, slice(0, lanes)), (convk, convk_before, slice(lanes, width))):
        cext[0:8, at] = jnp.where(b > 0, halo[8:16, :].astype(F32), 0.0)
        cext[8:, at] = source[...].astype(F32)
    pre, masks = conv_forward(cext, taps, bounds, start)
    sig = sigmoid(pre)
    act = pre * sig
    low = act.astype(BF)
    full = act[:, :lanes]
    keys, query = low[:, lanes : lanes + N], low[:, lanes + N :]
    z, step, rate, cum, bias, enter, end, keep = scan_terms(raw[...], hp, bounds, start)
    cum_t, step_t, enter_t = cum.T, step.T, enter.T
    gram = dot_nt(query, keys)
    grad = gssm[...]
    grad_f = grad.astype(F32)
    grad_t = grad_f.T.astype(BF)
    first = iota((BLOCK, 2 * PS), 1) < PS
    lane = iota((128, 128), 1)
    row_totals = [jnp.zeros((128, 128), F32), jnp.zeros((128, 128), F32)]
    col_totals = []
    ggram[...] = jnp.zeros_like(ggram)
    for p in range(pairs):
        at = slice(2 * PS * p, 2 * PS * (p + 1))
        pair = low[:, at]
        halves = (jnp.where(first, pair, 0), jnp.where(first, 0, pair))
        for k in range(2):
            h = 2 * p + k
            own = slice(PS * h, PS * (h + 1))
            cols_total = None
            for t in range(2):
                rows, cols = slice(128 * t, 128 * (t + 1)), slice(0, 128 * (t + 1))
                decay = jnp.exp(cum[rows, h : h + 1] - cum_t[h : h + 1, cols] + bias[rows, cols])
                table = dot_nt(grad[rows, at], halves[k][cols, :])
                gram_here = gram[rows, cols]
                step_row = step_t[h : h + 1, cols]
                weights = (gram_here * decay * step_row).astype(BF)
                common = table * decay
                stepped = common * step_row
                ggram[rows, cols] += stepped
                col = jnp.sum(common * gram_here, axis=0, keepdims=True)
                total = jnp.sum(stepped * gram_here, axis=1, keepdims=True)
                row_totals[t] = jnp.where(lane == h, total, row_totals[t])
                part = dot(grad_t[own, rows], weights)
                if t == 0:
                    ght[own, 0:128] = part
                    cols_total = col
                else:
                    ght[own, 0:128] += part[:, 0:128]
                    ght[own, 128:256] = part[:, 128:256]
                    cols_total = col + jnp.concatenate(
                        [cols_total, jnp.zeros((1, 128), F32)], axis=1
                    )
            col_totals.append(cols_total)
    col_totals.append(jnp.zeros((128 - heads, BLOCK), F32))
    grad_step = jnp.concatenate(col_totals, axis=0).T
    grad_cum = jnp.concatenate(row_totals, axis=0) - step * grad_step
    gg = ggram[...].astype(BF)
    start_state = starts[0]
    start_low = start_state.astype(BF)
    grad_cum += head_sum(grad_f * dot_nt(query, start_low)) * enter
    entered = (grad_f * expand(enter, pairs)).astype(BF)
    grad_query = dot(gg, keys) + dot(entered, start_low)
    later = end_grad[...]
    end_low = later.astype(BF)
    scaled = end * step
    scaled_wide = expand(scaled, pairs)
    weighted = (full * scaled_wide).astype(BF)
    grad_weighted = dot_nt(keys, end_low)
    grad_keys = dot_tn(gg, query) + dot(weighted, end_low)
    grad_end = head_sum(grad_weighted * full)
    grad_step += grad_end * end
    end_terms = grad_end * scaled
    ones = jnp.ones((8, N), BF)
    held = sum(dot_nt(ones, part) for part in pieces(later * start_state, 2))
    grad_tail = jnp.sum(end_terms, axis=0, keepdims=True) + head_sum(held)[0:1, :] * keep
    final = iota((BLOCK, 1), 0) == BLOCK - 1
    grad_cum = grad_cum - end_terms + jnp.where(final, grad_tail, 0.0)
    upper = (iota((BLOCK, BLOCK), 0) <= iota((BLOCK, BLOCK), 1)).astype(BF)
    grad_log = sum(dot(upper, part) for part in pieces(grad_cum, 3))
    grad_step += grad_log * rate
    grad_rate = jnp.sum(grad_log * step, axis=0, keepdims=True)
    grad_heads = ght[...].T + grad_weighted * scaled_wide + grad_f * skip[...]
    grad_skip = jnp.sum(grad_f * full, axis=0, keepdims=True)
    grad_act = jnp.concatenate([grad_heads, grad_keys, grad_query], axis=1)
    grad_pre = grad_act * (sig * (1.0 + pre * (1.0 - sig)))
    conv_low = conv_backward(grad_pre, gext, cext, masks, taps, bounds, start, small_o).astype(BF)
    grad_raw = grad_step * sigmoid(z)
    small_o[0:1, width : width + 128] += jnp.sum(grad_raw, axis=0, keepdims=True)
    small_o[1:2, width : width + 128] += grad_rate * rate
    small_o[2:3, width : width + 128] += head_sum(jnp.broadcast_to(grad_skip, (8, lanes)))[0:1, :]
    here = normed_t[...]
    raw_low = grad_raw.astype(BF)
    small_o[:, width + 128 :] += dot_nt(raw_low.T[0:16, :], here)[0:8, :]
    acc[...] += dot(here, conv_low)
    proj_o[:, :width] = conv_low
    proj_o[:, width:] = pltpu.roll(grad_raw, scal[0] * own_heads, 1).astype(BF)
    geared = jnp.concatenate(
        [grad_t[PS * h : PS * (h + 1), :].astype(F32) * enter_t[h : h + 1, :] for h in range(heads)],
        axis=0,
    ).astype(BF)
    end_grad[...] = head_rows(keep, lanes) * later + dot(geared, query)

    @pl.when(i == pl.num_programs(0) - 1)
    def _():
        store_shares(acc, dw_o, n, nd, scal)


def conv_backward(grad_pre, gext, cext, masks, taps, bounds, start, small_o):
    count = grad_pre.shape[1]
    gext[0:BLOCK, :] = grad_pre
    position = start + iota((BLOCK, 1), 0)
    left = document_end(bounds, position) - position
    total = None
    for k in range(KCONV):
        back = KCONV - 1 - k
        taken = cext[pl.ds(8 - back, BLOCK), :]
        after = gext[pl.ds(back, BLOCK), :]
        if back:
            taken = taken * masks[k]
            after = after * jnp.where(left > back, 1.0, 0.0)
        small_o[k : k + 1, 0:count] += jnp.sum(grad_pre * taken, axis=0, keepdims=True)
        term = taps[k : k + 1, :] * after
        total = term if total is None else total + term
    small_o[4:5, 0:count] += jnp.sum(grad_pre, axis=0, keepdims=True)
    gext[BLOCK:, :] = gext[0:8, :]
    return total


def normed_kernel(n, lanes, scal, *refs):
    ws, wks = refs[:n], refs[n : 2 * n]
    proj, ggr, gn_o, wv, wgv, sem_w, sem_k, sem_g = refs[2 * n :]

    @pl.when(pl.program_id(0) == 0)
    def _():
        rows = ws[0].shape[0]
        copies = load_blocks(ws, wv, scal[0], rows, sem_w, (0, 0, lanes))
        copies += load_blocks(wks, wv, scal[0], rows, sem_k, (lanes, 0, 2 * N + 128))
        copies += load_blocks(ws, wgv, scal[0], rows, sem_g, (0, lanes, lanes))
        for copy in copies:
            copy.wait()

    gn_o[0] = (dot_nt(proj[...], wv[...]) + dot_nt(ggr[...], wgv[...])).astype(BF)


def rows_dot(value, weight):
    product = value * weight.astype(F32)
    ones = jnp.ones((8, product.shape[1]), BF)
    return sum(dot_nt(ones, part) for part in pieces(product, 2))


def weights_kernel(n, own, order, scal, *refs):
    late, step, weight, gain, out, gain_o = refs
    rows, lanes = late.shape[1], (late.shape[2] - 2 * N) // (2 * n)
    me = scal[0]
    at = [
        0 if len(order) == 1 else pl.multiple_of((place ^ scal[1]) * rows, 8) for place in order
    ]

    def put(first):
        for e in range(len(order)):
            for k in range(n):
                for c in range(2):
                    from_lane = (2 * k + c) * lanes
                    value = late[e, :, from_lane : from_lane + own].astype(F32)
                    out[pl.ds(at[e], rows), pl.ds(c * DI + first(k), own)] = value

    if own % 128 == 0:
        put(lambda k: pl.multiple_of((me ^ k) * own, 128))
    else:
        for q in range(n):
            pl.when(me == q)(functools.partial(put, lambda k, q=q: (q ^ k) * own))
    for e in range(len(order)):
        out[pl.ds(at[e], rows), 2 * DI : 2 * DI + 2 * N] = late[e, :, late.shape[2] - 2 * N :].astype(F32)
    out[:, 2 * DI + 2 * N :] = step[:, :H]
    gain_o[...] = rows_dot(out[...], weight[...]) / gain[...]


def small_kernel(n, own_heads, scal, *refs):
    parts, (conv_o, step_o, heads_o), wide = refs[:n], refs[n : n + 3], refs[n + 3]
    own, rows = own_heads * PS, step_o.shape[0]
    lanes = own + own % 128
    width, chans = lanes + 2 * N, conv_o.shape[1]
    me = scal[0]
    for q in range(n):

        @pl.when(me == q)
        def _(q=q):
            shared, steps = jnp.zeros((8, 2 * N), F32), []
            for j in range(n):
                part = parts[q ^ j]
                wide[:, j * own : (j + 1) * own] = part[:, 0:own]
                shared = shared + part[:, lanes:width]
                first = width + 128 + q * rows
                steps.append(part[0:own_heads, first : first + rows])
            wide[:, DI:] = shared
            conv_o[...] = wide[:, q * chans : (q + 1) * chans]
            steps.append(jnp.zeros((128 - n * own_heads, rows), F32))
            step_o[...] = jnp.concatenate(steps, axis=0).T

    heads_o[...] = parts[0][:, width : width + 128]


def out_weight_kernel(order, scal, share, weight, gain, out, gain_o):
    rows = share.shape[1]
    for e, place in enumerate(order):
        at = 0 if len(order) == 1 else pl.multiple_of((place ^ scal[1]) * rows, 8)
        out[pl.ds(at, rows), :] = share[e].astype(F32)
    gain_o[...] = rows_dot(out[...], weight[...]) / gain[...]


def packets_kernel(n, own, scal, weight, *outs):
    for k in range(n):
        first = pl.multiple_of((scal[0] ^ k) * own, 128)
        outs[k][:, 0:own] = weight[:, pl.ds(DI + first, own)]
        outs[k][:, own:] = weight[:, pl.ds(first, own)]
    shared = outs[n]
    shared[:, 0 : 2 * N] = weight[:, 2 * DI : 2 * DI + 2 * N]
    shared[:, 2 * N :] = jnp.zeros((shared.shape[0], 128), BF)
    shared[:, 2 * N : 2 * N + H] = weight[:, 2 * DI + 2 * N :]


def xor(value, axis, k):
    return lax.ppermute(value, axis, [(s, s ^ k) for s in range(lax.axis_size(axis))])


def gather_xor(value, axis):
    out = [value]
    for k in range(1, lax.axis_size(axis)):
        out.append(xor(value, axis, k) if k % 2 == 0 or k == 1 else xor(out[k - 1], axis, 1))
    return out


def by_owner(parts, me):
    stacked = jnp.stack(parts)
    return [lax.dynamic_index_in_dim(stacked, me ^ j, 0, False) for j in range(len(parts))]


def stages(count):
    out, low = [], 0
    bits = count.bit_length() - 1
    while low < bits:
        take = 1 if low == 0 else min(2, bits - low)
        out.append((low, take))
        low += take
    return out


def gather_order(count):
    order = [0]
    for low, take in reversed(stages(count)):
        order = [o | (m << low) for m in range(1 << take) for o in order]
    return order


class Shares:
    def __init__(self, value, dim):
        self.value, self.dim = value, dim
        self.low = [low for low, _ in stages(value.shape[dim])]
        self.bits = dict(stages(value.shape[dim]))
        sizes = [1 << self.bits[low] for low in reversed(self.low)]
        self.value = value.reshape(value.shape[:dim] + tuple(sizes) + value.shape[dim + 1 :])
        self.left = list(reversed(self.low))

    def reduce(self, low):
        at = self.dim + self.left.index(low)
        take = lambda m: lax.index_in_dim(self.value, m, at, False)
        recv = [xor(take(m), "dp", m << low) for m in range(1, 1 << self.bits[low])]
        total = take(0).astype(F32)
        for part in recv:
            total = total + part.astype(F32)
        self.value = total.astype(BF)
        self.left.remove(low)


def gather_step(value, low, take):
    return jnp.concatenate([value] + [xor(value, "dp", m << low) for m in range(1, 1 << take)], 0)


def pair_step(value, hop):
    return jnp.concatenate([value, xor(value, "dp", hop)], 0)


def pair_order(count):
    order = [0]
    bits = [1 << bit for bit in range(count.bit_length() - 1)]
    for hop in bits[1:][::-1] + bits[:1]:
        order += [place | hop for place in order]
    return order


def tie(*values):
    return lax.optimization_barrier(values)


def call(
    kernel, name, grid, scal, in_specs, args, out_specs, out_shape, scratch, flops, bytes_, aliases={}
):
    return pl.pallas_call(
        kernel,
        grid_spec=pltpu.PrefetchScalarGridSpec(
            num_scalar_prefetch=1,
            grid=grid,
            in_specs=in_specs,
            out_specs=out_specs,
            scratch_shapes=scratch,
        ),
        out_shape=out_shape,
        name=name,
        input_output_aliases=aliases,
        compiler_params=pltpu.CompilerParams(vmem_limit_bytes=VMEM_LIMIT),
        cost_estimate=pl.CostEstimate(flops=flops, bytes_accessed=bytes_, transcendentals=0),
    )(scal, *args)


def local(
    block_input,
    out_cotangent,
    doc_lengths,
    norm_gain,
    in_weight,
    conv_weight,
    conv_bias,
    step_bias,
    decay_log,
    skip_gain,
    out_gain,
    out_weight,
):
    n, ndp = lax.axis_size("fsdp"), lax.axis_size("dp")
    me, dpi = lax.axis_index("fsdp"), lax.axis_index("dp")
    _, toks, model = block_input.shape
    length = toks * n
    nb = length // BLOCK
    own_heads = H // n
    heads = own_heads + own_heads % 2
    own, lanes = own_heads * PS, heads * PS
    width = lanes + 2 * N
    rows = model // n
    share = rows // ndp
    nd = ndp if share % 8 == 0 else 1
    x_own, g_own = block_input[0], out_cotangent[0]
    bounds = jnp.cumsum(doc_lengths[0])[:-1].astype(jnp.int32)
    scal = jnp.concatenate([jnp.stack([me, dpi]).astype(jnp.int32), bounds])

    def exchange(mine):
        return [mine[0]] + [xor(mine[k], "fsdp", k) for k in range(1, n)]

    xs = gather_xor(x_own, "fsdp")
    if own % 128 == 0:
        packets = call(
            functools.partial(packets_kernel, n, own),
            "packets",
            (1,),
            scal,
            [pl.BlockSpec(in_weight.shape, lambda b, s: (0, 0))],
            (in_weight,),
            [pl.BlockSpec((rows, 2 * own), lambda b, s: (0, 0))] * n
            + [pl.BlockSpec((rows, 2 * N + 128), lambda b, s: (0, 0))],
            [jax.ShapeDtypeStruct((rows, 2 * own), BF)] * n
            + [jax.ShapeDtypeStruct((rows, 2 * N + 128), BF)],
            [],
            10**6,
            3 * 10**6,
        )
        own_cols, shared = list(packets[:n]), packets[-1]
    else:

        def columns(first):
            part = in_weight[:, first : first + DI].reshape(rows, n, own).transpose(1, 0, 2)
            part = jnp.pad(part, ((0, 0), (0, 0), (0, lanes - own)))
            return [lax.dynamic_index_in_dim(part, me ^ k, 0, False) for k in range(n)]

        own_cols = [jnp.concatenate(both, axis=1) for both in zip(columns(DI), columns(0))]
        shared = jnp.pad(in_weight[:, 2 * DI :], ((0, 0), (0, 128 - H)))
    small = jnp.concatenate([norm_gain, conv_bias, conv_weight.reshape(-1)])
    small = jnp.pad(small, (0, -small.shape[0] % 1024)).reshape(-1, 128)
    shared, small = tie(shared, small)
    smalls = by_owner([small] + [xor(small, "fsdp", k) for k in range(1, n)], me)
    flat = jnp.stack(smalls).reshape(n, -1)
    chans = CONVCH // n
    gain_full = flat[:, :rows].reshape(1, model).astype(F32)
    conv_full = jnp.concatenate(
        [
            flat[:, rows + chans : rows + chans * (1 + KCONV)]
            .reshape(n, KCONV, chans)
            .transpose(1, 0, 2)
            .reshape(KCONV, CONVCH),
            flat[:, rows : rows + chans].reshape(1, CONVCH),
        ],
        axis=0,
    ).astype(F32)
    conv_heads = lax.dynamic_slice_in_dim(conv_full, me * own, own, 1)
    taps = jnp.concatenate(
        [jnp.pad(conv_heads, ((0, 0), (0, lanes - own))), conv_full[:, DI:]], axis=1
    )
    taps = jnp.pad(taps, ((0, 3), (0, 0)))
    hp = jnp.stack([step_bias, decay_log]).astype(F32)
    hp = jnp.pad(hp, ((0, 6), (0, 128 - own_heads)))
    skip = jnp.pad(jnp.repeat(skip_gain.astype(F32), PS), (0, lanes - own)).reshape(1, lanes)

    xs[2], *own_cols = tie(xs[2], *own_cols)
    xs[3] = xor(xs[2], "fsdp", 1)
    wks = gather_xor(shared, "fsdp")
    ws = exchange(own_cols)
    g_tied, *_ = tie(g_own, *ws[1:])
    gs = gather_xor(g_tied, "fsdp")

    any_spec = pl.BlockSpec(memory_space=ANY)

    def whole(*shape):
        return pl.BlockSpec(shape, lambda b, s: (0,) * len(shape))

    def tokens(cols):
        return pl.BlockSpec((BLOCK, cols), lambda b, s: (b, 0))

    shape = jax.ShapeDtypeStruct
    normed, normed_t, conv_in, convk_in, raw_step, mixer, starts = call(
        functools.partial(forward_kernel, n, heads, own_heads),
        "forward",
        (nb,),
        scal,
        [any_spec] * (3 * n) + [whole(1, model), whole(8, width), whole(8, 128), whole(1, lanes)],
        (*xs, *ws, *wks, gain_full, taps, hp, skip),
        [
            tokens(model),
            pl.BlockSpec((model, BLOCK), lambda b, s: (0, b)),
            tokens(lanes),
            tokens(2 * N),
            tokens(128),
            tokens(lanes),
            pl.BlockSpec((1, lanes, N), lambda b, s: (b, 0, 0)),
        ],
        [
            shape((length, model), BF),
            shape((model, length), BF),
            shape((length, lanes), BF),
            shape((length, 2 * N), BF),
            shape((length, 128), F32),
            shape((length, lanes), F32),
            shape((nb, lanes, N), F32),
        ],
        [
            pltpu.VMEM((length, model), BF),
            pltpu.VMEM((model, width + 128), BF),
            pltpu.VMEM((8 + BLOCK, width), F32),
            pltpu.VMEM((lanes, N), F32),
            pltpu.SemaphoreType.DMA((n,)),
            pltpu.SemaphoreType.DMA((n,)),
            pltpu.SemaphoreType.DMA((n,)),
        ],
        9 * 10**9,
        10**7,
    )

    gs[2], normed = tie(gs[2], normed)
    gs[3::2] = [xor(value, "fsdp", 1) for value in gs[2::2]]
    out_w = jnp.pad(out_weight, ((0, lanes - own), (0, 0)))
    out_g = jnp.pad(out_gain.astype(F32), (0, lanes - own)).reshape(1, lanes)
    raw_gate, gno, stat = call(
        functools.partial(gate_kernel, n),
        "gate",
        (nb,),
        scal,
        [any_spec] * (2 * n)
        + [tokens(model), tokens(lanes), whole(lanes, model), whole(1, lanes)],
        (*gs, *ws, normed, mixer, out_w, out_g),
        [tokens(lanes), tokens(lanes), pl.BlockSpec((8, BLOCK), lambda b, s: (0, b))],
        [
            shape((length, lanes), BF),
            shape((length, lanes), F32),
            shape((8, length), F32),
        ],
        [
            pltpu.VMEM((length, model), BF),
            pltpu.VMEM((model, lanes), BF),
            pltpu.SemaphoreType.DMA((n,)),
            pltpu.SemaphoreType.DMA((n,)),
        ],
        2 * 10**9,
        10**7,
    )
    side = max(1, model // lanes)
    early_count = lanes // nd + -(-n // side) * (rows // nd)
    stats = [stat] + [xor(stat, "fsdp", k) for k in range(1, n)]

    out_part, gssm, ggr, early = call(
        functools.partial(output_kernel, n, nd, DI),
        "output",
        (nb,),
        scal,
        [any_spec] * n
        + [pl.BlockSpec((8, BLOCK), lambda b, s: (0, b))] * n
        + [pl.BlockSpec((model, BLOCK), lambda b, s: (0, b))]
        + [tokens(lanes), tokens(lanes), tokens(lanes)]
        + [whole(lanes, model), whole(1, lanes)],
        (*gs, *stats, normed_t, mixer, raw_gate, gno, out_w, out_g),
        [
            pl.BlockSpec((1, BLOCK, model), lambda b, s: (b ^ s[0], 0, 0)),
            tokens(lanes),
            tokens(lanes),
            whole(nd, early_count, model),
        ],
        [
            shape((nb, BLOCK, model), BF),
            shape((length, lanes), BF),
            shape((length, lanes), BF),
            shape((nd, early_count, model), BF),
        ],
        [
            pltpu.VMEM((length, model), BF),
            pltpu.VMEM((lanes, model), F32),
            pltpu.VMEM((model, lanes), F32),
            pltpu.SemaphoreType.DMA((n,)),
        ],
        3 * 10**9,
        10**7,
    )

    def core_sum(parts):
        paired = parts.reshape(n // 2, 2, BLOCK, model)
        other = xor(paired[:, 1], "fsdp", 1)
        return (paired[:, 0].astype(F32) + other.astype(F32)).astype(BF)

    def chip_exchange(both):
        return both[0], [xor(both[k // 2], "fsdp", k) for k in range(2, n, 2)]

    def total_of(mine, recv):
        return functools.reduce(lambda a, c: a + c.astype(F32), recv, mine.astype(F32))

    def to_owners(shares):
        return [shares[0]] + [xor(shares[k], "fsdp", k) for k in range(1, n)]

    def late_rows(parts):
        shared_sum = functools.reduce(
            lambda a, c: a + c, [part[:, 2 * lanes :].astype(F32) for part in parts]
        )
        return jnp.concatenate(
            [part[:, : 2 * lanes] for part in parts] + [shared_sum.astype(BF)], axis=1
        )

    order = gather_order(ndp) if nd > 1 else [0]
    back = lambda b: nb - 1 - b

    def tokens_back(cols, at=0):
        return pl.BlockSpec((BLOCK, cols), lambda b, s: (back(b), at))

    def halo_back(cols, at=0):
        return pl.BlockSpec(
            (16, cols), lambda b, s: (jnp.maximum(back(b) * (BLOCK // 16) - 1, 0), at)
        )

    normed_back = pl.BlockSpec((model, BLOCK), lambda b, s: (0, back(b)))

    if nd > 1:
        early = Shares(early, 0)
        early.reduce(0)
    out_sum = core_sum(out_part)

    proj_low, dw, small_grads = call(
        functools.partial(scan_kernel, n, nd, heads, own_heads),
        "scan_back",
        (nb,),
        scal,
        [
            normed_back,
            tokens_back(lanes),
            halo_back(lanes),
            tokens_back(2 * N),
            halo_back(2 * N),
            tokens_back(128),
            pl.BlockSpec((1, lanes, N), lambda b, s: (back(b), 0, 0)),
            tokens_back(lanes),
            whole(8, width),
            whole(8, 128),
            whole(1, lanes),
        ],
        (
            normed_t,
            conv_in,
            conv_in,
            convk_in,
            convk_in,
            raw_step,
            starts,
            gssm,
            taps,
            hp,
            skip,
        ),
        [
            tokens_back(width + 128),
            whole(n, nd, rows // nd, width),
            whole(8, width + 128 + model),
        ],
        [
            shape((length, width + 128), BF),
            shape((n, nd, rows // nd, width), BF),
            shape((8, width + 128 + model), F32),
        ],
        [
            pltpu.VMEM((8 + BLOCK, width), F32),
            pltpu.VMEM((BLOCK + 8, width), F32),
            pltpu.VMEM((lanes, N), F32),
            pltpu.VMEM((model, width), F32),
            pltpu.VMEM((BLOCK, BLOCK), F32),
            pltpu.VMEM((lanes, BLOCK), F32),
        ],
        20 * 10**9,
        10**7,
    )
    if nd > 1:
        proj_low, dw, small_grads, early.value, out_sum = tie(
            proj_low, dw, small_grads, early.value, out_sum
        )
        late = Shares(dw, 1)
        late.reduce(0)
        for low in early.low[1:]:
            early.reduce(low)
        bits = [1 << bit for bit in range(ndp.bit_length() - 1)]
        small_grads = small_grads + xor(small_grads, "dp", bits[0])
    (gn_part,) = call(
        functools.partial(normed_kernel, n, lanes),
        "normed_grad",
        (nb,),
        scal,
        [any_spec] * (2 * n) + [tokens(width + 128), tokens(lanes)],
        (*ws, *wks, proj_low, ggr),
        [pl.BlockSpec((1, BLOCK, model), lambda b, s: (b ^ s[0], 0, 0))],
        [shape((nb, BLOCK, model), BF)],
        [
            pltpu.VMEM((model, width + 128), BF),
            pltpu.VMEM((model, lanes), BF),
            pltpu.SemaphoreType.DMA((n,)),
            pltpu.SemaphoreType.DMA((n,)),
            pltpu.SemaphoreType.DMA((n,)),
        ],
        5 * 10**9,
        10**7,
    )
    if nd > 1:
        gn_part, late.value, early.value, small_grads = tie(
            gn_part, late.value, early.value, small_grads
        )
        own_rows, part = lanes // nd, rows // nd
        wo, gates = early.value[:own_rows], early.value[own_rows:]
        for low in late.low[1:]:
            late.reduce(low)
        gn_mine, gn_recv = chip_exchange(core_sum(gn_part))
        late.value, wo, small_grads, *gn_recv = tie(late.value, wo, small_grads, *gn_recv)
        owned = to_owners(
            [
                jnp.concatenate(
                    [
                        gates[k // side * part : (k // side + 1) * part, k % side * lanes :][:, :lanes],
                        late.value[k],
                    ],
                    axis=1,
                )
                for k in range(n)
            ]
        )
        wo = wo[None]
        for hop in bits[1:][::-1]:
            wo = pair_step(wo, hop)
            small_grads = small_grads + xor(small_grads, "dp", hop)
        late = late_rows(owned)
        late, wo, small_grads = tie(late, wo, small_grads)
        gather = list(reversed(stages(ndp)))
        late = gather_step(late[None], *gather[0])
        wo = pair_step(wo, bits[0])
        small_other = xor(small_grads, "fsdp", 1)
        late, wo, small_other, out_sum = tie(late, wo, small_other, out_sum)
        for low, take in gather[1:]:
            late = gather_step(late, low, take)
        small_parts = [small_grads, small_other]
        for k in range(2, n, 2):
            pair = xor(jnp.concatenate([small_grads, small_other], axis=1), "fsdp", k)
            small_parts += [pair[:, : small_grads.shape[1]], pair[:, small_grads.shape[1] :]]
        out_mine, out_recv = chip_exchange(out_sum)
    else:
        out_mine, out_recv = chip_exchange(out_sum)
        gn_mine, gn_recv = chip_exchange(core_sum(gn_part))
        gates = [
            early[0, lanes + k // side * rows : lanes + (k // side + 1) * rows, k % side * lanes :][
                :, :lanes
            ]
            for k in range(n)
        ]
        owned = [jnp.concatenate([gates[k], dw[k, 0]], axis=1) for k in range(n)]
        late = lax.psum(late_rows(to_owners(owned)), "dp")[None]
        wo = lax.psum(early[0, :lanes], "dp")[None]
        small_parts = to_owners([lax.psum(small_grads, "dp")] * n)
    block_output = (x_own.astype(F32) + total_of(out_mine, out_recv)).astype(BF)[None]
    total_in = total_of(gn_mine, gn_recv)
    inputs = x_own.astype(F32)
    scale_in = lax.rsqrt(jnp.mean(inputs * inputs, axis=-1, keepdims=True) + EPS)
    gained = total_in * gain_full
    input_grad = scale_in * (
        gained - inputs * jnp.mean(gained * inputs, axis=-1, keepdims=True) * scale_in * scale_in
    ) + g_own.astype(F32)
    input_grad = input_grad.astype(BF)[None]

    conv_grads, step_cols, head_grads = call(
        functools.partial(small_kernel, n, own_heads),
        "small_grads",
        (1,),
        scal,
        [whole(*part.shape) for part in small_parts],
        small_parts,
        [whole(8, chans), whole(rows, 128), whole(8, 128)],
        [shape((8, chans), F32), shape((rows, 128), F32), shape((8, 128), F32)],
        [pltpu.VMEM((8, CONVCH), F32)],
        10**6,
        10**6,
    )
    head_grads = head_grads[:3, :own_heads]

    grad_in, grad_gain = call(
        functools.partial(weights_kernel, n, own, order),
        "in_weight_grad",
        (1,),
        scal,
        [
            whole(*late.shape),
            whole(rows, 128),
            whole(*in_weight.shape),
            whole(1, rows),
        ],
        (late, step_cols, in_weight, norm_gain.astype(F32).reshape(1, rows)),
        [whole(*in_weight.shape), whole(8, rows)],
        [shape(in_weight.shape, F32), shape((8, rows), F32)],
        [],
        10**8,
        6 * 10**6,
    )
    gain_ones = jnp.pad(out_gain.astype(F32), (0, lanes - own), constant_values=1.0)
    grad_out, grad_out_gain = call(
        functools.partial(out_weight_kernel, pair_order(ndp) if nd > 1 else [0]),
        "out_weight_grad",
        (1,),
        scal,
        [whole(*wo.shape), whole(lanes, model), whole(1, lanes)],
        (wo, out_w, gain_ones.reshape(1, lanes)),
        [whole(lanes, model), whole(8, lanes)],
        [shape((lanes, model), F32), shape((8, lanes), F32)],
        [],
        10**8,
        3 * 10**6,
    )
    return (
        block_output,
        input_grad,
        grad_gain[0],
        grad_in,
        conv_grads[:KCONV],
        conv_grads[KCONV],
        head_grads[0],
        head_grads[1],
        head_grads[2],
        grad_out_gain[0, :own],
        grad_out[:own],
    )


def solution(mesh):
    return jax.shard_map(
        local,
        mesh=mesh,
        in_specs=(
            P("dp", "fsdp", None),
            P("dp", "fsdp", None),
            P("dp", None),
            P("fsdp"),
            P("fsdp", None),
            P(None, "fsdp"),
            P("fsdp"),
            P("fsdp"),
            P("fsdp"),
            P("fsdp"),
            P("fsdp"),
            P("fsdp", None),
        ),
        out_specs=(
            P("dp", "fsdp", None),
            P("dp", "fsdp", None),
            P("fsdp"),
            P("fsdp", None),
            P(None, "fsdp"),
            P("fsdp"),
            P("fsdp"),
            P("fsdp"),
            P("fsdp"),
            P("fsdp"),
            P("fsdp", None),
        ),
        check_vma=False,
    )
```

time: 239 us -> 182 us (0.76)
  starting transfers between devices: 60.9 us -> 42.6 us
  Pallas kernels: 72 us -> 55.6 us
  local copies, waits for them, and re-layouts: 30.1 us -> 16 us
  other arithmetic: 12.9 us -> 7.1 us
    ppermute x59 -> x45, starting transfers between devices: 60.9 us -> 42.6 us  [xor(): lax.ppermute(value, axis, [(s, s ^ k) for s in range(lax.axis_size(axis))])]
    pallas_call x6 -> x9, Pallas kernels: 72 us -> 55.6 us  [call(): pl.pallas_call(kernel, grid_spec=pltpu.PrefetchScalarGridSpec(num_scalar_...]
    squeeze x12 -> x8, local copies, waits for them, and re-layouts: 5.62 us -> 1.15 us  [the longest x2 0.98 us: core_sum(): other = xor(paired[:, 1], 'fsdp', 1)]
    pallas_call x2 -> x0, other arithmetic: 3.22 us -> none  [call(): pl.pallas_call(kernel, grid_spec=pltpu.PrefetchScalarGridSpec(num_scalar_...]
    unnamed x91 -> x45, local copies, waits for them, and re-layouts: 10.5 us -> 7.4 us
    concatenate x3 -> x0, local copies, waits for them, and re-layouts: 2.74 us -> none  [gather_dp(): jnp.concatenate([out] + [xor(out, 'dp', m << low) for m in range(1, 1 <<...]
    ppermute x59 -> x45, waiting for transfers between devices: 60.4 us -> 58.8 us  [xor(): lax.ppermute(value, axis, [(s, s ^ k) for s in range(lax.axis_size(axis))])]
  transfers between devices with their start and end apart: 59 -> 45, of which waited for: 28 -> 18; matrix products, arithmetic and copies ran while one was open for 15% -> 7% of each run, Pallas kernels for 12% -> 22%
where the time goes in v2:
time: 182 us; the launch traced here: 181 us
  waiting for transfers between devices  58.8 us (32%)
  Pallas kernels  55.6 us (31%)
  starting transfers between devices  42.6 us (23%)
  local copies, waits for them, and re-layouts  16 us (9%)
  other arithmetic  7.1 us (4%)
    ppermute x45, waiting for transfers between devices, xor(): lax.ppermute(value, axis, [(s, s ^ k) for s in range(lax.axis_size(axis))])  58.8 us
    pallas_call x9, Pallas kernels, call(): pl.pallas_call(kernel, grid_spec=pltpu.PrefetchScalarGridSpec(num_scalar_...  55.6 us
    ppermute x45, starting transfers between devices, xor(): lax.ppermute(value, axis, [(s, s ^ k) for s in range(lax.axis_size(axis))])  42.6 us
    unnamed x45, local copies, waits for them, and re-layouts  7.4 us
  transfers between devices with their start and end apart: 45, of which 18 were waited for; matrix products, arithmetic and copies ran while one was open for 7% of the time, Pallas kernels for 22%

profile of v2, /device:TPU:0, one launch (start us, length us, event | category | flops | bytes accessed | tf_op | source)
XLA Modules:
  0.0 181.3 jit_solution(14356933339340598077)
XLA Ops:
  0.6 3.0 %collective-permute-start = (bf16[256,768]{1,0:T(8,128)(2,1)}, bf16[256,768]{1,0:T(8,128)(2,1)S(1)}, u32[]{:S(2)}, u32[]{:S(2)}) collective-permute-start(bf16[256,768]{1,0:T(8,128)(2,1)} %bitcast.132), channel_id=1, source_target_pairs={{0,16},{8,24},{16,0},{24,8},{1,17},{9,25},{17,1},{25,9},{2,18},{10... | collective-permute-start | bytes 1179656 | tf_op jit(solution)/shard_map/ppermute | solution.py:539
  3.6 0.8 reduce-window.4
  4.5 0.8 reshape.121
  5.3 1.4 concatenate.47
  6.8 1.3 copy-done
  8.1 1.5 packets.1
  9.8 1.9 %collective-permute-start.10 = (bf16[24,128]{1,0:T(8,128)(2,1)S(1)}, bf16[24,128]{1,0:T(8,128)(2,1)S(1)}, u32[]{:S(2)}, u32[]{:S(2)}) collective-permute-start(bf16[24,128]{1,0:T(8,128)(2,1)S(1)} %pad_bitcast_fusion), channel_id=1, source_target_pairs={{0,16},{8,24},{16,0},{24,8},{1,17},{9,25},{17,1},{25,9},{2,18},{10... | collective-permute-start | bytes 18440 | tf_op jit(solution)/shard_map/ppermute | solution.py:539
  12.5 0.7 broadcast_in_dim.17
  14.2 1.1 collective-permute-start.1
  15.2 0.9 collective-permute-start.2
  16.7 3.3 %collective-permute-done.5.refs_10_.refs_6_ = bf16[192,384]{1,0:T(8,128)(2,1)} collective-permute-done((bf16[192,384]{1,0:T(8,128)(2,1)S(1)}, bf16[192,384]{1,0:T(8,128)(2,1)}, u32[]{:S(2)}, u32[]{:S(2)}) %collective-permute-start.5) | collective-permute-done | bytes 147488 | tf_op jit(solution)/shard_map/ppermute | solution.py:539
  21.3 5.0 %collective-permute-done.2.refs_6_.refs_2_ = bf16[192,768]{1,0:T(8,128)(2,1)S(1)} collective-permute-done((bf16[192,768]{1,0:T(8,128)(2,1)}, bf16[192,768]{1,0:T(8,128)(2,1)S(1)}, u32[]{:S(2)}, u32[]{:S(2)}) %collective-permute-start.2) | collective-permute-done | bytes 294944 | tf_op jit(solution)/shard_map/ppermute | solution.py:539
  26.2 0.7 copy-done.10
  27.1 4.7 %collective-permute-done.3.refs_7_.refs_3_ = bf16[192,768]{1,0:T(8,128)(2,1)S(1)} collective-permute-done((bf16[192,768]{1,0:T(8,128)(2,1)}, bf16[192,768]{1,0:T(8,128)(2,1)S(1)}, u32[]{:S(2)}, u32[]{:S(2)}) %collective-permute-start.3) | collective-permute-done | bytes 294944 | tf_op jit(solution)/shard_map/ppermute | solution.py:539
  31.8 0.7 copy-done.13
  32.7 1.1 collective-permute-start.13
  33.9 1.0 copy-done.8
  34.9 1.0 copy-done.11
  35.8 1.0 copy-done.14
  36.8 12.6 %forward.1 = (bf16[1024,768]{1,0:T(8,128)(2,1)S(1)}, bf16[768,1024]{1,0:T(8,128)(2,1)S(1)}, bf16[1024,384]{1,0:T(8,128)(2,1)S(1)}, bf16[1024,256]{1,0:T(8,128)(2...) custom-call(s32[5]{0:T(128)S(1)} %pad_add_fusion.scal, ...), custom_call_target="tpu_custom_call" | custom-call | flops 8999999488 | bytes 10000000 | tf_op jit(solution)/shard_map/forward/pallas_call | solution.py:614
  49.7 1.5 collective-permute-done.14.refs_3_
  51.2 5.2 %gate.1 = (bf16[1024,384]{1,0:T(8,128)(2,1)S(1)}, f32[1024,384]{1,0:T(8,128)S(1)}, f32[8,1024]{1,0:T(8,128)S(1)}) custom-call(s32[5]{0:T(128)S(1)} %pad_add_fusion.scal, bf16[256,768]{1,0:T(8,128)(2,1)S(1)} %bitcast.140, bf16[256,768]{1,0:T(8,128)(2,1)S(1)} %collective-permute-done.12.refs_1_, bf16[256,768]{1,0:T(8,128)(2,1)S(1)} %collective-permute-done.13.refs_2_, ...), custom_call_target="tpu_custom_call" | custom-call | flops 2000000000 | bytes 10000000 | tf_op jit(solution)/shard_map/gate/pallas_call | solution.py:614
  56.7 0.9 collective-permute-start.16
  57.6 0.8 collective-permute-start.17
  58.4 2.3 %collective-permute-done.16.refs_6_ = f32[8,1024]{1,0:T(8,128)S(1)} collective-permute-done((f32[8,1024]{1,0:T(8,128)S(1)}, f32[8,1024]{1,0:T(8,128)S(1)}, u32[]{:S(2)}, u32[]{:S(2)}) %collective-permute-start.16) | collective-permute-done | bytes 32800 | tf_op jit(solution)/shard_map/ppermute | solution.py:539
  61.1 7.0 %output.1 = (bf16[4,256,768]{2,1,0:T(8,128)(2,1)S(1)}, bf16[1024,384]{1,0:T(8,128)(2,1)S(1)}, bf16[1024,384]{1,0:T(8,128)(2,1)S(1)}, bf16[8,96,768]{2,1,0:T(8,128)(2,1)S(1)}) custom-call(s32[5]{0:T(128)S(1)} %pad_add_fusion.scal, bf16[256,768]{1,0:T(8,128)(2,1)S(1)} %bitcast.141, bf16[256,768]{1,0:T(8,128)(2,1)S(1)} %collective-permute-done.12.refs_1_, ...), custom_call_target="tpu_custom_call" | custom-call | flops 3000000000 | bytes 10000000 | tf_op jit(solution)/shard_map/output/pallas_call | solution.py:614
  68.2 1.8 collective-permute-start.18
  70.1 19.3 %scan_back.1 = (bf16[1024,768]{1,0:T(8,128)(2,1)S(1)}, bf16[4,8,24,640]{3,2,1,0:T(8,128)(2,1)S(1)}, f32[8,1536]{1,0:T(8,128)S(1)}) custom-call(s32[5]{0:T(128)S(1)} %pad_add_fusion.scal, bf16[768,1024]{1,0:T(8,128)(2,1)S(1)} %get-tuple-element.82.refs_8_.refs_0_, bf16[1024,384]{1,0:T(8,128)(2,1)S(1)} %get-tuple-element.83.refs_1_.refs_2_, ...), custom_call_target="tpu_custom_call" | custom-call | flops 20000000000 | bytes 10000000 | tf_op jit(solution)/shard_map/scan_back/pallas_call | solution.py:614
  89.6 1.1 fusion.1
  91.3 3.8 %collective-permute-start.23 = (bf16[96,768]{1,0:T(8,128)(2,1)S(1)}, bf16[96,768]{1,0:T(8,128)(2,1)S(1)}, u32[]{:S(2)}, u32[]{:S(2)}) collective-permute-start(bf16[96,768]{1,0:T(8,128)(2,1)S(1)} %get-tuple-element.134), channel_id=1, source_target_pairs={{0,6},{1,7},{2,4},{3,5},{4,2},{5,3},{6,0},{7,1},{8,14},{9,15},{10,... | collective-permute-start | bytes 442376 | tf_op jit(solution)/shard_map/ppermute | solution.py:539
  95.7 1.6 collective-permute-start.24
  97.4 4.6 %normed_grad.1 = bf16[4,256,768]{2,1,0:T(8,128)(2,1)S(1)} custom-call(s32[5]{0:T(128)S(1)} %pad_add_fusion.scal, bf16[192,768]{1,0:T(8,128)(2,1)S(1)} %copy-done.6, bf16[192,768]{1,0:T(8,128)(2,1)S(1)} %copy-done.9, bf16[192,768]{1,0:T(8,128)(2,1)S(1)} %copy-done.12, bf16[192,768]{1,0:T(8,128)(2,1)S(1)} %copy-done.15, ...), custom_call_target="tpu_custom_call" | custom-call | flops 5000000000 | bytes 10000000 | tf_op jit(solution)/shard_map/normed_grad/pallas_call | solution.py:614
  102.0 3.5 %collective-permute-done.24 = f32[8,1536]{1,0:T(8,128)S(1)} collective-permute-done((f32[8,1536]{1,0:T(8,128)S(1)}, f32[8,1536]{1,0:T(8,128)S(1)}, u32[]{:S(2)}, u32[]{:S(2)}) %collective-permute-start.24) | collective-permute-done | bytes 49184 | tf_op jit(solution)/shard_map/ppermute | solution.py:539
  105.6 2.4 %collective-permute-done.22 = bf16[96,768]{1,0:T(8,128)(2,1)S(1)} collective-permute-done((bf16[96,768]{1,0:T(8,128)(2,1)S(1)}, bf16[96,768]{1,0:T(8,128)(2,1)S(1)}, u32[]{:S(2)}, u32[]{:S(2)}) %collective-permute-start.22) | collective-permute-done | bytes 147488 | tf_op jit(solution)/shard_map/ppermute | solution.py:539
  107.9 0.7 fusion.18
  108.8 0.9 slice_bitcast_fusion
  109.9 2.5 %collective-permute-start.27 = (bf16[4,24,640]{2,1,0:T(8,128)(2,1)S(1)}, bf16[4,24,640]{2,1,0:T(8,128)(2,1)S(1)}, u32[]{:S(2)}, u32[]{:S(2)}) collective-permute-start(bf16[4,24,640]{2,1,0:T(8,128)(2,1)S(1)} %get-tuple-element.137), channel_id=1, source_target_pairs={{0,6},{1,7},{2,4},{3,5},{4,2},{5,3},{6,0},{7,1},{8,14},{9,15},{10,... | collective-permute-start | bytes 368648 | tf_op jit(solution)/shard_map/ppermute | solution.py:539
  112.4 1.9 %collective-permute-start.25 = (bf16[4,24,640]{2,1,0:T(8,128)(2,1)S(1)}, bf16[4,24,640]{2,1,0:T(8,128)(2,1)S(1)}, u32[]{:S(2)}, u32[]{:S(2)}) collective-permute-start(bf16[4,24,640]{2,1,0:T(8,128)(2,1)S(1)} %get-tuple-element.136), channel_id=1, source_target_pairs={{0,2},{1,3},{2,0},{3,1},{4,6},{5,7},{6,4},{7,5},{8,10},{9,11},{10,... | collective-permute-start | bytes 368648 | tf_op jit(solution)/shard_map/ppermute | solution.py:539
  114.3 0.9 slice.190
  115.2 1.4 fusion
  116.6 1.1 collective-permute-start.29
  118.0 4.8 %collective-permute-done.26 = bf16[4,24,640]{2,1,0:T(8,128)(2,1)S(1)} collective-permute-done((bf16[4,24,640]{2,1,0:T(8,128)(2,1)S(1)}, bf16[4,24,640]{2,1,0:T(8,128)(2,1)S(1)}, u32[]{:S(2)}, u32[]{:S(2)}) %collective-permute-start.26) | collective-permute-done | bytes 122912 | tf_op jit(solution)/shard_map/ppermute | solution.py:539
  122.9 4.5 %collective-permute-done.29 = bf16[256,768]{1,0:T(8,128)(2,1)S(1)} collective-permute-done((bf16[256,768]{1,0:T(8,128)(2,1)S(1)}, bf16[256,768]{1,0:T(8,128)(2,1)S(1)}, u32[]{:S(2)}, u32[]{:S(2)}) %collective-permute-start.29) | collective-permute-done | bytes 393248 | tf_op jit(solution)/shard_map/ppermute | solution.py:539
  127.5 1.1 collective-permute-start.31
  128.6 0.8 collective-permute-start.32
  129.3 1.3 collective-permute-start.33
  130.6 1.6 collective-permute-start.35
  132.6 5.7 %collective-permute-done.35 = f32[8,1536]{1,0:T(8,128)S(1)} collective-permute-done((f32[8,1536]{1,0:T(8,128)S(1)}, f32[8,1536]{1,0:T(8,128)S(1)}, u32[]{:S(2)}, u32[]{:S(2)}) %collective-permute-start.35) | collective-permute-done | bytes 49184 | tf_op jit(solution)/shard_map/ppermute | solution.py:539
  138.5 2.1 %collective-permute-start.34 = (bf16[2,48,768]{2,1,0:T(8,128)(2,1)S(1)}, bf16[2,48,768]{2,1,0:T(8,128)(2,1)S(1)}, u32[]{:S(2)}, u32[]{:S(2)}) collective-permute-start(bf16[2,48,768]{2,1,0:T(8,128)(2,1)S(1)} %pad_maximum_fusion.4), channel_id=1, source_target_pairs={{0,2},{1,3},{2,0},{3,1},{4,6},{5,7},{6,4},{7,5},{8,10},{9,11},{10,... | collective-permute-start | bytes 442376 | tf_op jit(solution)/shard_map/ppermute | solution.py:539
  140.6 2.4 %collective-permute-done.36 = f32[8,1536]{1,0:T(8,128)S(1)} collective-permute-done((f32[8,1536]{1,0:T(8,128)S(1)}, f32[8,1536]{1,0:T(8,128)S(1)}, u32[]{:S(2)}, u32[]{:S(2)}) %collective-permute-start.36) | collective-permute-done | bytes 49184 | tf_op jit(solution)/shard_map/ppermute | solution.py:539
  143.0 2.3 %collective-permute-done.34 = bf16[2,48,768]{2,1,0:T(8,128)(2,1)S(1)} collective-permute-done((bf16[2,48,768]{2,1,0:T(8,128)(2,1)S(1)}, bf16[2,48,768]{2,1,0:T(8,128)(2,1)S(1)}, u32[]{:S(2)}, u32[]{:S(2)}) %collective-permute-start.34) | collective-permute-done | bytes 147488 | tf_op jit(solution)/shard_map/ppermute | solution.py:539
  145.3 2.4 %collective-permute-start.39 = (bf16[1,24,3328]{2,1,0:T(8,128)(2,1)S(1)}, bf16[1,24,3328]{2,1,0:T(8,128)(2,1)S(1)}, u32[]{:S(2)}, u32[]{:S(2)}) collective-permute-start(bf16[1,24,3328]{2,1,0:T(8,128)(2,1)S(1)} %bitcast.147), channel_id=1, source_target_pairs={{0,6},{1,7},{2,4},{3,5},{4,2},{5,3},{6,0},{7,1},{8,14},{9,15},{10,... | collective-permute-start | bytes 479240 | tf_op jit(solution)/shard_map/ppermute | solution.py:539
  147.7 2.0 %collective-permute-start.37 = (bf16[1,24,3328]{2,1,0:T(8,128)(2,1)S(1)}, bf16[1,24,3328]{2,1,0:T(8,128)(2,1)S(1)}, u32[]{:S(2)}, u32[]{:S(2)}) collective-permute-start(bf16[1,24,3328]{2,1,0:T(8,128)(2,1)S(1)} %bitcast.149), channel_id=1, source_target_pairs={{0,2},{1,3},{2,0},{3,1},{4,6},{5,7},{6,4},{7,5},{8,10},{9,11},{10,... | collective-permute-start | bytes 479240 | tf_op jit(solution)/shard_map/ppermute | solution.py:539
  149.7 1.5 collective-permute-start.40
  151.2 3.0 %collective-permute-done.39 = bf16[1,24,3328]{2,1,0:T(8,128)(2,1)S(1)} collective-permute-done((bf16[1,24,3328]{2,1,0:T(8,128)(2,1)S(1)}, bf16[1,24,3328]{2,1,0:T(8,128)(2,1)S(1)}, u32[]{:S(2)}, u32[]{:S(2)}) %collective-permute-start.39) | collective-permute-done | bytes 159776 | tf_op jit(solution)/shard_map/ppermute | solution.py:539
  154.2 6.7 %collective-permute-done.38 = bf16[1,24,3328]{2,1,0:T(8,128)(2,1)S(1)} collective-permute-done((bf16[1,24,3328]{2,1,0:T(8,128)(2,1)S(1)}, bf16[1,24,3328]{2,1,0:T(8,128)(2,1)S(1)}, u32[]{:S(2)}, u32[]{:S(2)}) %collective-permute-start.38) | collective-permute-done | bytes 159776 | tf_op jit(solution)/shard_map/ppermute | solution.py:539
  161.1 1.1 collective-permute-start.42
  162.2 1.5 collective-permute-start.43
  163.8 1.1 collective-permute-start.44
  164.8 1.6 out_weight_grad.1
  167.0 5.8 %collective-permute-done.44 = f32[8,3072]{1,0:T(8,128)S(1)} collective-permute-done((f32[8,3072]{1,0:T(8,128)S(1)}, f32[8,3072]{1,0:T(8,128)S(1)}, u32[]{:S(2)}, u32[]{:S(2)}) %collective-permute-start.44) | collective-permute-done | bytes 98336 | tf_op jit(solution)/shard_map/ppermute | solution.py:539
  175.2 1.3 fusion.14
  176.8 0.9 copy-done.1
  177.8 2.9 %in_weight_grad.1 = (f32[192,3352]{1,0:T(8,128)}, f32[8,192]{1,0:T(8,128)S(1)}) custom-call(s32[5]{0:T(128)S(1)} %pad_add_fusion.scal, bf16[8,24,3328]{2,1,0:T(8,128)(2,1)S(1)} %pad_maximum_fusion.refs_0_, f32[192,128]{1,0:T(8,128)S(1)} %get-tuple-element.121.refs_1_, bf16[192,3352]{1,0:T(8,128)(2,1)S(1)} %copy-done.1, f32[1,192]{1,0:T(1,128)S(1)} %bitcast.142), custom_call_target="tpu_custom_call" | custom-call | flops 100000000 | bytes 6000000 | tf_op jit(solution)/shard_map/in_weight_grad/pallas_call | solution.py:614
  (147 shorter events, 11.9 us)
Async XLA Ops:
  0.6 13.5 %collective-permute-start = (bf16[256,768]{1,0:T(8,128)(2,1)}, bf16[256,768]{1,0:T(8,128)(2,1)S(1)}, u32[]{:S(2)}, u32[]{:S(2)}) collective-permute-start(bf16[256,768]{1,0:T(8,128)(2,1)} %bitcast.132), channel_id=1, source_target_pairs={{0,16},{8,24},{16,0},{24,8},{1,17},{9,25},{17,1},{25,9},{2,18},{10... | collective-permute-start | bytes 1179656 | tf_op jit(solution)/shard_map/ppermute | solution.py:539
  3.6 30.2 %collective-permute-start.7 = (bf16[256,768]{1,0:T(8,128)(2,1)}, bf16[256,768]{1,0:T(8,128)(2,1)S(1)}, u32[]{:S(2)}, u32[]{:S(2)}) collective-permute-start(bf16[256,768]{1,0:T(8,128)(2,1)} %bitcast.133), channel_id=1, source_target_pairs={{0,8},{8,0},{16,24},{24,16},{1,9},{9,1},{17,25},{25,17},{2,10},{10... | collective-permute-start | bytes 1179656 | tf_op jit(solution)/shard_map/ppermute | solution.py:539
  6.8 1.3 copy-start
  8.1 24.4 %copy-start.4 = (bf16[1,256,768]{2,1,0:T(8,128)(2,1)S(1)}, bf16[1,256,768]{2,1,0:T(8,128)(2,1)}, u32[]{:S(2)}) copy-start(bf16[1,256,768]{2,1,0:T(8,128)(2,1)} %param.13) | copy-start | bytes 1179652
  8.1 25.8 %copy-start.2 = (bf16[1,256,768]{2,1,0:T(8,128)(2,1)S(1)}, bf16[1,256,768]{2,1,0:T(8,128)(2,1)}, u32[]{:S(2)}) copy-start(bf16[1,256,768]{2,1,0:T(8,128)(2,1)} %param.12) | copy-start | bytes 1179652
  9.6 41.6 %copy-start.5 = (bf16[192,768]{1,0:T(8,128)(2,1)}, bf16[192,768]{1,0:T(8,128)(2,1)S(1)}, u32[]{:S(2)}) copy-start(bf16[192,768]{1,0:T(8,128)(2,1)S(1)} %get-tuple-element.74.refs_4_.refs_0_) | copy-start | bytes 884740
  9.6 3.6 %collective-permute-start.11 = (bf16[24,128]{1,0:T(8,128)(2,1)S(1)}, bf16[24,128]{1,0:T(8,128)(2,1)S(1)}, u32[]{:S(2)}, u32[]{:S(2)}) collective-permute-start(bf16[24,128]{1,0:T(8,128)(2,1)S(1)} %pad_bitcast_fusion), channel_id=1, source_target_pairs={{0,24},{8,16},{16,8},{24,0},{1,25},{9,17},{17,9},{25,1},{2,26},{10... | collective-permute-start | bytes 18440 | tf_op jit(solution)/shard_map/ppermute | solution.py:539
  9.8 3.9 %collective-permute-start.10 = (bf16[24,128]{1,0:T(8,128)(2,1)S(1)}, bf16[24,128]{1,0:T(8,128)(2,1)S(1)}, u32[]{:S(2)}, u32[]{:S(2)}) collective-permute-start(bf16[24,128]{1,0:T(8,128)(2,1)S(1)} %pad_bitcast_fusion), channel_id=1, source_target_pairs={{0,16},{8,24},{16,0},{24,8},{1,17},{9,25},{17,1},{25,9},{2,18},{10... | collective-permute-start | bytes 18440 | tf_op jit(solution)/shard_map/ppermute | solution.py:539
  11.8 1.9 %collective-permute-start.9 = (bf16[24,128]{1,0:T(8,128)(2,1)S(1)}, bf16[24,128]{1,0:T(8,128)(2,1)S(1)}, u32[]{:S(2)}, u32[]{:S(2)}) collective-permute-start(bf16[24,128]{1,0:T(8,128)(2,1)S(1)} %pad_bitcast_fusion), channel_id=1, source_target_pairs={{0,8},{8,0},{16,24},{24,16},{1,9},{9,1},{17,25},{25,17},{2,10},{10... | collective-permute-start | bytes 18440 | tf_op jit(solution)/shard_map/ppermute | solution.py:539
  13.3 6.8 %collective-permute-start.5 = (bf16[192,384]{1,0:T(8,128)(2,1)S(1)}, bf16[192,384]{1,0:T(8,128)(2,1)}, u32[]{:S(2)}, u32[]{:S(2)}) collective-permute-start(bf16[192,384]{1,0:T(8,128)(2,1)S(1)} %get-tuple-element.79.refs_8_.refs_4_), channel_id=1, source_target_pairs={{0,16},{8,24},{16,0},{24,8},{1,17},{9,25},{17,1},{25,9},{2,18},{10... | collective-permute-start | bytes 442376 | tf_op jit(solution)/shard_map/ppermute | solution.py:539
  14.2 5.9 %collective-permute-start.1 = (bf16[192,768]{1,0:T(8,128)(2,1)}, bf16[192,768]{1,0:T(8,128)(2,1)S(1)}, u32[]{:S(2)}, u32[]{:S(2)}) collective-permute-start(bf16[192,768]{1,0:T(8,128)(2,1)} %get-tuple-element.75), channel_id=1, source_target_pairs={{0,8},{8,0},{16,24},{24,16},{1,9},{9,1},{17,25},{25,17},{2,10},{10... | collective-permute-start | bytes 884744 | tf_op jit(solution)/shard_map/ppermute | solution.py:539
  15.2 11.0 %collective-permute-start.2 = (bf16[192,768]{1,0:T(8,128)(2,1)}, bf16[192,768]{1,0:T(8,128)(2,1)S(1)}, u32[]{:S(2)}, u32[]{:S(2)}) collective-permute-start(bf16[192,768]{1,0:T(8,128)(2,1)} %get-tuple-element.76), channel_id=1, source_target_pairs={{0,16},{8,24},{16,0},{24,8},{1,17},{9,25},{17,1},{25,9},{2,18},{10... | collective-permute-start | bytes 884744 | tf_op jit(solution)/shard_map/ppermute | solution.py:539
  16.1 15.7 %collective-permute-start.3 = (bf16[192,768]{1,0:T(8,128)(2,1)}, bf16[192,768]{1,0:T(8,128)(2,1)S(1)}, u32[]{:S(2)}, u32[]{:S(2)}) collective-permute-start(bf16[192,768]{1,0:T(8,128)(2,1)} %get-tuple-element.77), channel_id=1, source_target_pairs={{0,24},{8,16},{16,8},{24,0},{1,25},{9,17},{17,9},{25,1},{2,26},{10... | collective-permute-start | bytes 884744 | tf_op jit(solution)/shard_map/ppermute | solution.py:539
  20.0 13.8 %collective-permute-start.8 = (bf16[256,768]{1,0:T(8,128)(2,1)S(1)}, bf16[256,768]{1,0:T(8,128)(2,1)S(1)}, u32[]{:S(2)}, u32[]{:S(2)}) collective-permute-start(bf16[256,768]{1,0:T(8,128)(2,1)S(1)} %collective-permute-done.refs_2_), channel_id=1, source_target_pairs={{0,8},{8,0},{16,24},{24,16},{1,9},{9,1},{17,25},{25,17},{2,10},{10... | collective-permute-start | bytes 1179656 | tf_op jit(solution)/shard_map/ppermute | solution.py:539
  20.0 0.7 copy-start.7
  20.8 12.0 %collective-permute-start.4 = (bf16[192,384]{1,0:T(8,128)(2,1)S(1)}, bf16[192,384]{1,0:T(8,128)(2,1)}, u32[]{:S(2)}, u32[]{:S(2)}) collective-permute-start(bf16[192,384]{1,0:T(8,128)(2,1)S(1)} %get-tuple-element.79.refs_8_.refs_4_), channel_id=1, source_target_pairs={{0,8},{8,0},{16,24},{24,16},{1,9},{9,1},{17,25},{25,17},{2,10},{10... | collective-permute-start | bytes 442376 | tf_op jit(solution)/shard_map/ppermute | solution.py:539
  26.2 0.7 copy-start.10
  27.0 6.9 %collective-permute-start.6 = (bf16[192,384]{1,0:T(8,128)(2,1)}, bf16[192,384]{1,0:T(8,128)(2,1)}, u32[]{:S(2)}, u32[]{:S(2)}) collective-permute-start(bf16[192,384]{1,0:T(8,128)(2,1)} %collective-permute-done.5.refs_10_.refs_6_), channel_id=1, source_target_pairs={{0,8},{8,0},{16,24},{24,16},{1,9},{9,1},{17,25},{25,17},{2,10},{10... | collective-permute-start | bytes 442376 | tf_op jit(solution)/shard_map/ppermute | solution.py:539
  32.5 17.2 %copy-start.18 = (bf16[384]{0:T(512)(128)(2,1)S(1)}, bf16[384]{0:T(512)(128)(2,1)}, u32[]{:S(2)}) copy-start(bf16[384]{0:T(512)(128)(2,1)} %param.22) | copy-start | bytes 2308
  32.5 18.7 %copy-start.3 = (bf16[384,768]{1,0:T(8,128)(2,1)S(1)}, bf16[384,768]{1,0:T(8,128)(2,1)}, u32[]{:S(2)}) copy-start(bf16[384,768]{1,0:T(8,128)(2,1)} %weight.3) | copy-start | bytes 1769476
  32.5 17.2 %collective-permute-start.12 = (bf16[256,768]{1,0:T(8,128)(2,1)S(1)}, bf16[256,768]{1,0:T(8,128)(2,1)S(1)}, u32[]{:S(2)}, u32[]{:S(2)}) collective-permute-start(bf16[256,768]{1,0:T(8,128)(2,1)S(1)} %bitcast.138), channel_id=1, source_target_pairs={{0,8},{8,0},{16,24},{24,16},{1,9},{9,1},{17,25},{25,17},{2,10},{10... | collective-permute-start | bytes 1179656 | tf_op jit(solution)/shard_map/ppermute | solution.py:539
  32.7 16.7 %collective-permute-start.13 = (bf16[256,768]{1,0:T(8,128)(2,1)S(1)}, bf16[256,768]{1,0:T(8,128)(2,1)S(1)}, u32[]{:S(2)}, u32[]{:S(2)}) collective-permute-start(bf16[256,768]{1,0:T(8,128)(2,1)S(1)} %bitcast.139), channel_id=1, source_target_pairs={{0,16},{8,24},{16,0},{24,8},{1,17},{9,25},{17,1},{25,9},{2,18},{10... | collective-permute-start | bytes 1179656 | tf_op jit(solution)/shard_map/ppermute | solution.py:539
  33.9 1.0 copy-start.8
  34.8 1.0 copy-start.11
  35.8 1.0 copy-start.14
  49.4 1.8 collective-permute-start.14
  56.5 1.9 %collective-permute-start.15 = (f32[8,1024]{1,0:T(8,128)S(1)}, f32[8,1024]{1,0:T(8,128)S(1)}, u32[]{:S(2)}, u32[]{:S(2)}) collective-permute-start(f32[8,1024]{1,0:T(8,128)S(1)} %get-tuple-element.92.refs_4_), channel_id=1, source_target_pairs={{0,8},{8,0},{16,24},{24,16},{1,9},{9,1},{17,25},{25,17},{2,10},{10... | collective-permute-start | bytes 98312 | tf_op jit(solution)/shard_map/ppermute | solution.py:539
  56.7 4.0 %collective-permute-start.16 = (f32[8,1024]{1,0:T(8,128)S(1)}, f32[8,1024]{1,0:T(8,128)S(1)}, u32[]{:S(2)}, u32[]{:S(2)}) collective-permute-start(f32[8,1024]{1,0:T(8,128)S(1)} %get-tuple-element.92.refs_4_), channel_id=1, source_target_pairs={{0,16},{8,24},{16,0},{24,8},{1,17},{9,25},{17,1},{25,9},{2,18},{10... | collective-permute-start | bytes 98312 | tf_op jit(solution)/shard_map/ppermute | solution.py:539
  57.6 3.5 %collective-permute-start.17 = (f32[8,1024]{1,0:T(8,128)S(1)}, f32[8,1024]{1,0:T(8,128)S(1)}, u32[]{:S(2)}, u32[]{:S(2)}) collective-permute-start(f32[8,1024]{1,0:T(8,128)S(1)} %get-tuple-element.92.refs_4_), channel_id=1, source_target_pairs={{0,24},{8,16},{16,8},{24,0},{1,25},{9,17},{17,9},{25,1},{2,26},{10... | collective-permute-start | bytes 98312 | tf_op jit(solution)/shard_map/ppermute | solution.py:539
  68.2 21.2 %collective-permute-start.18 = (bf16[4,96,768]{2,1,0:T(8,128)(2,1)S(1)}, bf16[4,96,768]{2,1,0:T(8,128)(2,1)S(1)}, u32[]{:S(2)}, u32[]{:S(2)}) collective-permute-start(bf16[4,96,768]{2,1,0:T(8,128)(2,1)S(1)} %slice_bitcast_fusion.4), channel_id=1, source_target_pairs={{0,1},{1,0},{2,3},{3,2},{4,5},{5,4},{6,7},{7,6},{8,9},{9,8},{10,11... | collective-permute-start | bytes 1769480 | tf_op jit(solution)/shard_map/ppermute | solution.py:539
  70.0 19.6 %collective-permute-start.19 = (bf16[2,256,768]{2,1,0:T(8,128)(2,1)S(1)}, bf16[2,256,768]{2,1,0:T(8,128)(2,1)S(1)}, u32[]{:S(2)}, u32[]{:S(2)}) collective-permute-start(bf16[2,256,768]{2,1,0:T(8,128)(2,1)S(1)} %slice_bitcast_fusion.2), channel_id=1, source_target_pairs={{0,8},{8,0},{16,24},{24,16},{1,9},{9,1},{17,25},{25,17},{2,10},{10... | collective-permute-start | bytes 2359304 | tf_op jit(solution)/shard_map/ppermute | solution.py:539
  90.7 6.7 %copy-start.6 = (bf16[192,768]{1,0:T(8,128)(2,1)S(1)}, bf16[192,768]{1,0:T(8,128)(2,1)}, u32[]{:S(2)}) copy-start(bf16[192,768]{1,0:T(8,128)(2,1)} %copy-done.5) | copy-start | bytes 884740
  90.7 6.7 %copy-start.9 = (bf16[192,768]{1,0:T(8,128)(2,1)S(1)}, bf16[192,768]{1,0:T(8,128)(2,1)}, u32[]{:S(2)}) copy-start(bf16[192,768]{1,0:T(8,128)(2,1)} %copy-done.7) | copy-start | bytes 884740
  90.7 6.7 %copy-start.12 = (bf16[192,768]{1,0:T(8,128)(2,1)S(1)}, bf16[192,768]{1,0:T(8,128)(2,1)}, u32[]{:S(2)}) copy-start(bf16[192,768]{1,0:T(8,128)(2,1)} %copy-done.10) | copy-start | bytes 884740
  90.7 6.7 %copy-start.15 = (bf16[192,768]{1,0:T(8,128)(2,1)S(1)}, bf16[192,768]{1,0:T(8,128)(2,1)}, u32[]{:S(2)}) copy-start(bf16[192,768]{1,0:T(8,128)(2,1)} %copy-done.13) | copy-start | bytes 884740
  90.8 17.9 %collective-permute-start.20 = (bf16[4,4,24,640]{3,2,0,1:T(8,128)(2,1)S(1)}, bf16[4,4,24,640]{3,2,0,1:T(8,128)(2,1)S(1)}, u32[]{:S(2)}, u32[]{:S(2)}) collective-permute-start(bf16[4,4,24,640]{3,2,0,1:T(8,128)(2,1)S(1)} %bitcast.146), channel_id=1, source_target_pairs={{0,1},{1,0},{2,3},{3,2},{4,5},{5,4},{6,7},{7,6},{8,9},{9,8},{10,11... | collective-permute-start | bytes 1474568 | tf_op jit(solution)/shard_map/ppermute | solution.py:539
  91.3 14.3 %collective-permute-start.23 = (bf16[96,768]{1,0:T(8,128)(2,1)S(1)}, bf16[96,768]{1,0:T(8,128)(2,1)S(1)}, u32[]{:S(2)}, u32[]{:S(2)}) collective-permute-start(bf16[96,768]{1,0:T(8,128)(2,1)S(1)} %get-tuple-element.134), channel_id=1, source_target_pairs={{0,6},{1,7},{2,4},{3,5},{4,2},{5,3},{6,0},{7,1},{8,14},{9,15},{10,... | collective-permute-start | bytes 442376 | tf_op jit(solution)/shard_map/ppermute | solution.py:539
  95.1 12.8 %collective-permute-start.22 = (bf16[96,768]{1,0:T(8,128)(2,1)S(1)}, bf16[96,768]{1,0:T(8,128)(2,1)S(1)}, u32[]{:S(2)}, u32[]{:S(2)}) collective-permute-start(bf16[96,768]{1,0:T(8,128)(2,1)S(1)} %get-tuple-element.135), channel_id=1, source_target_pairs={{0,4},{1,5},{2,6},{3,7},{4,0},{5,1},{6,2},{7,3},{8,12},{9,13},{10,... | collective-permute-start | bytes 442376 | tf_op jit(solution)/shard_map/ppermute | solution.py:539
  95.1 12.8 %collective-permute-start.21 = (bf16[96,768]{1,0:T(8,128)(2,1)S(1)}, bf16[96,768]{1,0:T(8,128)(2,1)S(1)}, u32[]{:S(2)}, u32[]{:S(2)}) collective-permute-start(bf16[96,768]{1,0:T(8,128)(2,1)S(1)} %get-tuple-element.133), channel_id=1, source_target_pairs={{0,2},{1,3},{2,0},{3,1},{4,6},{5,7},{6,4},{7,5},{8,10},{9,11},{10,... | collective-permute-start | bytes 442376 | tf_op jit(solution)/shard_map/ppermute | solution.py:539
  95.7 9.8 %collective-permute-start.24 = (f32[8,1536]{1,0:T(8,128)S(1)}, f32[8,1536]{1,0:T(8,128)S(1)}, u32[]{:S(2)}, u32[]{:S(2)}) collective-permute-start(f32[8,1536]{1,0:T(8,128)S(1)} %get-tuple-element.105), channel_id=1, source_target_pairs={{0,1},{1,0},{2,3},{3,2},{4,5},{5,4},{6,7},{7,6},{8,9},{9,8},{10,11... | collective-permute-start | bytes 147464 | tf_op jit(solution)/shard_map/ppermute | solution.py:539
  108.7 1.1 copy-start.19
  109.7 5.5 %collective-permute-start.28 = (bf16[2,256,768]{2,1,0:T(8,128)(2,1)}, bf16[2,256,768]{2,1,0:T(8,128)(2,1)}, u32[]{:S(2)}, u32[]{:S(2)}) collective-permute-start(bf16[2,256,768]{2,1,0:T(8,128)(2,1)} %slice_bitcast_fusion), channel_id=1, source_target_pairs={{0,8},{8,0},{16,24},{24,16},{1,9},{9,1},{17,25},{25,17},{2,10},{10... | collective-permute-start | bytes 2359304 | tf_op jit(solution)/shard_map/ppermute | solution.py:539
  109.9 8.1 %collective-permute-start.27 = (bf16[4,24,640]{2,1,0:T(8,128)(2,1)S(1)}, bf16[4,24,640]{2,1,0:T(8,128)(2,1)S(1)}, u32[]{:S(2)}, u32[]{:S(2)}) collective-permute-start(bf16[4,24,640]{2,1,0:T(8,128)(2,1)S(1)} %get-tuple-element.137), channel_id=1, source_target_pairs={{0,6},{1,7},{2,4},{3,5},{4,2},{5,3},{6,0},{7,1},{8,14},{9,15},{10,... | collective-permute-start | bytes 368648 | tf_op jit(solution)/shard_map/ppermute | solution.py:539
  112.4 10.4 %collective-permute-start.26 = (bf16[4,24,640]{2,1,0:T(8,128)(2,1)S(1)}, bf16[4,24,640]{2,1,0:T(8,128)(2,1)S(1)}, u32[]{:S(2)}, u32[]{:S(2)}) collective-permute-start(bf16[4,24,640]{2,1,0:T(8,128)(2,1)S(1)} %get-tuple-element.138), channel_id=1, source_target_pairs={{0,4},{1,5},{2,6},{3,7},{4,0},{5,1},{6,2},{7,3},{8,12},{9,13},{10,... | collective-permute-start | bytes 368648 | tf_op jit(solution)/shard_map/ppermute | solution.py:539
  112.4 10.4 %collective-permute-start.25 = (bf16[4,24,640]{2,1,0:T(8,128)(2,1)S(1)}, bf16[4,24,640]{2,1,0:T(8,128)(2,1)S(1)}, u32[]{:S(2)}, u32[]{:S(2)}) collective-permute-start(bf16[4,24,640]{2,1,0:T(8,128)(2,1)S(1)} %get-tuple-element.136), channel_id=1, source_target_pairs={{0,2},{1,3},{2,0},{3,1},{4,6},{5,7},{6,4},{7,5},{8,10},{9,11},{10,... | collective-permute-start | bytes 368648 | tf_op jit(solution)/shard_map/ppermute | solution.py:539
  115.2 2.5 %copy-start.17 = (bf16[96,768]{1,0:T(8,128)(2,1)S(1)}, bf16[96,768]{1,0:T(8,128)(2,1)}, u32[]{:S(2)}) copy-start(bf16[96,768]{1,0:T(8,128)(2,1)} %fusion.18) | copy-start | bytes 442372
  116.6 10.8 %collective-permute-start.29 = (bf16[256,768]{1,0:T(8,128)(2,1)S(1)}, bf16[256,768]{1,0:T(8,128)(2,1)S(1)}, u32[]{:S(2)}, u32[]{:S(2)}) collective-permute-start(bf16[256,768]{1,0:T(8,128)(2,1)S(1)} %slice_bitcast_fusion.7), channel_id=1, source_target_pairs={{0,16},{8,24},{16,0},{24,8},{1,17},{9,25},{17,1},{25,9},{2,18},{10... | collective-permute-start | bytes 1179656 | tf_op jit(solution)/shard_map/ppermute | solution.py:539
  127.4 11.0 %collective-permute-start.30 = (bf16[24,1024]{1,0:T(8,128)(2,1)S(1)}, bf16[24,1024]{1,0:T(8,128)(2,1)S(1)}, u32[]{:S(2)}, u32[]{:S(2)}) collective-permute-start(bf16[24,1024]{1,0:T(8,128)(2,1)S(1)} %pad_maximum_fusion.6), channel_id=1, source_target_pairs={{0,8},{8,0},{16,24},{24,16},{1,9},{9,1},{17,25},{25,17},{2,10},{10... | collective-permute-start | bytes 147464 | tf_op jit(solution)/shard_map/ppermute | solution.py:539
  127.5 10.9 %collective-permute-start.31 = (bf16[24,1024]{1,0:T(8,128)(2,1)S(1)}, bf16[24,1024]{1,0:T(8,128)(2,1)S(1)}, u32[]{:S(2)}, u32[]{:S(2)}) collective-permute-start(bf16[24,1024]{1,0:T(8,128)(2,1)S(1)} %pad_maximum_fusion.7), channel_id=1, source_target_pairs={{0,16},{8,24},{16,0},{24,8},{1,17},{9,25},{17,1},{25,9},{2,18},{10... | collective-permute-start | bytes 147464 | tf_op jit(solution)/shard_map/ppermute | solution.py:539
  128.6 9.8 %collective-permute-start.32 = (bf16[24,1024]{1,0:T(8,128)(2,1)S(1)}, bf16[24,1024]{1,0:T(8,128)(2,1)S(1)}, u32[]{:S(2)}, u32[]{:S(2)}) collective-permute-start(bf16[24,1024]{1,0:T(8,128)(2,1)S(1)} %pad_maximum_fusion.8), channel_id=1, source_target_pairs={{0,24},{8,16},{16,8},{24,0},{1,25},{9,17},{17,9},{25,1},{2,26},{10... | collective-permute-start | bytes 147464 | tf_op jit(solution)/shard_map/ppermute | solution.py:539
  129.3 9.1 %collective-permute-start.33 = (bf16[1,48,768]{2,1,0:T(8,128)(2,1)S(1)}, bf16[1,48,768]{2,1,0:T(8,128)(2,1)S(1)}, u32[]{:S(2)}, u32[]{:S(2)}) collective-permute-start(bf16[1,48,768]{2,1,0:T(8,128)(2,1)S(1)} %bitcast.143), channel_id=1, source_target_pairs={{0,4},{1,5},{2,6},{3,7},{4,0},{5,1},{6,2},{7,3},{8,12},{9,13},{10,... | collective-permute-start | bytes 221192 | tf_op jit(solution)/shard_map/ppermute | solution.py:539
  130.6 7.6 %collective-permute-start.35 = (f32[8,1536]{1,0:T(8,128)S(1)}, f32[8,1536]{1,0:T(8,128)S(1)}, u32[]{:S(2)}, u32[]{:S(2)}) collective-permute-start(f32[8,1536]{1,0:T(8,128)S(1)} %add.104), channel_id=1, source_target_pairs={{0,4},{1,5},{2,6},{3,7},{4,0},{5,1},{6,2},{7,3},{8,12},{9,13},{10,... | collective-permute-start | bytes 147464 | tf_op jit(solution)/shard_map/ppermute | solution.py:539
  138.3 4.7 %collective-permute-start.36 = (f32[8,1536]{1,0:T(8,128)S(1)}, f32[8,1536]{1,0:T(8,128)S(1)}, u32[]{:S(2)}, u32[]{:S(2)}) collective-permute-start(f32[8,1536]{1,0:T(8,128)S(1)} %add.112), channel_id=1, source_target_pairs={{0,2},{1,3},{2,0},{3,1},{4,6},{5,7},{6,4},{7,5},{8,10},{9,11},{10,... | collective-permute-start | bytes 147464 | tf_op jit(solution)/shard_map/ppermute | solution.py:539
  138.5 6.7 %collective-permute-start.34 = (bf16[2,48,768]{2,1,0:T(8,128)(2,1)S(1)}, bf16[2,48,768]{2,1,0:T(8,128)(2,1)S(1)}, u32[]{:S(2)}, u32[]{:S(2)}) collective-permute-start(bf16[2,48,768]{2,1,0:T(8,128)(2,1)S(1)} %pad_maximum_fusion.4), channel_id=1, source_target_pairs={{0,2},{1,3},{2,0},{3,1},{4,6},{5,7},{6,4},{7,5},{8,10},{9,11},{10,... | collective-permute-start | bytes 442376 | tf_op jit(solution)/shard_map/ppermute | solution.py:539
  140.6 20.5 %copy-start.16 = (bf16[2,256,768]{2,1,0:T(8,128)(2,1)S(1)}, bf16[2,256,768]{2,1,0:T(8,128)(2,1)}, u32[]{:S(2)}) copy-start(bf16[2,256,768]{2,1,0:T(8,128)(2,1)} %fusion.1) | copy-start | bytes 2359300
  145.3 8.9 %collective-permute-start.39 = (bf16[1,24,3328]{2,1,0:T(8,128)(2,1)S(1)}, bf16[1,24,3328]{2,1,0:T(8,128)(2,1)S(1)}, u32[]{:S(2)}, u32[]{:S(2)}) collective-permute-start(bf16[1,24,3328]{2,1,0:T(8,128)(2,1)S(1)} %bitcast.147), channel_id=1, source_target_pairs={{0,6},{1,7},{2,4},{3,5},{4,2},{5,3},{6,0},{7,1},{8,14},{9,15},{10,... | collective-permute-start | bytes 479240 | tf_op jit(solution)/shard_map/ppermute | solution.py:539
  147.7 13.2 %collective-permute-start.38 = (bf16[1,24,3328]{2,1,0:T(8,128)(2,1)S(1)}, bf16[1,24,3328]{2,1,0:T(8,128)(2,1)S(1)}, u32[]{:S(2)}, u32[]{:S(2)}) collective-permute-start(bf16[1,24,3328]{2,1,0:T(8,128)(2,1)S(1)} %bitcast.148), channel_id=1, source_target_pairs={{0,4},{1,5},{2,6},{3,7},{4,0},{5,1},{6,2},{7,3},{8,12},{9,13},{10,... | collective-permute-start | bytes 479240 | tf_op jit(solution)/shard_map/ppermute | solution.py:539
  147.7 13.2 %collective-permute-start.37 = (bf16[1,24,3328]{2,1,0:T(8,128)(2,1)S(1)}, bf16[1,24,3328]{2,1,0:T(8,128)(2,1)S(1)}, u32[]{:S(2)}, u32[]{:S(2)}) collective-permute-start(bf16[1,24,3328]{2,1,0:T(8,128)(2,1)S(1)} %bitcast.149), channel_id=1, source_target_pairs={{0,2},{1,3},{2,0},{3,1},{4,6},{5,7},{6,4},{7,5},{8,10},{9,11},{10,... | collective-permute-start | bytes 479240 | tf_op jit(solution)/shard_map/ppermute | solution.py:539
  149.7 11.3 %collective-permute-start.40 = (bf16[4,48,768]{2,1,0:T(8,128)(2,1)S(1)}, bf16[4,48,768]{2,1,0:T(8,128)(2,1)S(1)}, u32[]{:S(2)}, u32[]{:S(2)}) collective-permute-start(bf16[4,48,768]{2,1,0:T(8,128)(2,1)S(1)} %pad_maximum_fusion.3), channel_id=1, source_target_pairs={{0,1},{1,0},{2,3},{3,2},{4,5},{5,4},{6,7},{7,6},{8,9},{9,8},{10,11... | collective-permute-start | bytes 884744 | tf_op jit(solution)/shard_map/ppermute | solution.py:539
  151.2 9.8 %collective-permute-start.41 = (f32[8,1536]{1,0:T(8,128)S(1)}, f32[8,1536]{1,0:T(8,128)S(1)}, u32[]{:S(2)}, u32[]{:S(2)}) collective-permute-start(f32[8,1536]{1,0:T(8,128)S(1)} %add.113.refs_0_), channel_id=1, source_target_pairs={{0,8},{8,0},{16,24},{24,16},{1,9},{9,1},{17,25},{25,17},{2,10},{10... | collective-permute-start | bytes 147464 | tf_op jit(solution)/shard_map/ppermute | solution.py:539
  161.1 14.1 %collective-permute-start.42 = (bf16[256,768]{1,0:T(8,128)(2,1)S(1)}, bf16[256,768]{1,0:T(8,128)(2,1)S(1)}, u32[]{:S(2)}, u32[]{:S(2)}) collective-permute-start(bf16[256,768]{1,0:T(8,128)(2,1)S(1)} %slice_bitcast_fusion.8), channel_id=1, source_target_pairs={{0,16},{8,24},{16,0},{24,8},{1,17},{9,25},{17,1},{25,9},{2,18},{10... | collective-permute-start | bytes 1179656 | tf_op jit(solution)/shard_map/ppermute | solution.py:539
  162.2 14.5 %collective-permute-start.43 = (bf16[4,24,3328]{2,1,0:T(8,128)(2,1)S(1)}, bf16[4,24,3328]{2,1,0:T(8,128)(2,1)S(1)}, u32[]{:S(2)}, u32[]{:S(2)}) collective-permute-start(bf16[4,24,3328]{2,1,0:T(8,128)(2,1)S(1)} %pad_maximum_fusion.1), channel_id=1, source_target_pairs={{0,1},{1,0},{2,3},{3,2},{4,5},{5,4},{6,7},{7,6},{8,9},{9,8},{10,11... | collective-permute-start | bytes 1916936 | tf_op jit(solution)/shard_map/ppermute | solution.py:539
  163.8 9.1 %collective-permute-start.44 = (f32[8,3072]{1,0:T(8,128)S(1)}, f32[8,3072]{1,0:T(8,128)S(1)}, u32[]{:S(2)}, u32[]{:S(2)}) collective-permute-start(f32[8,3072]{1,0:T(8,128)S(1)} %pad_maximum_fusion.5), channel_id=1, source_target_pairs={{0,16},{8,24},{16,0},{24,8},{1,17},{9,25},{17,1},{25,9},{2,18},{10... | collective-permute-start | bytes 294920 | tf_op jit(solution)/shard_map/ppermute | solution.py:539
  176.5 1.3 copy-start.1
  (1 other events, 0.7 us)

commit v3 on v2

--- a/solution.py
+++ b/solution.py
@@ -19,6 +19,7 @@
 F32 = jnp.float32
 ANY = pltpu.HBM
 VMEM_LIMIT = 24 * 1024 * 1024
+LIMITS = {"params": 4 << 20, "packets": 16 << 20}
 
 
 def dot(a, b):
@@ -145,8 +146,8 @@
 def forward_kernel(n, heads, own_heads, scal, *refs):
     xs, ws, wks = refs[:n], refs[n : 2 * n], refs[2 * n : 3 * n]
     gain, taps, hp, skip = refs[3 * n : 3 * n + 4]
-    normed_o, normed_t_o, conv_o, convk_o, raw_o, mixer_o, start_o = refs[3 * n + 4 : 3 * n + 11]
-    xv, wv, cext, state, sem_x, sem_w, sem_k = refs[3 * n + 11 :]
+    normed_o, normed_t_o, conv_o, convk_o, raw_o, mixer_o, start_o, w_o, wg_o = refs[3 * n + 4 : 3 * n + 13]
+    xv, wv, cext, state, sem_o, sem_x, sem_w, sem_k, sem_g = refs[3 * n + 13 :]
     lanes = heads * PS
     width = lanes + 2 * N
     b = pl.program_id(0)
@@ -159,10 +160,20 @@
         load_blocks(xs, xv, me, BLOCK, sem_x)
         copies = load_blocks(ws, wv, me, ws[0].shape[0], sem_w, (0, 0, lanes))
         copies += load_blocks(wks, wv, me, ws[0].shape[0], sem_k, (lanes, 0, 2 * N + 128))
+        load_blocks(ws, wg_o, me, ws[0].shape[0], sem_g, (0, lanes, lanes))
         cext[0:8, :] = jnp.zeros((8, width), F32)
         state[...] = jnp.zeros_like(state)
         for copy in copies:
             copy.wait()
+        pltpu.make_async_copy(wv, w_o, sem_o).start()
+
+    @pl.when(b == pl.num_programs(0) - 1)
+    def _():
+        rows = ws[0].shape[0]
+        for k in range(n):
+            to = wg_o.at[pl.ds(0, rows), pl.ds(0, lanes)]
+            pltpu.make_async_copy(ws[k].at[:, pl.ds(lanes, lanes)], to, sem_g.at[k]).wait()
+        pltpu.make_async_copy(wv, w_o, sem_o).wait()
 
     x = wait_block(xs[0], xv, scal[0], b, sem_x).astype(F32)
     scale = lax.rsqrt(jnp.mean(x * x, axis=1, keepdims=True) + EPS)
@@ -207,19 +218,13 @@
 
 
 def gate_kernel(n, scal, *refs):
-    gs, ws = refs[:n], refs[n : 2 * n]
-    normed, mixer, wo, gain = refs[2 * n : 2 * n + 4]
-    raw_o, gno_o, stat_o = refs[2 * n + 4 : 2 * n + 7]
-    gv, wv, sem_g, sem_w = refs[2 * n + 7 :]
+    gs = refs[:n]
+    wv, normed, mixer, wo, gain, raw_o, stat_o, gv, sem_g = refs[n:]
     b = pl.program_id(0)
 
     @pl.when(b == 0)
     def _():
-        me = scal[0]
-        load_blocks(gs, gv, me, BLOCK, sem_g)
-        lanes = wv.shape[1]
-        for copy in load_blocks(ws, wv, me, ws[0].shape[0], sem_w, (0, lanes, lanes)):
-            copy.wait()
+        load_blocks(gs, gv, scal[0], BLOCK, sem_g)
 
     raw = dot(normed[...], wv[...]).astype(BF)
     raw_o[...] = raw
@@ -227,7 +232,6 @@
     gated = mixer[...] * (gate * sigmoid(gate))
     g = wait_block(gs[0], gv, scal[0], b, sem_g)
     gno = dot_nt(g, wo[...])
-    gno_o[...] = gno
     first = jnp.sum(gated * gated, axis=1, keepdims=True)
     second = jnp.sum(gno * gain[...] * gated, axis=1, keepdims=True)
     lane = iota((BLOCK, 128), 1)
@@ -238,9 +242,9 @@
 def output_kernel(n, nd, inner, scal, *refs):
     gs = refs[:n]
     stats = refs[n : 2 * n]
-    normed_t, mixer, raw, gno, wo, gain = refs[2 * n : 2 * n + 6]
-    out_o, gssm_o, ggr_o, early_o = refs[2 * n + 6 : 2 * n + 10]
-    gv, acc_o, acc_g, sem_g = refs[2 * n + 10 :]
+    normed_t, mixer, raw, wo, gain = refs[2 * n : 2 * n + 5]
+    out_o, gssm_o, ggr_o, early_o = refs[2 * n + 5 : 2 * n + 9]
+    gv, acc_o, acc_g, sem_g = refs[2 * n + 9 :]
     b = pl.program_id(0)
 
     @pl.when(b == 0)
@@ -262,7 +266,7 @@
     g = wait_block(gs[0], gv, scal[0], b, sem_g)
     out_o[0] = dot(normed_out, wo[...]).astype(BF)
     acc_o[...] += dot_tn(normed_out, g)
-    grad_gated = scale * (gno[...] * gain[...] - gated * (mean * scale * scale))
+    grad_gated = scale * (dot_nt(g, wo[...]) * gain[...] - gated * (mean * scale * scale))
     grad_raw = (grad_gated * mix * (sig * (1.0 + gate * (1.0 - sig)))).astype(BF)
     ggr_o[...] = grad_raw
     gssm_o[...] = (grad_gated * act).astype(BF)
@@ -442,19 +446,7 @@
     return total
 
 
-def normed_kernel(n, lanes, scal, *refs):
-    ws, wks = refs[:n], refs[n : 2 * n]
-    proj, ggr, gn_o, wv, wgv, sem_w, sem_k, sem_g = refs[2 * n :]
-
-    @pl.when(pl.program_id(0) == 0)
-    def _():
-        rows = ws[0].shape[0]
-        copies = load_blocks(ws, wv, scal[0], rows, sem_w, (0, 0, lanes))
-        copies += load_blocks(wks, wv, scal[0], rows, sem_k, (lanes, 0, 2 * N + 128))
-        copies += load_blocks(ws, wgv, scal[0], rows, sem_g, (0, lanes, lanes))
-        for copy in copies:
-            copy.wait()
-
+def normed_kernel(scal, proj, ggr, wv, wgv, gn_o):
     gn_o[0] = (dot_nt(proj[...], wv[...]) + dot_nt(ggr[...], wgv[...])).astype(BF)
 
 
@@ -522,6 +514,24 @@
         at = 0 if len(order) == 1 else pl.multiple_of((place ^ scal[1]) * rows, 8)
         out[pl.ds(at, rows), :] = share[e].astype(F32)
     gain_o[...] = rows_dot(out[...], weight[...]) / gain[...]
+
+
+def params_kernel(n, own_heads, scal, *refs):
+    parts, (gain_o, taps_o, wide) = refs[:n], refs[n:]
+    own = own_heads * PS
+    lanes, chans, rows = own + own % 128, CONVCH // n, gain_o.shape[1] // n
+    for q in range(n):
+
+        @pl.when(scal[0] == q)
+        def _(q=q):
+            for j in range(n):
+                part = parts[q ^ j][...].astype(F32)
+                gain_o[:, j * rows : (j + 1) * rows] = part[0:1, 0:rows]
+                wide[:, j * chans : (j + 1) * chans] = part[:, 0:chans]
+            taps_o[...] = jnp.zeros(taps_o.shape, F32)
+            for to, at, size in ((0, q * own, own), (lanes, DI, 2 * N)):
+                taps_o[0:KCONV, to : to + size] = wide[2 : 2 + KCONV, at : at + size]
+                taps_o[KCONV : KCONV + 1, to : to + size] = wide[1:2, at : at + size]
 
 
 def packets_kernel(n, own, scal, weight, *outs):
@@ -623,7 +633,7 @@
         out_shape=out_shape,
         name=name,
         input_output_aliases=aliases,
-        compiler_params=pltpu.CompilerParams(vmem_limit_bytes=VMEM_LIMIT),
+        compiler_params=pltpu.CompilerParams(vmem_limit_bytes=LIMITS.get(name, VMEM_LIMIT)),
         cost_estimate=pl.CostEstimate(flops=flops, bytes_accessed=bytes_, transcendentals=0),
     )(scal, *args)
 
@@ -662,6 +672,7 @@
         return [mine[0]] + [xor(mine[k], "fsdp", k) for k in range(1, n)]
 
     xs = gather_xor(x_own, "fsdp")
+    xs[1], packed_weight = tie(xs[1], in_weight)
     if own % 128 == 0:
         packets = call(
             functools.partial(packets_kernel, n, own),
@@ -669,7 +680,7 @@
             (1,),
             scal,
             [pl.BlockSpec(in_weight.shape, lambda b, s: (0, 0))],
-            (in_weight,),
+            (packed_weight,),
             [pl.BlockSpec((rows, 2 * own), lambda b, s: (0, 0))] * n
             + [pl.BlockSpec((rows, 2 * N + 128), lambda b, s: (0, 0))],
             [jax.ShapeDtypeStruct((rows, 2 * own), BF)] * n
@@ -688,33 +699,39 @@
 
         own_cols = [jnp.concatenate(both, axis=1) for both in zip(columns(DI), columns(0))]
         shared = jnp.pad(in_weight[:, 2 * DI :], ((0, 0), (0, 128 - H)))
-    small = jnp.concatenate([norm_gain, conv_bias, conv_weight.reshape(-1)])
-    small = jnp.pad(small, (0, -small.shape[0] % 1024)).reshape(-1, 128)
-    shared, small = tie(shared, small)
-    smalls = by_owner([small] + [xor(small, "fsdp", k) for k in range(1, n)], me)
-    flat = jnp.stack(smalls).reshape(n, -1)
     chans = CONVCH // n
-    gain_full = flat[:, :rows].reshape(1, model).astype(F32)
-    conv_full = jnp.concatenate(
-        [
-            flat[:, rows + chans : rows + chans * (1 + KCONV)]
-            .reshape(n, KCONV, chans)
-            .transpose(1, 0, 2)
-            .reshape(KCONV, CONVCH),
-            flat[:, rows : rows + chans].reshape(1, CONVCH),
-        ],
-        axis=0,
-    ).astype(F32)
-    conv_heads = lax.dynamic_slice_in_dim(conv_full, me * own, own, 1)
-    taps = jnp.concatenate(
-        [jnp.pad(conv_heads, ((0, 0), (0, lanes - own))), conv_full[:, DI:]], axis=1
-    )
-    taps = jnp.pad(taps, ((0, 3), (0, 0)))
+    pack = -(-max(rows, chans) // 128) * 128
+    line = lambda value: jnp.pad(value, ((0, 0), (0, pack - value.shape[1])))
+    small = jnp.concatenate(
+        [line(norm_gain[None]), line(conv_bias[None]), line(conv_weight), jnp.zeros((2, pack), BF)]
+    )
+    xs[1], small = tie(xs[1], small)
+    smalls = [small] + [xor(small, "fsdp", k) for k in range(1, n)]
     hp = jnp.stack([step_bias, decay_log]).astype(F32)
     hp = jnp.pad(hp, ((0, 6), (0, 128 - own_heads)))
     skip = jnp.pad(jnp.repeat(skip_gain.astype(F32), PS), (0, lanes - own)).reshape(1, lanes)
 
-    xs[2], *own_cols = tie(xs[2], *own_cols)
+    out_w = jnp.pad(out_weight, ((0, lanes - own), (0, 0)))
+    out_g = jnp.pad(out_gain.astype(F32), (0, lanes - own), constant_values=1.0).reshape(1, lanes)
+    gain_row = norm_gain.astype(F32).reshape(1, rows)
+    hp, skip, out_g, gain_row, scal, xs[2], *rest = tie(
+        hp, skip, out_g, gain_row, scal, xs[2], *smalls[1:], *own_cols
+    )
+    smalls[1:], own_cols = rest[: n - 1], rest[n - 1 :]
+    full = lambda *dims: pl.BlockSpec(dims, lambda b, s: (0,) * len(dims))
+    gain_full, taps = call(
+        functools.partial(params_kernel, n, own_heads),
+        "params",
+        (1,),
+        scal,
+        [full(8, pack)] * n,
+        smalls,
+        [full(1, model), full(8, width)],
+        [jax.ShapeDtypeStruct((1, model), F32), jax.ShapeDtypeStruct((8, width), F32)],
+        [pltpu.VMEM((8, CONVCH), F32)],
+        10**6,
+        10**5,
+    )
     xs[3] = xor(xs[2], "fsdp", 1)
     wks = gather_xor(shared, "fsdp")
     ws = exchange(own_cols)
@@ -730,7 +747,7 @@
         return pl.BlockSpec((BLOCK, cols), lambda b, s: (b, 0))
 
     shape = jax.ShapeDtypeStruct
-    normed, normed_t, conv_in, convk_in, raw_step, mixer, starts = call(
+    normed, normed_t, conv_in, convk_in, raw_step, mixer, starts, w_conv, w_gate = call(
         functools.partial(forward_kernel, n, heads, own_heads),
         "forward",
         (nb,),
@@ -745,6 +762,8 @@
             tokens(128),
             tokens(lanes),
             pl.BlockSpec((1, lanes, N), lambda b, s: (b, 0, 0)),
+            any_spec,
+            any_spec,
         ],
         [
             shape((length, model), BF),
@@ -754,15 +773,19 @@
             shape((length, 128), F32),
             shape((length, lanes), F32),
             shape((nb, lanes, N), F32),
+            shape((model, width + 128), BF),
+            shape((model, lanes), BF),
         ],
         [
             pltpu.VMEM((length, model), BF),
             pltpu.VMEM((model, width + 128), BF),
             pltpu.VMEM((8 + BLOCK, width), F32),
             pltpu.VMEM((lanes, N), F32),
+            pltpu.SemaphoreType.DMA,
             pltpu.SemaphoreType.DMA((n,)),
             pltpu.SemaphoreType.DMA((n,)),
             pltpu.SemaphoreType.DMA((n,)),
+            pltpu.SemaphoreType.DMA((n,)),
         ],
         9 * 10**9,
         10**7,
@@ -770,26 +793,21 @@
 
     gs[2], normed = tie(gs[2], normed)
     gs[3::2] = [xor(value, "fsdp", 1) for value in gs[2::2]]
-    out_w = jnp.pad(out_weight, ((0, lanes - own), (0, 0)))
-    out_g = jnp.pad(out_gain.astype(F32), (0, lanes - own)).reshape(1, lanes)
-    raw_gate, gno, stat = call(
+    raw_gate, stat = call(
         functools.partial(gate_kernel, n),
         "gate",
         (nb,),
         scal,
-        [any_spec] * (2 * n)
-        + [tokens(model), tokens(lanes), whole(lanes, model), whole(1, lanes)],
-        (*gs, *ws, normed, mixer, out_w, out_g),
-        [tokens(lanes), tokens(lanes), pl.BlockSpec((8, BLOCK), lambda b, s: (0, b))],
+        [any_spec] * n
+        + [whole(model, lanes), tokens(model), tokens(lanes), whole(lanes, model), whole(1, lanes)],
+        (*gs, w_gate, normed, mixer, out_w, out_g),
+        [tokens(lanes), pl.BlockSpec((8, BLOCK), lambda b, s: (0, b))],
         [
             shape((length, lanes), BF),
-            shape((length, lanes), F32),
             shape((8, length), F32),
         ],
         [
             pltpu.VMEM((length, model), BF),
-            pltpu.VMEM((model, lanes), BF),
-            pltpu.SemaphoreType.DMA((n,)),
             pltpu.SemaphoreType.DMA((n,)),
         ],
         2 * 10**9,
@@ -807,9 +825,9 @@
         [any_spec] * n
         + [pl.BlockSpec((8, BLOCK), lambda b, s: (0, b))] * n
         + [pl.BlockSpec((model, BLOCK), lambda b, s: (0, b))]
-        + [tokens(lanes), tokens(lanes), tokens(lanes)]
+        + [tokens(lanes), tokens(lanes)]
         + [whole(lanes, model), whole(1, lanes)],
-        (*gs, *stats, normed_t, mixer, raw_gate, gno, out_w, out_g),
+        (*gs, *stats, normed_t, mixer, raw_gate, out_w, out_g),
         [
             pl.BlockSpec((1, BLOCK, model), lambda b, s: (b ^ s[0], 0, 0)),
             tokens(lanes),
@@ -935,21 +953,15 @@
         bits = [1 << bit for bit in range(ndp.bit_length() - 1)]
         small_grads = small_grads + xor(small_grads, "dp", bits[0])
     (gn_part,) = call(
-        functools.partial(normed_kernel, n, lanes),
+        normed_kernel,
         "normed_grad",
         (nb,),
         scal,
-        [any_spec] * (2 * n) + [tokens(width + 128), tokens(lanes)],
-        (*ws, *wks, proj_low, ggr),
+        [tokens(width + 128), tokens(lanes), whole(model, width + 128), whole(model, lanes)],
+        (proj_low, ggr, w_conv, w_gate),
         [pl.BlockSpec((1, BLOCK, model), lambda b, s: (b ^ s[0], 0, 0))],
         [shape((nb, BLOCK, model), BF)],
-        [
-            pltpu.VMEM((model, width + 128), BF),
-            pltpu.VMEM((model, lanes), BF),
-            pltpu.SemaphoreType.DMA((n,)),
-            pltpu.SemaphoreType.DMA((n,)),
-            pltpu.SemaphoreType.DMA((n,)),
-        ],
+        [],
         5 * 10**9,
         10**7,
     )
@@ -962,7 +974,9 @@
         for low in late.low[1:]:
             late.reduce(low)
         gn_mine, gn_recv = chip_exchange(core_sum(gn_part))
-        late.value, wo, small_grads, *gn_recv = tie(late.value, wo, small_grads, *gn_recv)
+        hops = bits[1:][::-1]
+        wo = pair_step(wo[None], hops[0])
+        late.value, wo, small_grads = tie(late.value, wo, small_grads)
         owned = to_owners(
             [
                 jnp.concatenate(
@@ -975,19 +989,20 @@
                 for k in range(n)
             ]
         )
-        wo = wo[None]
-        for hop in bits[1:][::-1]:
+        for hop in hops[1:]:
             wo = pair_step(wo, hop)
-            small_grads = small_grads + xor(small_grads, "dp", hop)
+        small_grads = small_grads + xor(small_grads, "dp", hops[0])
         late = late_rows(owned)
         late, wo, small_grads = tie(late, wo, small_grads)
         gather = list(reversed(stages(ndp)))
         late = gather_step(late[None], *gather[0])
         wo = pair_step(wo, bits[0])
-        small_other = xor(small_grads, "fsdp", 1)
-        late, wo, small_other, out_sum = tie(late, wo, small_other, out_sum)
+        for hop in hops[1:]:
+            small_grads = small_grads + xor(small_grads, "dp", hop)
+        late, wo, small_grads, out_sum, *gn_recv = tie(late, wo, small_grads, out_sum, *gn_recv)
         for low, take in gather[1:]:
             late = gather_step(late, low, take)
+        small_other = xor(small_grads, "fsdp", 1)
         small_parts = [small_grads, small_other]
         for k in range(2, n, 2):
             pair = xor(jnp.concatenate([small_grads, small_other], axis=1), "fsdp", k)
@@ -1042,21 +1057,20 @@
             whole(*in_weight.shape),
             whole(1, rows),
         ],
-        (late, step_cols, in_weight, norm_gain.astype(F32).reshape(1, rows)),
+        (late, step_cols, in_weight, gain_row),
         [whole(*in_weight.shape), whole(8, rows)],
         [shape(in_weight.shape, F32), shape((8, rows), F32)],
         [],
         10**8,
         6 * 10**6,
     )
-    gain_ones = jnp.pad(out_gain.astype(F32), (0, lanes - own), constant_values=1.0)
     grad_out, grad_out_gain = call(
         functools.partial(out_weight_kernel, pair_order(ndp) if nd > 1 else [0]),
         "out_weight_grad",
         (1,),
         scal,
         [whole(*wo.shape), whole(lanes, model), whole(1, lanes)],
-        (wo, out_w, gain_ones.reshape(1, lanes)),
+        (wo, out_w, out_g),
         [whole(lanes, model), whole(8, lanes)],
         [shape((lanes, model), F32), shape((8, lanes), F32)],
         [],

time: 182 us -> 177 us (0.973)
  local copies, waits for them, and re-layouts: 16 us -> 10.6 us
  starting transfers between devices: 42.6 us -> 45.1 us
  waiting for transfers between devices: 58.8 us -> 56.4 us
  other arithmetic: 7.1 us -> 9 us
    unnamed x45 -> x18, local copies, waits for them, and re-layouts: 7.4 us -> 3.59 us
    ppermute x45, starting transfers between devices: 42.6 us -> 45.1 us  [xor(): lax.ppermute(value, axis, [(s, s ^ k) for s in range(lax.axis_size(axis))])]
    ppermute x45, waiting for transfers between devices: 58.8 us -> 56.4 us  [xor(): lax.ppermute(value, axis, [(s, s ^ k) for s in range(lax.axis_size(axis))])]
    pallas_call x9 -> x10, Pallas kernels: 55.6 us -> 54.4 us  [call(): pl.pallas_call(kernel, grid_spec=pltpu.PrefetchScalarGridSpec(num_scalar_...]
  transfers between devices with their start and end apart: 45 -> 45, of which waited for: 18 -> 16; matrix products, arithmetic and copies ran while one was open for 7% -> 8% of each run, Pallas kernels for 22% -> 22%
where the time goes in v3:
time: 177 us
  waiting for transfers between devices  56.4 us (32%)
  Pallas kernels  54.4 us (31%)
  starting transfers between devices  45.1 us (25%)
  local copies, waits for them, and re-layouts  10.6 us (6%)
  other arithmetic  9 us (5%)
    ppermute x45, waiting for transfers between devices, xor(): lax.ppermute(value, axis, [(s, s ^ k) for s in range(lax.axis_size(axis))])  56.4 us
    pallas_call x10, Pallas kernels, call(): pl.pallas_call(kernel, grid_spec=pltpu.PrefetchScalarGridSpec(num_scalar_...  54.4 us
    ppermute x45, starting transfers between devices, xor(): lax.ppermute(value, axis, [(s, s ^ k) for s in range(lax.axis_size(axis))])  45.1 us
    unnamed x18, local copies, waits for them, and re-layouts  3.59 us
  transfers between devices with their start and end apart: 45, of which 16 were waited for; matrix products, arithmetic and copies ran while one was open for 8% of the time, Pallas kernels for 22%

profile of v3, /device:TPU:0, one launch (start us, length us, event | category | flops | bytes accessed | tf_op | source)
XLA Modules:
  0.0 176.6 jit_solution(3562113197441711574)
XLA Ops:
  1.2 2.6 %collective-permute-start = (bf16[256,768]{1,0:T(8,128)(2,1)}, bf16[256,768]{1,0:T(8,128)(2,1)S(1)}, u32[]{:S(2)}, u32[]{:S(2)}) collective-permute-start(bf16[256,768]{1,0:T(8,128)(2,1)} %bitcast.119), channel_id=1, source_target_pairs={{0,16},{8,24},{16,0},{24,8},{1,17},{9,25},{17,1},{25,9},{2,18},{10... | collective-permute-start | bytes 1179656 | tf_op jit(solution)/shard_map/ppermute | solution.py:549
  3.7 0.8 reduce-window.4
  4.6 0.7 fusion.38.refs_14_.refs_9_
  5.2 0.7 reshape_convert_fusion.refs_3_
  5.9 0.7 reshape.88
  6.6 0.7 broadcast_in_dim.25
  7.3 0.8 fusion.30.refs_0_
  8.5 1.4 collective-permute-start.4
  10.0 0.7 broadcast_in_dim.24
  10.8 0.7 reshape.96.refs_8_.refs_12_.gain
  11.5 1.3 copy-done
  12.8 0.7 packets.1
  14.4 1.8 collective-permute-start.7
  16.2 1.5 collective-permute-start.10
  17.6 15.3 %collective-permute-done.10.refs_10_ = bf16[192,384]{1,0:T(8,128)(2,1)S(1)} collective-permute-done((bf16[192,384]{1,0:T(8,128)(2,1)S(1)}, bf16[192,384]{1,0:T(8,128)(2,1)S(1)}, u32[]{:S(2)}, u32[]{:S(2)}) %collective-permute-start.10) | collective-permute-done | bytes 147488 | tf_op jit(solution)/shard_map/ppermute | solution.py:549
  33.5 0.6 params.1
  34.1 1.8 %collective-permute-start.13 = (bf16[256,768]{1,0:T(8,128)(2,1)}, bf16[256,768]{1,0:T(8,128)(2,1)S(1)}, u32[]{:S(2)}, u32[]{:S(2)}) collective-permute-start(bf16[256,768]{1,0:T(8,128)(2,1)} %bitcast.124), channel_id=1, source_target_pairs={{0,16},{8,24},{16,0},{24,8},{1,17},{9,25},{17,1},{25,9},{2,18},{10... | collective-permute-start | bytes 1179656 | tf_op jit(solution)/shard_map/ppermute | solution.py:549
  36.0 1.0 copy-done.2
  37.0 12.0 %forward.1 = (bf16[1024,768]{1,0:T(8,128)(2,1)S(1)}, bf16[768,1024]{1,0:T(8,128)(2,1)S(1)}, bf16[1024,384]{1,0:T(8,128)(2,1)S(1)}, bf16[1024,256]{1,0:T(8,128)(2...) custom-call(s32[5]{0:T(128)S(1)} %pad_add_fusion.scal, ...), custom_call_target="tpu_custom_call" | custom-call | flops 8999999488 | bytes 10000000 | tf_op jit(solution)/shard_map/forward/pallas_call | solution.py:624
  49.0 0.6 collective-permute-start.14
  49.6 1.3 collective-permute-done.14.refs_3_
  50.9 5.1 %gate.1 = (bf16[1024,384]{1,0:T(8,128)(2,1)S(1)}, f32[8,1024]{1,0:T(8,128)S(1)}) custom-call(s32[5]{0:T(128)S(1)} %pad_add_fusion.scal, bf16[256,768]{1,0:T(8,128)(2,1)S(1)} %bitcast.126, bf16[256,768]{1,0:T(8,128)(2,1)S(1)} %collective-permute-done.12.refs_1_, bf16[256,768]{1,0:T(8,128)(2,1)S(1)} %collective-permute-done.13.refs_2_, ...), custom_call_target="tpu_custom_call" | custom-call | flops 2000000000 | bytes 10000000 | tf_op jit(solution)/shard_map/gate/pallas_call | solution.py:624
  56.8 1.2 collective-permute-start.17
  58.0 2.5 %collective-permute-done.16.refs_6_ = f32[8,1024]{1,0:T(8,128)S(1)} collective-permute-done((f32[8,1024]{1,0:T(8,128)S(1)}, f32[8,1024]{1,0:T(8,128)S(1)}, u32[]{:S(2)}, u32[]{:S(2)}) %collective-permute-start.16) | collective-permute-done | bytes 32800 | tf_op jit(solution)/shard_map/ppermute | solution.py:549
  60.5 8.2 %output.1 = (bf16[4,256,768]{2,1,0:T(8,128)(2,1)S(1)}, bf16[1024,384]{1,0:T(8,128)(2,1)S(1)}, bf16[1024,384]{1,0:T(8,128)(2,1)S(1)}, bf16[8,96,768]{2,1,0:T(8,128)(2,1)S(1)}) custom-call(s32[5]{0:T(128)S(1)} %pad_add_fusion.scal, bf16[256,768]{1,0:T(8,128)(2,1)S(1)} %bitcast.127, bf16[256,768]{1,0:T(8,128)(2,1)S(1)} %collective-permute-done.12.refs_1_, ...), custom_call_target="tpu_custom_call" | custom-call | flops 3000000000 | bytes 10000000 | tf_op jit(solution)/shard_map/output/pallas_call | solution.py:624
  69.1 1.8 %collective-permute-start.18 = (bf16[4,96,768]{2,1,0:T(8,128)(2,1)S(1)}, bf16[4,96,768]{2,1,0:T(8,128)(2,1)S(1)}, u32[]{:S(2)}, u32[]{:S(2)}) collective-permute-start(bf16[4,96,768]{2,1,0:T(8,128)(2,1)S(1)} %slice_bitcast_fusion.4), channel_id=1, source_target_pairs={{0,1},{1,0},{2,3},{3,2},{4,5},{5,4},{6,7},{7,6},{8,9},{9,8},{10,11... | collective-permute-start | bytes 1769480 | tf_op jit(solution)/shard_map/ppermute | solution.py:549
  70.9 19.2 %scan_back.1 = (bf16[1024,768]{1,0:T(8,128)(2,1)S(1)}, bf16[4,8,24,640]{3,2,1,0:T(8,128)(2,1)S(1)}, f32[8,1536]{1,0:T(8,128)S(1)}) custom-call(s32[5]{0:T(128)S(1)} %pad_add_fusion.scal, bf16[768,1024]{1,0:T(8,128)(2,1)S(1)} %get-tuple-element.105.refs_8_.refs_0_, bf16[1024,384]{1,0:T(8,128)(2,1)S(1)} %get-tuple-element.106.refs_1_.refs_2_, ...), custom_call_target="tpu_custom_call" | custom-call | flops 20000000000 | bytes 10000000 | tf_op jit(solution)/shard_map/scan_back/pallas_call | solution.py:624
  90.8 1.9 %collective-permute-start.21 = (bf16[96,768]{1,0:T(8,128)(2,1)S(1)}, bf16[96,768]{1,0:T(8,128)(2,1)S(1)}, u32[]{:S(2)}, u32[]{:S(2)}) collective-permute-start(bf16[96,768]{1,0:T(8,128)(2,1)S(1)} %get-tuple-element.159), channel_id=1, source_target_pairs={{0,2},{1,3},{2,0},{3,1},{4,6},{5,7},{6,4},{7,5},{8,10},{9,11},{10,... | collective-permute-start | bytes 442376 | tf_op jit(solution)/shard_map/ppermute | solution.py:549
  92.7 2.6 %collective-permute-start.22 = (bf16[96,768]{1,0:T(8,128)(2,1)S(1)}, bf16[96,768]{1,0:T(8,128)(2,1)S(1)}, u32[]{:S(2)}, u32[]{:S(2)}) collective-permute-start(bf16[96,768]{1,0:T(8,128)(2,1)S(1)} %get-tuple-element.161), channel_id=1, source_target_pairs={{0,4},{1,5},{2,6},{3,7},{4,0},{5,1},{6,2},{7,3},{8,12},{9,13},{10,... | collective-permute-start | bytes 442376 | tf_op jit(solution)/shard_map/ppermute | solution.py:549
  95.4 1.8 %collective-permute-start.20 = (bf16[4,4,24,640]{3,2,0,1:T(8,128)(2,1)S(1)}, bf16[4,4,24,640]{3,2,0,1:T(8,128)(2,1)S(1)}, u32[]{:S(2)}, u32[]{:S(2)}) collective-permute-start(bf16[4,4,24,640]{3,2,0,1:T(8,128)(2,1)S(1)} %bitcast.128), channel_id=1, source_target_pairs={{0,1},{1,0},{2,3},{3,2},{4,5},{5,4},{6,7},{7,6},{8,9},{9,8},{10,11... | collective-permute-start | bytes 1474568 | tf_op jit(solution)/shard_map/ppermute | solution.py:549
  97.2 3.3 %normed_grad.1 = bf16[4,256,768]{2,1,0:T(8,128)(2,1)S(1)} custom-call(s32[5]{0:T(128)S(1)} %pad_add_fusion.scal, bf16[1024,768]{1,0:T(8,128)(2,1)S(1)} %get-tuple-element.125.proj, bf16[1024,384]{1,0:T(8,128)(2,1)S(1)} %get-tuple-element.126.ggr, bf16[768,768]{1,0:T(8,128)(2,1)S(1)} %get-tuple-element.127.wv, bf16[768,384]{1,0:T(8,128)(2,1)S(1)} %get-tuple-element.113.refs_4_.wgv), custom_call_target="tpu_custom_call" | custom-call | flops 5000000000 | bytes 10000000 | tf_op jit(solution)/shard_map/normed_grad/pallas_call | solution.py:624
  100.6 6.1 %collective-permute-done.22 = bf16[96,768]{1,0:T(8,128)(2,1)S(1)} collective-permute-done((bf16[96,768]{1,0:T(8,128)(2,1)S(1)}, bf16[96,768]{1,0:T(8,128)(2,1)S(1)}, u32[]{:S(2)}, u32[]{:S(2)}) %collective-permute-start.22) | collective-permute-done | bytes 147488 | tf_op jit(solution)/shard_map/ppermute | solution.py:549
  106.8 1.1 collective-permute-done.20
  108.0 0.9 slice_bitcast_fusion
  108.9 2.2 %collective-permute-start.28 = (bf16[1,48,768]{2,1,0:T(8,128)(2,1)S(1)}, bf16[1,48,768]{2,1,0:T(8,128)(2,1)S(1)}, u32[]{:S(2)}, u32[]{:S(2)}) collective-permute-start(bf16[1,48,768]{2,1,0:T(8,128)(2,1)S(1)} %slice_bitcast_fusion.15), channel_id=1, source_target_pairs={{0,4},{1,5},{2,6},{3,7},{4,0},{5,1},{6,2},{7,3},{8,12},{9,13},{10,... | collective-permute-start | bytes 221192 | tf_op jit(solution)/shard_map/ppermute | solution.py:549
  111.1 2.0 %collective-permute-start.25 = (bf16[4,24,640]{2,1,0:T(8,128)(2,1)S(1)}, bf16[4,24,640]{2,1,0:T(8,128)(2,1)S(1)}, u32[]{:S(2)}, u32[]{:S(2)}) collective-permute-start(bf16[4,24,640]{2,1,0:T(8,128)(2,1)S(1)} %get-tuple-element.162), channel_id=1, source_target_pairs={{0,2},{1,3},{2,0},{3,1},{4,6},{5,7},{6,4},{7,5},{8,10},{9,11},{10,... | collective-permute-start | bytes 368648 | tf_op jit(solution)/shard_map/ppermute | solution.py:549
  113.1 2.5 %collective-permute-start.27 = (bf16[4,24,640]{2,1,0:T(8,128)(2,1)S(1)}, bf16[4,24,640]{2,1,0:T(8,128)(2,1)S(1)}, u32[]{:S(2)}, u32[]{:S(2)}) collective-permute-start(bf16[4,24,640]{2,1,0:T(8,128)(2,1)S(1)} %get-tuple-element.163), channel_id=1, source_target_pairs={{0,6},{1,7},{2,4},{3,5},{4,2},{5,3},{6,0},{7,1},{8,14},{9,15},{10,... | collective-permute-start | bytes 368648 | tf_op jit(solution)/shard_map/ppermute | solution.py:549
  115.8 1.1 collective-permute-done.25
  116.9 7.1 %collective-permute-done.26 = bf16[4,24,640]{2,1,0:T(8,128)(2,1)S(1)} collective-permute-done((bf16[4,24,640]{2,1,0:T(8,128)(2,1)S(1)}, bf16[4,24,640]{2,1,0:T(8,128)(2,1)S(1)}, u32[]{:S(2)}, u32[]{:S(2)}) %collective-permute-start.26) | collective-permute-done | bytes 122912 | tf_op jit(solution)/shard_map/ppermute | solution.py:549
  124.0 2.9 %collective-permute-start.33 = (f32[8,1536]{1,0:T(8,128)S(1)}, f32[8,1536]{1,0:T(8,128)S(1)}, u32[]{:S(2)}, u32[]{:S(2)}) collective-permute-start(f32[8,1536]{1,0:T(8,128)S(1)} %add.85), channel_id=1, source_target_pairs={{0,4},{1,5},{2,6},{3,7},{4,0},{5,1},{6,2},{7,3},{8,12},{9,13},{10,... | collective-permute-start | bytes 147464 | tf_op jit(solution)/shard_map/ppermute | solution.py:549
  127.2 1.7 collective-permute-start.29
  128.9 0.9 collective-permute-done.29
  130.2 3.6 %collective-permute-done.30 = bf16[24,1024]{1,0:T(8,128)(2,1)S(1)} collective-permute-done((bf16[24,1024]{1,0:T(8,128)(2,1)S(1)}, bf16[24,1024]{1,0:T(8,128)(2,1)S(1)}, u32[]{:S(2)}, u32[]{:S(2)}) %collective-permute-start.30) | collective-permute-done | bytes 49184 | tf_op jit(solution)/shard_map/ppermute | solution.py:549
  133.8 0.6 add.92
  134.5 0.7 pad_maximum_fusion.3
  135.2 1.9 %collective-permute-start.38 = (f32[8,1536]{1,0:T(8,128)}, f32[8,1536]{1,0:T(8,128)}, u32[]{:S(2)}, u32[]{:S(2)}) collective-permute-start(f32[8,1536]{1,0:T(8,128)} %add.92), channel_id=1, source_target_pairs={{0,2},{1,3},{2,0},{3,1},{4,6},{5,7},{6,4},{7,5},{8,10},{9,11},{10,... | collective-permute-start | bytes 147464 | tf_op jit(solution)/shard_map/ppermute | solution.py:549
  137.4 2.0 %collective-permute-start.35 = (bf16[1,24,3328]{2,1,0:T(8,128)(2,1)S(1)}, bf16[1,24,3328]{2,1,0:T(8,128)(2,1)S(1)}, u32[]{:S(2)}, u32[]{:S(2)}) collective-permute-start(bf16[1,24,3328]{2,1,0:T(8,128)(2,1)S(1)} %bitcast.130), channel_id=1, source_target_pairs={{0,4},{1,5},{2,6},{3,7},{4,0},{5,1},{6,2},{7,3},{8,12},{9,13},{10,... | collective-permute-start | bytes 479240 | tf_op jit(solution)/shard_map/ppermute | solution.py:549
  139.3 2.3 %collective-permute-start.36 = (bf16[1,24,3328]{2,1,0:T(8,128)(2,1)S(1)}, bf16[1,24,3328]{2,1,0:T(8,128)(2,1)S(1)}, u32[]{:S(2)}, u32[]{:S(2)}) collective-permute-start(bf16[1,24,3328]{2,1,0:T(8,128)(2,1)S(1)} %bitcast.131), channel_id=1, source_target_pairs={{0,6},{1,7},{2,4},{3,5},{4,2},{5,3},{6,0},{7,1},{8,14},{9,15},{10,... | collective-permute-start | bytes 479240 | tf_op jit(solution)/shard_map/ppermute | solution.py:549
  141.9 1.4 collective-permute-start.37
  143.3 0.8 add.93.refs_0_
  144.2 1.3 fusion
  146.1 5.6 %collective-permute-done.35 = bf16[1,24,3328]{2,1,0:T(8,128)(2,1)S(1)} collective-permute-done((bf16[1,24,3328]{2,1,0:T(8,128)(2,1)S(1)}, bf16[1,24,3328]{2,1,0:T(8,128)(2,1)S(1)}, u32[]{:S(2)}, u32[]{:S(2)}) %collective-permute-start.35) | collective-permute-done | bytes 159776 | tf_op jit(solution)/shard_map/ppermute | solution.py:549
  151.9 2.2 %collective-permute-done.40 = bf16[256,768]{1,0:T(8,128)(2,1)S(1)} collective-permute-done((bf16[256,768]{1,0:T(8,128)(2,1)S(1)}, bf16[256,768]{1,0:T(8,128)(2,1)S(1)}, u32[]{:S(2)}, u32[]{:S(2)}) %collective-permute-start.40) | collective-permute-done | bytes 393248 | tf_op jit(solution)/shard_map/ppermute | solution.py:549
  154.1 0.6 collective-permute-start.42
  155.6 1.6 out_weight_grad.1
  157.2 1.7 collective-permute-start.44
  158.9 0.6 slice_reduce_fusion
  159.5 8.7 %collective-permute-done.44 = f32[8,3072]{1,0:T(8,128)S(1)} collective-permute-done((f32[8,3072]{1,0:T(8,128)S(1)}, f32[8,3072]{1,0:T(8,128)S(1)}, u32[]{:S(2)}, u32[]{:S(2)}) %collective-permute-start.44) | collective-permute-done | bytes 98336 | tf_op jit(solution)/shard_map/ppermute | solution.py:549
  168.2 0.7 small_grads.1
  168.8 0.6 slice.199
  169.4 0.6 slice.200
  170.5 1.3 fusion.14
  171.9 1.2 copy-done.1
  173.1 2.9 %in_weight_grad.1 = (f32[192,3352]{1,0:T(8,128)}, f32[8,192]{1,0:T(8,128)S(1)}) custom-call(s32[5]{0:T(128)S(1)} %pad_add_fusion.scal, bf16[8,24,3328]{2,1,0:T(8,128)(2,1)S(1)} %pad_maximum_fusion.refs_0_, f32[192,128]{1,0:T(8,128)S(1)} %get-tuple-element.146.refs_1_, bf16[192,3352]{1,0:T(8,128)(2,1)S(1)} %copy-done.1, f32[1,192]{1,0:T(1,128)S(1)} %reshape_convert_fusion.refs_3_), custom_call_target="tpu_custom_call" | custom-call | flops 100000000 | bytes 6000000 | tf_op jit(solution)/shard_map/in_weight_grad/pallas_call | solution.py:624
  (108 shorter events, 9.1 us)
Async XLA Ops:
  0.6 7.4 %collective-permute-start.1 = (bf16[256,768]{1,0:T(8,128)(2,1)}, bf16[256,768]{1,0:T(8,128)(2,1)S(1)}, u32[]{:S(2)}, u32[]{:S(2)}) collective-permute-start(bf16[256,768]{1,0:T(8,128)(2,1)} %bitcast.118), channel_id=1, source_target_pairs={{0,8},{8,0},{16,24},{24,16},{1,9},{9,1},{17,25},{25,17},{2,10},{10... | collective-permute-start | bytes 1179656 | tf_op jit(solution)/shard_map/ppermute | solution.py:549
  1.2 12.7 %collective-permute-start = (bf16[256,768]{1,0:T(8,128)(2,1)}, bf16[256,768]{1,0:T(8,128)(2,1)S(1)}, u32[]{:S(2)}, u32[]{:S(2)}) collective-permute-start(bf16[256,768]{1,0:T(8,128)(2,1)} %bitcast.119), channel_id=1, source_target_pairs={{0,16},{8,24},{16,0},{24,8},{1,17},{9,25},{17,1},{25,9},{2,18},{10... | collective-permute-start | bytes 1179656 | tf_op jit(solution)/shard_map/ppermute | solution.py:549
  8.1 5.7 %collective-permute-start.2 = (bf16[8,512]{1,0:T(8,128)(2,1)S(1)}, bf16[8,512]{1,0:T(8,128)(2,1)S(1)}, u32[]{:S(2)}, u32[]{:S(2)}) collective-permute-start(bf16[8,512]{1,0:T(8,128)(2,1)S(1)} %fusion.30.refs_0_), channel_id=1, source_target_pairs={{0,8},{8,0},{16,24},{24,16},{1,9},{9,1},{17,25},{25,17},{2,10},{10... | collective-permute-start | bytes 24584 | tf_op jit(solution)/shard_map/ppermute | solution.py:549
  8.3 5.6 %collective-permute-start.3 = (bf16[8,512]{1,0:T(8,128)(2,1)S(1)}, bf16[8,512]{1,0:T(8,128)(2,1)S(1)}, u32[]{:S(2)}, u32[]{:S(2)}) collective-permute-start(bf16[8,512]{1,0:T(8,128)(2,1)S(1)} %fusion.30.refs_0_), channel_id=1, source_target_pairs={{0,16},{8,24},{16,0},{24,8},{1,17},{9,25},{17,1},{25,9},{2,18},{10... | collective-permute-start | bytes 24584 | tf_op jit(solution)/shard_map/ppermute | solution.py:549
  8.5 5.4 %collective-permute-start.4 = (bf16[8,512]{1,0:T(8,128)(2,1)S(1)}, bf16[8,512]{1,0:T(8,128)(2,1)S(1)}, u32[]{:S(2)}, u32[]{:S(2)}) collective-permute-start(bf16[8,512]{1,0:T(8,128)(2,1)S(1)} %fusion.30.refs_0_), channel_id=1, source_target_pairs={{0,24},{8,16},{16,8},{24,0},{1,25},{9,17},{17,9},{25,1},{2,26},{10... | collective-permute-start | bytes 24584 | tf_op jit(solution)/shard_map/ppermute | solution.py:549
  11.5 1.3 copy-start
  13.9 19.1 %collective-permute-start.6 = (bf16[192,768]{1,0:T(8,128)(2,1)S(1)}, bf16[192,768]{1,0:T(8,128)(2,1)S(1)}, u32[]{:S(2)}, u32[]{:S(2)}) collective-permute-start(bf16[192,768]{1,0:T(8,128)(2,1)S(1)} %get-tuple-element.94), channel_id=1, source_target_pairs={{0,8},{8,0},{16,24},{24,16},{1,9},{9,1},{17,25},{25,17},{2,10},{10... | collective-permute-start | bytes 884744 | tf_op jit(solution)/shard_map/ppermute | solution.py:549
  14.1 21.9 %collective-permute-start.5 = (bf16[256,768]{1,0:T(8,128)(2,1)S(1)}, bf16[256,768]{1,0:T(8,128)(2,1)S(1)}, u32[]{:S(2)}, u32[]{:S(2)}) collective-permute-start(bf16[256,768]{1,0:T(8,128)(2,1)S(1)} %collective-permute-done.refs_2_), channel_id=1, source_target_pairs={{0,8},{8,0},{16,24},{24,16},{1,9},{9,1},{17,25},{25,17},{2,10},{10... | collective-permute-start | bytes 1179656 | tf_op jit(solution)/shard_map/ppermute | solution.py:549
  14.4 19.7 %collective-permute-start.7 = (bf16[192,768]{1,0:T(8,128)(2,1)S(1)}, bf16[192,768]{1,0:T(8,128)(2,1)S(1)}, u32[]{:S(2)}, u32[]{:S(2)}) collective-permute-start(bf16[192,768]{1,0:T(8,128)(2,1)S(1)} %get-tuple-element.95), channel_id=1, source_target_pairs={{0,16},{8,24},{16,0},{24,8},{1,17},{9,25},{17,1},{25,9},{2,18},{10... | collective-permute-start | bytes 884744 | tf_op jit(solution)/shard_map/ppermute | solution.py:549
  16.2 18.0 %collective-permute-start.8 = (bf16[192,768]{1,0:T(8,128)(2,1)S(1)}, bf16[192,768]{1,0:T(8,128)(2,1)S(1)}, u32[]{:S(2)}, u32[]{:S(2)}) collective-permute-start(bf16[192,768]{1,0:T(8,128)(2,1)S(1)} %get-tuple-element.96), channel_id=1, source_target_pairs={{0,24},{8,16},{16,8},{24,0},{1,25},{9,17},{17,9},{25,1},{2,26},{10... | collective-permute-start | bytes 884744 | tf_op jit(solution)/shard_map/ppermute | solution.py:549
  16.2 16.8 %collective-permute-start.10 = (bf16[192,384]{1,0:T(8,128)(2,1)S(1)}, bf16[192,384]{1,0:T(8,128)(2,1)S(1)}, u32[]{:S(2)}, u32[]{:S(2)}) collective-permute-start(bf16[192,384]{1,0:T(8,128)(2,1)S(1)} %get-tuple-element.97.refs_8_), channel_id=1, source_target_pairs={{0,16},{8,24},{16,0},{24,8},{1,17},{9,25},{17,1},{25,9},{2,18},{10... | collective-permute-start | bytes 442376 | tf_op jit(solution)/shard_map/ppermute | solution.py:549
  33.0 2.9 %collective-permute-start.9 = (bf16[192,384]{1,0:T(8,128)(2,1)S(1)}, bf16[192,384]{1,0:T(8,128)(2,1)S(1)}, u32[]{:S(2)}, u32[]{:S(2)}) collective-permute-start(bf16[192,384]{1,0:T(8,128)(2,1)S(1)} %get-tuple-element.97.refs_8_), channel_id=1, source_target_pairs={{0,8},{8,0},{16,24},{24,16},{1,9},{9,1},{17,25},{25,17},{2,10},{10... | collective-permute-start | bytes 442376 | tf_op jit(solution)/shard_map/ppermute | solution.py:549
  33.0 2.9 %collective-permute-start.11 = (bf16[192,384]{1,0:T(8,128)(2,1)S(1)}, bf16[192,384]{1,0:T(8,128)(2,1)S(1)}, u32[]{:S(2)}, u32[]{:S(2)}) collective-permute-start(bf16[192,384]{1,0:T(8,128)(2,1)S(1)} %collective-permute-done.10.refs_10_), channel_id=1, source_target_pairs={{0,8},{8,0},{16,24},{24,16},{1,9},{9,1},{17,25},{25,17},{2,10},{10... | collective-permute-start | bytes 442376 | tf_op jit(solution)/shard_map/ppermute | solution.py:549
  34.1 14.9 %collective-permute-start.13 = (bf16[256,768]{1,0:T(8,128)(2,1)}, bf16[256,768]{1,0:T(8,128)(2,1)S(1)}, u32[]{:S(2)}, u32[]{:S(2)}) collective-permute-start(bf16[256,768]{1,0:T(8,128)(2,1)} %bitcast.124), channel_id=1, source_target_pairs={{0,16},{8,24},{16,0},{24,8},{1,17},{9,25},{17,1},{25,9},{2,18},{10... | collective-permute-start | bytes 1179656 | tf_op jit(solution)/shard_map/ppermute | solution.py:549
  35.9 13.7 %collective-permute-start.12 = (bf16[256,768]{1,0:T(8,128)(2,1)}, bf16[256,768]{1,0:T(8,128)(2,1)S(1)}, u32[]{:S(2)}, u32[]{:S(2)}) collective-permute-start(bf16[256,768]{1,0:T(8,128)(2,1)} %bitcast.125), channel_id=1, source_target_pairs={{0,8},{8,0},{16,24},{24,16},{1,9},{9,1},{17,25},{25,17},{2,10},{10... | collective-permute-start | bytes 1179656 | tf_op jit(solution)/shard_map/ppermute | solution.py:549
  36.0 1.0 copy-start.2
  37.0 14.0 %copy-start.4 = (bf16[384,768]{1,0:T(8,128)(2,1)S(1)}, bf16[384,768]{1,0:T(8,128)(2,1)}, u32[]{:S(2)}) copy-start(bf16[384,768]{1,0:T(8,128)(2,1)} %weight.2) | copy-start | bytes 1769476
  37.0 14.0 %copy-start.5 = (bf16[1,256,768]{2,1,0:T(8,128)(2,1)S(1)}, bf16[1,256,768]{2,1,0:T(8,128)(2,1)}, u32[]{:S(2)}) copy-start(bf16[1,256,768]{2,1,0:T(8,128)(2,1)} %param.13) | copy-start | bytes 1179652
  49.0 1.9 %collective-permute-start.14 = (bf16[256,768]{1,0:T(8,128)(2,1)S(1)}, bf16[256,768]{1,0:T(8,128)(2,1)S(1)}, u32[]{:S(2)}, u32[]{:S(2)}) collective-permute-start(bf16[256,768]{1,0:T(8,128)(2,1)S(1)} %collective-permute-done.13.refs_2_), channel_id=1, source_target_pairs={{0,8},{8,0},{16,24},{24,16},{1,9},{9,1},{17,25},{25,17},{2,10},{10... | collective-permute-start | bytes 1179656 | tf_op jit(solution)/shard_map/ppermute | solution.py:549
  56.1 1.9 %collective-permute-start.15 = (f32[8,1024]{1,0:T(8,128)S(1)}, f32[8,1024]{1,0:T(8,128)S(1)}, u32[]{:S(2)}, u32[]{:S(2)}) collective-permute-start(f32[8,1024]{1,0:T(8,128)S(1)} %get-tuple-element.117.refs_4_), channel_id=1, source_target_pairs={{0,8},{8,0},{16,24},{24,16},{1,9},{9,1},{17,25},{25,17},{2,10},{10... | collective-permute-start | bytes 98312 | tf_op jit(solution)/shard_map/ppermute | solution.py:549
  56.5 4.0 %collective-permute-start.16 = (f32[8,1024]{1,0:T(8,128)S(1)}, f32[8,1024]{1,0:T(8,128)S(1)}, u32[]{:S(2)}, u32[]{:S(2)}) collective-permute-start(f32[8,1024]{1,0:T(8,128)S(1)} %get-tuple-element.117.refs_4_), channel_id=1, source_target_pairs={{0,16},{8,24},{16,0},{24,8},{1,17},{9,25},{17,1},{25,9},{2,18},{10... | collective-permute-start | bytes 98312 | tf_op jit(solution)/shard_map/ppermute | solution.py:549
  56.8 3.7 %collective-permute-start.17 = (f32[8,1024]{1,0:T(8,128)S(1)}, f32[8,1024]{1,0:T(8,128)S(1)}, u32[]{:S(2)}, u32[]{:S(2)}) collective-permute-start(f32[8,1024]{1,0:T(8,128)S(1)} %get-tuple-element.117.refs_4_), channel_id=1, source_target_pairs={{0,24},{8,16},{16,8},{24,0},{1,25},{9,17},{17,9},{25,1},{2,26},{10... | collective-permute-start | bytes 98312 | tf_op jit(solution)/shard_map/ppermute | solution.py:549
  68.8 21.5 %collective-permute-start.19 = (bf16[2,256,768]{2,1,0:T(8,128)(2,1)S(1)}, bf16[2,256,768]{2,1,0:T(8,128)(2,1)S(1)}, u32[]{:S(2)}, u32[]{:S(2)}) collective-permute-start(bf16[2,256,768]{2,1,0:T(8,128)(2,1)S(1)} %slice_bitcast_fusion.2), channel_id=1, source_target_pairs={{0,8},{8,0},{16,24},{24,16},{1,9},{9,1},{17,25},{25,17},{2,10},{10... | collective-permute-start | bytes 2359304 | tf_op jit(solution)/shard_map/ppermute | solution.py:549
  69.1 21.0 %collective-permute-start.18 = (bf16[4,96,768]{2,1,0:T(8,128)(2,1)S(1)}, bf16[4,96,768]{2,1,0:T(8,128)(2,1)S(1)}, u32[]{:S(2)}, u32[]{:S(2)}) collective-permute-start(bf16[4,96,768]{2,1,0:T(8,128)(2,1)S(1)} %slice_bitcast_fusion.4), channel_id=1, source_target_pairs={{0,1},{1,0},{2,3},{3,2},{4,5},{5,4},{6,7},{7,6},{8,9},{9,8},{10,11... | collective-permute-start | bytes 1769480 | tf_op jit(solution)/shard_map/ppermute | solution.py:549
  90.5 10.1 %collective-permute-start.24 = (f32[8,1536]{1,0:T(8,128)S(1)}, f32[8,1536]{1,0:T(8,128)S(1)}, u32[]{:S(2)}, u32[]{:S(2)}) collective-permute-start(f32[8,1536]{1,0:T(8,128)S(1)} %get-tuple-element.130), channel_id=1, source_target_pairs={{0,1},{1,0},{2,3},{3,2},{4,5},{5,4},{6,7},{7,6},{8,9},{9,8},{10,11... | collective-permute-start | bytes 147464 | tf_op jit(solution)/shard_map/ppermute | solution.py:549
  90.8 9.7 %collective-permute-start.21 = (bf16[96,768]{1,0:T(8,128)(2,1)S(1)}, bf16[96,768]{1,0:T(8,128)(2,1)S(1)}, u32[]{:S(2)}, u32[]{:S(2)}) collective-permute-start(bf16[96,768]{1,0:T(8,128)(2,1)S(1)} %get-tuple-element.159), channel_id=1, source_target_pairs={{0,2},{1,3},{2,0},{3,1},{4,6},{5,7},{6,4},{7,5},{8,10},{9,11},{10,... | collective-permute-start | bytes 442376 | tf_op jit(solution)/shard_map/ppermute | solution.py:549
  92.7 14.0 %collective-permute-start.22 = (bf16[96,768]{1,0:T(8,128)(2,1)S(1)}, bf16[96,768]{1,0:T(8,128)(2,1)S(1)}, u32[]{:S(2)}, u32[]{:S(2)}) collective-permute-start(bf16[96,768]{1,0:T(8,128)(2,1)S(1)} %get-tuple-element.161), channel_id=1, source_target_pairs={{0,4},{1,5},{2,6},{3,7},{4,0},{5,1},{6,2},{7,3},{8,12},{9,13},{10,... | collective-permute-start | bytes 442376 | tf_op jit(solution)/shard_map/ppermute | solution.py:549
  95.3 11.4 %collective-permute-start.23 = (bf16[96,768]{1,0:T(8,128)(2,1)S(1)}, bf16[96,768]{1,0:T(8,128)(2,1)S(1)}, u32[]{:S(2)}, u32[]{:S(2)}) collective-permute-start(bf16[96,768]{1,0:T(8,128)(2,1)S(1)} %get-tuple-element.160), channel_id=1, source_target_pairs={{0,6},{1,7},{2,4},{3,5},{4,2},{5,3},{6,0},{7,1},{8,14},{9,15},{10,... | collective-permute-start | bytes 442376 | tf_op jit(solution)/shard_map/ppermute | solution.py:549
  95.4 12.4 %collective-permute-start.20 = (bf16[4,4,24,640]{3,2,0,1:T(8,128)(2,1)S(1)}, bf16[4,4,24,640]{3,2,0,1:T(8,128)(2,1)S(1)}, u32[]{:S(2)}, u32[]{:S(2)}) collective-permute-start(bf16[4,4,24,640]{3,2,0,1:T(8,128)(2,1)S(1)} %bitcast.128), channel_id=1, source_target_pairs={{0,1},{1,0},{2,3},{3,2},{4,5},{5,4},{6,7},{7,6},{8,9},{9,8},{10,11... | collective-permute-start | bytes 1474568 | tf_op jit(solution)/shard_map/ppermute | solution.py:549
  108.9 6.9 %collective-permute-start.28 = (bf16[1,48,768]{2,1,0:T(8,128)(2,1)S(1)}, bf16[1,48,768]{2,1,0:T(8,128)(2,1)S(1)}, u32[]{:S(2)}, u32[]{:S(2)}) collective-permute-start(bf16[1,48,768]{2,1,0:T(8,128)(2,1)S(1)} %slice_bitcast_fusion.15), channel_id=1, source_target_pairs={{0,4},{1,5},{2,6},{3,7},{4,0},{5,1},{6,2},{7,3},{8,12},{9,13},{10,... | collective-permute-start | bytes 221192 | tf_op jit(solution)/shard_map/ppermute | solution.py:549
  111.1 5.7 %collective-permute-start.25 = (bf16[4,24,640]{2,1,0:T(8,128)(2,1)S(1)}, bf16[4,24,640]{2,1,0:T(8,128)(2,1)S(1)}, u32[]{:S(2)}, u32[]{:S(2)}) collective-permute-start(bf16[4,24,640]{2,1,0:T(8,128)(2,1)S(1)} %get-tuple-element.162), channel_id=1, source_target_pairs={{0,2},{1,3},{2,0},{3,1},{4,6},{5,7},{6,4},{7,5},{8,10},{9,11},{10,... | collective-permute-start | bytes 368648 | tf_op jit(solution)/shard_map/ppermute | solution.py:549
  113.1 10.8 %collective-permute-start.26 = (bf16[4,24,640]{2,1,0:T(8,128)(2,1)S(1)}, bf16[4,24,640]{2,1,0:T(8,128)(2,1)S(1)}, u32[]{:S(2)}, u32[]{:S(2)}) collective-permute-start(bf16[4,24,640]{2,1,0:T(8,128)(2,1)S(1)} %get-tuple-element.164), channel_id=1, source_target_pairs={{0,4},{1,5},{2,6},{3,7},{4,0},{5,1},{6,2},{7,3},{8,12},{9,13},{10,... | collective-permute-start | bytes 368648 | tf_op jit(solution)/shard_map/ppermute | solution.py:549
  113.1 10.8 %collective-permute-start.27 = (bf16[4,24,640]{2,1,0:T(8,128)(2,1)S(1)}, bf16[4,24,640]{2,1,0:T(8,128)(2,1)S(1)}, u32[]{:S(2)}, u32[]{:S(2)}) collective-permute-start(bf16[4,24,640]{2,1,0:T(8,128)(2,1)S(1)} %get-tuple-element.163), channel_id=1, source_target_pairs={{0,6},{1,7},{2,4},{3,5},{4,2},{5,3},{6,0},{7,1},{8,14},{9,15},{10,... | collective-permute-start | bytes 368648 | tf_op jit(solution)/shard_map/ppermute | solution.py:549
  115.6 28.6 %collective-permute-start.39 = (bf16[2,256,768]{2,1,0:T(8,128)(2,1)}, bf16[2,256,768]{2,1,0:T(8,128)(2,1)}, u32[]{:S(2)}, u32[]{:S(2)}) collective-permute-start(bf16[2,256,768]{2,1,0:T(8,128)(2,1)} %slice_bitcast_fusion), channel_id=1, source_target_pairs={{0,8},{8,0},{16,24},{24,16},{1,9},{9,1},{17,25},{25,17},{2,10},{10... | collective-permute-start | bytes 2359304 | tf_op jit(solution)/shard_map/ppermute | solution.py:549
  124.0 9.8 %collective-permute-start.33 = (f32[8,1536]{1,0:T(8,128)S(1)}, f32[8,1536]{1,0:T(8,128)S(1)}, u32[]{:S(2)}, u32[]{:S(2)}) collective-permute-start(f32[8,1536]{1,0:T(8,128)S(1)} %add.85), channel_id=1, source_target_pairs={{0,4},{1,5},{2,6},{3,7},{4,0},{5,1},{6,2},{7,3},{8,12},{9,13},{10,... | collective-permute-start | bytes 147464 | tf_op jit(solution)/shard_map/ppermute | solution.py:549
  126.9 7.6 %collective-permute-start.32 = (bf16[2,48,768]{2,1,0:T(8,128)(2,1)S(1)}, bf16[2,48,768]{2,1,0:T(8,128)(2,1)S(1)}, u32[]{:S(2)}, u32[]{:S(2)}) collective-permute-start(bf16[2,48,768]{2,1,0:T(8,128)(2,1)S(1)} %pad_maximum_fusion.4), channel_id=1, source_target_pairs={{0,2},{1,3},{2,0},{3,1},{4,6},{5,7},{6,4},{7,5},{8,10},{9,11},{10,... | collective-permute-start | bytes 442376 | tf_op jit(solution)/shard_map/ppermute | solution.py:549
  127.1 7.4 %collective-permute-start.31 = (bf16[24,1024]{1,0:T(8,128)(2,1)S(1)}, bf16[24,1024]{1,0:T(8,128)(2,1)S(1)}, u32[]{:S(2)}, u32[]{:S(2)}) collective-permute-start(bf16[24,1024]{1,0:T(8,128)(2,1)S(1)} %pad_maximum_fusion.8), channel_id=1, source_target_pairs={{0,24},{8,16},{16,8},{24,0},{1,25},{9,17},{17,9},{25,1},{2,26},{10... | collective-permute-start | bytes 147464 | tf_op jit(solution)/shard_map/ppermute | solution.py:549
  127.2 2.6 %collective-permute-start.29 = (bf16[24,1024]{1,0:T(8,128)(2,1)S(1)}, bf16[24,1024]{1,0:T(8,128)(2,1)S(1)}, u32[]{:S(2)}, u32[]{:S(2)}) collective-permute-start(bf16[24,1024]{1,0:T(8,128)(2,1)S(1)} %pad_maximum_fusion.6), channel_id=1, source_target_pairs={{0,8},{8,0},{16,24},{24,16},{1,9},{9,1},{17,25},{25,17},{2,10},{10... | collective-permute-start | bytes 147464 | tf_op jit(solution)/shard_map/ppermute | solution.py:549
  129.7 4.1 %collective-permute-start.30 = (bf16[24,1024]{1,0:T(8,128)(2,1)S(1)}, bf16[24,1024]{1,0:T(8,128)(2,1)S(1)}, u32[]{:S(2)}, u32[]{:S(2)}) collective-permute-start(bf16[24,1024]{1,0:T(8,128)(2,1)S(1)} %pad_maximum_fusion.7), channel_id=1, source_target_pairs={{0,16},{8,24},{16,0},{24,8},{1,17},{9,25},{17,1},{25,9},{2,18},{10... | collective-permute-start | bytes 147464 | tf_op jit(solution)/shard_map/ppermute | solution.py:549
  135.2 6.6 %collective-permute-start.38 = (f32[8,1536]{1,0:T(8,128)}, f32[8,1536]{1,0:T(8,128)}, u32[]{:S(2)}, u32[]{:S(2)}) collective-permute-start(f32[8,1536]{1,0:T(8,128)} %add.92), channel_id=1, source_target_pairs={{0,2},{1,3},{2,0},{3,1},{4,6},{5,7},{6,4},{7,5},{8,10},{9,11},{10,... | collective-permute-start | bytes 147464 | tf_op jit(solution)/shard_map/ppermute | solution.py:549
  137.1 9.0 %collective-permute-start.34 = (bf16[1,24,3328]{2,1,0:T(8,128)(2,1)S(1)}, bf16[1,24,3328]{2,1,0:T(8,128)(2,1)S(1)}, u32[]{:S(2)}, u32[]{:S(2)}) collective-permute-start(bf16[1,24,3328]{2,1,0:T(8,128)(2,1)S(1)} %bitcast.129), channel_id=1, source_target_pairs={{0,2},{1,3},{2,0},{3,1},{4,6},{5,7},{6,4},{7,5},{8,10},{9,11},{10,... | collective-permute-start | bytes 479240 | tf_op jit(solution)/shard_map/ppermute | solution.py:549
  137.4 14.4 %collective-permute-start.35 = (bf16[1,24,3328]{2,1,0:T(8,128)(2,1)S(1)}, bf16[1,24,3328]{2,1,0:T(8,128)(2,1)S(1)}, u32[]{:S(2)}, u32[]{:S(2)}) collective-permute-start(bf16[1,24,3328]{2,1,0:T(8,128)(2,1)S(1)} %bitcast.130), channel_id=1, source_target_pairs={{0,4},{1,5},{2,6},{3,7},{4,0},{5,1},{6,2},{7,3},{8,12},{9,13},{10,... | collective-permute-start | bytes 479240 | tf_op jit(solution)/shard_map/ppermute | solution.py:549
  139.3 12.4 %collective-permute-start.36 = (bf16[1,24,3328]{2,1,0:T(8,128)(2,1)S(1)}, bf16[1,24,3328]{2,1,0:T(8,128)(2,1)S(1)}, u32[]{:S(2)}, u32[]{:S(2)}) collective-permute-start(bf16[1,24,3328]{2,1,0:T(8,128)(2,1)S(1)} %bitcast.131), channel_id=1, source_target_pairs={{0,6},{1,7},{2,4},{3,5},{4,2},{5,3},{6,0},{7,1},{8,14},{9,15},{10,... | collective-permute-start | bytes 479240 | tf_op jit(solution)/shard_map/ppermute | solution.py:549
  141.9 9.9 %collective-permute-start.37 = (bf16[4,48,768]{2,1,0:T(8,128)(2,1)}, bf16[4,48,768]{2,1,0:T(8,128)(2,1)S(1)}, u32[]{:S(2)}, u32[]{:S(2)}) collective-permute-start(bf16[4,48,768]{2,1,0:T(8,128)(2,1)} %pad_maximum_fusion.3), channel_id=1, source_target_pairs={{0,1},{1,0},{2,3},{3,2},{4,5},{5,4},{6,7},{7,6},{8,9},{9,8},{10,11... | collective-permute-start | bytes 884744 | tf_op jit(solution)/shard_map/ppermute | solution.py:549
  145.5 6.3 %copy-start.6 = (bf16[4,48,768]{2,1,0:T(8,128)(2,1)S(1)}, bf16[4,48,768]{2,1,0:T(8,128)(2,1)}, u32[]{:S(2)}) copy-start(bf16[4,48,768]{2,1,0:T(8,128)(2,1)} %pad_maximum_fusion.3) | copy-start | bytes 884740
  145.5 9.7 %copy-start.3 = (bf16[1,256,768]{2,1,0:T(8,128)(2,1)S(1)}, bf16[1,256,768]{2,1,0:T(8,128)(2,1)}, u32[]{:S(2)}) copy-start(bf16[1,256,768]{2,1,0:T(8,128)(2,1)} %param.12) | copy-start | bytes 1179652
  145.5 8.6 %collective-permute-start.40 = (bf16[256,768]{1,0:T(8,128)(2,1)S(1)}, bf16[256,768]{1,0:T(8,128)(2,1)S(1)}, u32[]{:S(2)}, u32[]{:S(2)}) collective-permute-start(bf16[256,768]{1,0:T(8,128)(2,1)S(1)} %slice_bitcast_fusion.7), channel_id=1, source_target_pairs={{0,16},{8,24},{16,0},{24,8},{1,17},{9,25},{17,1},{25,9},{2,18},{10... | collective-permute-start | bytes 1179656 | tf_op jit(solution)/shard_map/ppermute | solution.py:549
  154.1 3.1 %collective-permute-start.43 = (f32[8,1536]{1,0:T(8,128)S(1)}, f32[8,1536]{1,0:T(8,128)S(1)}, u32[]{:S(2)}, u32[]{:S(2)}) collective-permute-start(f32[8,1536]{1,0:T(8,128)S(1)} %add.93.refs_0_), channel_id=1, source_target_pairs={{0,8},{8,0},{16,24},{24,16},{1,9},{9,1},{17,25},{25,17},{2,10},{10... | collective-permute-start | bytes 147464 | tf_op jit(solution)/shard_map/ppermute | solution.py:549
  154.1 17.7 %collective-permute-start.42 = (bf16[4,24,3328]{2,1,0:T(8,128)(2,1)S(1)}, bf16[4,24,3328]{2,1,0:T(8,128)(2,1)S(1)}, u32[]{:S(2)}, u32[]{:S(2)}) collective-permute-start(bf16[4,24,3328]{2,1,0:T(8,128)(2,1)S(1)} %pad_maximum_fusion.1), channel_id=1, source_target_pairs={{0,1},{1,0},{2,3},{3,2},{4,5},{5,4},{6,7},{7,6},{8,9},{9,8},{10,11... | collective-permute-start | bytes 1916936 | tf_op jit(solution)/shard_map/ppermute | solution.py:549
  154.8 15.8 %collective-permute-start.41 = (bf16[256,768]{1,0:T(8,128)(2,1)S(1)}, bf16[256,768]{1,0:T(8,128)(2,1)S(1)}, u32[]{:S(2)}, u32[]{:S(2)}) collective-permute-start(bf16[256,768]{1,0:T(8,128)(2,1)S(1)} %slice_bitcast_fusion.8), channel_id=1, source_target_pairs={{0,16},{8,24},{16,0},{24,8},{1,17},{9,25},{17,1},{25,9},{2,18},{10... | collective-permute-start | bytes 1179656 | tf_op jit(solution)/shard_map/ppermute | solution.py:549
  157.2 10.9 %collective-permute-start.44 = (f32[8,3072]{1,0:T(8,128)S(1)}, f32[8,3072]{1,0:T(8,128)S(1)}, u32[]{:S(2)}, u32[]{:S(2)}) collective-permute-start(f32[8,3072]{1,0:T(8,128)S(1)} %pad_maximum_fusion.5), channel_id=1, source_target_pairs={{0,16},{8,24},{16,0},{24,8},{1,17},{9,25},{17,1},{25,9},{2,18},{10... | collective-permute-start | bytes 294920 | tf_op jit(solution)/shard_map/ppermute | solution.py:549
  171.8 1.3 copy-start.1

commit v4 on v3

--- a/solution.py
+++ b/solution.py
@@ -12,6 +12,7 @@
 N = 128
 KCONV = 4
 BLOCK = 256
+PAIR = 2
 DI = 1536
 CONVCH = 1792
 EPS = 1e-05
@@ -68,14 +69,9 @@
 
 
 def expand(table, pairs):
-    low = iota((table.shape[0], 128), 1) < PS
-    return jnp.concatenate(
-        [
-            jnp.where(low, table[:, 2 * p : 2 * p + 1], table[:, 2 * p + 1 : 2 * p + 2])
-            for p in range(pairs)
-        ],
-        axis=1,
-    )
+    lanes = 2 * PS * pairs
+    select = (iota((128, lanes), 0) == iota((128, lanes), 1) // PS).astype(BF)
+    return sum(dot(part, select) for part in pieces(table, 2))
 
 
 def head_select(lanes):
@@ -303,122 +299,140 @@
 def scan_kernel(n, nd, heads, own_heads, scal, *refs):
     normed_t, conv, conv_before, convk, convk_before, raw, starts, gssm, taps, hp, skip = refs[:11]
     proj_o, dw_o, small_o = refs[11:14]
-    cext, gext, end_grad, acc, ggram, ght = refs[14:]
+    cexts, gexts, end_grad, acc, ggrams, ghts = refs[14:]
     lanes = heads * PS
     width = lanes + 2 * N
     i = pl.program_id(0)
-    b = pl.num_programs(0) - 1 - i
+    group = pl.num_programs(0) - 1 - i
     bounds = [scal[k] for k in range(2, scal.shape[0])]
-    start = b * BLOCK
     pairs = heads // 2
+    later_of, conv_of = {}, {}
 
     @pl.when(i == 0)
     def _():
-        gext[BLOCK:, :] = jnp.zeros((8, width), F32)
+        gexts[0, 0:8, :] = jnp.zeros((8, width), F32)
         end_grad[...] = jnp.zeros_like(end_grad)
         acc[...] = jnp.zeros_like(acc)
         small_o[...] = jnp.zeros_like(small_o)
 
-    for source, halo, at in ((conv, conv_before, slice(0, lanes)), (convk, convk_before, slice(lanes, width))):
-        cext[0:8, at] = jnp.where(b > 0, halo[8:16, :].astype(F32), 0.0)
-        cext[8:, at] = source[...].astype(F32)
-    pre, masks = conv_forward(cext, taps, bounds, start)
-    sig = sigmoid(pre)
-    act = pre * sig
-    low = act.astype(BF)
-    full = act[:, :lanes]
-    keys, query = low[:, lanes : lanes + N], low[:, lanes + N :]
-    z, step, rate, cum, bias, enter, end, keep = scan_terms(raw[...], hp, bounds, start)
-    cum_t, step_t, enter_t = cum.T, step.T, enter.T
-    gram = dot_nt(query, keys)
-    grad = gssm[...]
-    grad_f = grad.astype(F32)
-    grad_t = grad_f.T.astype(BF)
-    first = iota((BLOCK, 2 * PS), 1) < PS
-    lane = iota((128, 128), 1)
-    row_totals = [jnp.zeros((128, 128), F32), jnp.zeros((128, 128), F32)]
-    col_totals = []
-    ggram[...] = jnp.zeros_like(ggram)
-    for p in range(pairs):
-        at = slice(2 * PS * p, 2 * PS * (p + 1))
-        pair = low[:, at]
-        halves = (jnp.where(first, pair, 0), jnp.where(first, 0, pair))
-        for k in range(2):
-            h = 2 * p + k
-            own = slice(PS * h, PS * (h + 1))
-            cols_total = None
-            for t in range(2):
-                rows, cols = slice(128 * t, 128 * (t + 1)), slice(0, 128 * (t + 1))
-                decay = jnp.exp(cum[rows, h : h + 1] - cum_t[h : h + 1, cols] + bias[rows, cols])
-                table = dot_nt(grad[rows, at], halves[k][cols, :])
-                gram_here = gram[rows, cols]
-                step_row = step_t[h : h + 1, cols]
-                weights = (gram_here * decay * step_row).astype(BF)
-                common = table * decay
-                stepped = common * step_row
-                ggram[rows, cols] += stepped
-                col = jnp.sum(common * gram_here, axis=0, keepdims=True)
-                total = jnp.sum(stepped * gram_here, axis=1, keepdims=True)
-                row_totals[t] = jnp.where(lane == h, total, row_totals[t])
-                part = dot(grad_t[own, rows], weights)
-                if t == 0:
-                    ght[own, 0:128] = part
-                    cols_total = col
-                else:
-                    ght[own, 0:128] += part[:, 0:128]
-                    ght[own, 128:256] = part[:, 128:256]
-                    cols_total = col + jnp.concatenate(
-                        [cols_total, jnp.zeros((1, 128), F32)], axis=1
-                    )
-            col_totals.append(cols_total)
-    col_totals.append(jnp.zeros((128 - heads, BLOCK), F32))
-    grad_step = jnp.concatenate(col_totals, axis=0).T
-    grad_cum = jnp.concatenate(row_totals, axis=0) - step * grad_step
-    gg = ggram[...].astype(BF)
-    start_state = starts[0]
-    start_low = start_state.astype(BF)
-    grad_cum += head_sum(grad_f * dot_nt(query, start_low)) * enter
-    entered = (grad_f * expand(enter, pairs)).astype(BF)
-    grad_query = dot(gg, keys) + dot(entered, start_low)
-    later = end_grad[...]
-    end_low = later.astype(BF)
-    scaled = end * step
-    scaled_wide = expand(scaled, pairs)
-    weighted = (full * scaled_wide).astype(BF)
-    grad_weighted = dot_nt(keys, end_low)
-    grad_keys = dot_tn(gg, query) + dot(weighted, end_low)
-    grad_end = head_sum(grad_weighted * full)
-    grad_step += grad_end * end
-    end_terms = grad_end * scaled
-    ones = jnp.ones((8, N), BF)
-    held = sum(dot_nt(ones, part) for part in pieces(later * start_state, 2))
-    grad_tail = jnp.sum(end_terms, axis=0, keepdims=True) + head_sum(held)[0:1, :] * keep
-    final = iota((BLOCK, 1), 0) == BLOCK - 1
-    grad_cum = grad_cum - end_terms + jnp.where(final, grad_tail, 0.0)
-    upper = (iota((BLOCK, BLOCK), 0) <= iota((BLOCK, BLOCK), 1)).astype(BF)
-    grad_log = sum(dot(upper, part) for part in pieces(grad_cum, 3))
-    grad_step += grad_log * rate
-    grad_rate = jnp.sum(grad_log * step, axis=0, keepdims=True)
-    grad_heads = ght[...].T + grad_weighted * scaled_wide + grad_f * skip[...]
-    grad_skip = jnp.sum(grad_f * full, axis=0, keepdims=True)
-    grad_act = jnp.concatenate([grad_heads, grad_keys, grad_query], axis=1)
-    grad_pre = grad_act * (sig * (1.0 + pre * (1.0 - sig)))
-    conv_low = conv_backward(grad_pre, gext, cext, masks, taps, bounds, start, small_o).astype(BF)
-    grad_raw = grad_step * sigmoid(z)
-    small_o[0:1, width : width + 128] += jnp.sum(grad_raw, axis=0, keepdims=True)
-    small_o[1:2, width : width + 128] += grad_rate * rate
-    small_o[2:3, width : width + 128] += head_sum(jnp.broadcast_to(grad_skip, (8, lanes)))[0:1, :]
-    here = normed_t[...]
-    raw_low = grad_raw.astype(BF)
-    small_o[:, width + 128 :] += dot_nt(raw_low.T[0:16, :], here)[0:8, :]
-    acc[...] += dot(here, conv_low)
-    proj_o[:, :width] = conv_low
-    proj_o[:, width:] = pltpu.roll(grad_raw, scal[0] * own_heads, 1).astype(BF)
-    geared = jnp.concatenate(
-        [grad_t[PS * h : PS * (h + 1), :].astype(F32) * enter_t[h : h + 1, :] for h in range(heads)],
-        axis=0,
-    ).astype(BF)
-    end_grad[...] = head_rows(keep, lanes) * later + dot(geared, query)
+    def one(u):
+        here = slice(u * BLOCK, (u + 1) * BLOCK)
+        start = (group * PAIR + u) * BLOCK
+        cext, gext, ggram, ght = (ref.at[u] for ref in (cexts, gexts, ggrams, ghts))
+        for source, halo, at in ((conv, conv_before, slice(0, lanes)), (convk, convk_before, slice(lanes, width))):
+            if u == 0:
+                cext[0:8, at] = jnp.where(start > 0, halo[8:16, :].astype(F32), 0.0)
+            else:
+                cext[0:8, at] = source[u * BLOCK - 16 : u * BLOCK, :].astype(F32)[8:16, :]
+            cext[8:, at] = source[here, :].astype(F32)
+        pre, masks = conv_forward(cext, taps, bounds, start)
+        sig = sigmoid(pre)
+        act = pre * sig
+        low = act.astype(BF)
+        full = act[:, :lanes]
+        keys, query = low[:, lanes : lanes + N], low[:, lanes + N :]
+        z, step, rate, cum, bias, enter, end, keep = scan_terms(raw[here, :], hp, bounds, start)
+        cum_t, step_t, enter_t = cum.T, step.T, enter.T
+        yield
+        gram = dot_nt(query, keys)
+        grad = gssm[here, :]
+        grad_f = grad.astype(F32)
+        grad_t = grad_f.T.astype(BF)
+        geared = jnp.concatenate(
+            [grad_t[PS * h : PS * (h + 1), :].astype(F32) * enter_t[h : h + 1, :] for h in range(heads)],
+            axis=0,
+        ).astype(BF)
+        later = end_grad[...] if u == PAIR - 1 else later_of[u + 1]
+        later_of[u] = head_rows(keep, lanes) * later + dot(geared, query)
+        yield
+        first = iota((BLOCK, 2 * PS), 1) < PS
+        lane = iota((128, 128), 1)
+        row_totals = [jnp.zeros((128, 128), F32), jnp.zeros((128, 128), F32)]
+        col_totals = []
+        ggram[...] = jnp.zeros_like(ggram)
+        for p in range(pairs):
+            at = slice(2 * PS * p, 2 * PS * (p + 1))
+            pair = low[:, at]
+            halves = (jnp.where(first, pair, 0), jnp.where(first, 0, pair))
+            for k in range(2):
+                h = 2 * p + k
+                own = slice(PS * h, PS * (h + 1))
+                cols_total = None
+                for t in range(2):
+                    rows, cols = slice(128 * t, 128 * (t + 1)), slice(0, 128 * (t + 1))
+                    decay = jnp.exp(cum[rows, h : h + 1] - cum_t[h : h + 1, cols] + bias[rows, cols])
+                    table = dot_nt(grad[rows, at], halves[k][cols, :])
+                    gram_here = gram[rows, cols]
+                    step_row = step_t[h : h + 1, cols]
+                    weights = (gram_here * decay * step_row).astype(BF)
+                    common = table * decay
+                    stepped = common * step_row
+                    ggram[rows, cols] += stepped
+                    col = jnp.sum(common * gram_here, axis=0, keepdims=True)
+                    total = jnp.sum(stepped * gram_here, axis=1, keepdims=True)
+                    row_totals[t] = jnp.where(lane == h, total, row_totals[t])
+                    part = dot(grad_t[own, rows], weights)
+                    if t == 0:
+                        ght[own, 0:128] = part
+                        cols_total = col
+                    else:
+                        ght[own, 0:128] += part[:, 0:128]
+                        ght[own, 128:256] = part[:, 128:256]
+                        cols_total = col + jnp.concatenate(
+                            [cols_total, jnp.zeros((1, 128), F32)], axis=1
+                        )
+                col_totals.append(cols_total)
+                yield
+        col_totals.append(jnp.zeros((128 - heads, BLOCK), F32))
+        grad_step = jnp.concatenate(col_totals, axis=0).T
+        grad_cum = jnp.concatenate(row_totals, axis=0) - step * grad_step
+        gg = ggram[...].astype(BF)
+        start_state = starts[u]
+        start_low = start_state.astype(BF)
+        grad_cum += head_sum(grad_f * dot_nt(query, start_low)) * enter
+        entered = (grad_f * expand(enter, pairs)).astype(BF)
+        grad_query = dot(gg, keys) + dot(entered, start_low)
+        end_low = later.astype(BF)
+        scaled = end * step
+        scaled_wide = expand(scaled, pairs)
+        weighted = (full * scaled_wide).astype(BF)
+        grad_weighted = dot_nt(keys, end_low)
+        grad_keys = dot_tn(gg, query) + dot(weighted, end_low)
+        grad_end = head_sum(grad_weighted * full)
+        grad_step += grad_end * end
+        end_terms = grad_end * scaled
+        yield
+        ones = jnp.ones((8, N), BF)
+        held = sum(dot_nt(ones, part) for part in pieces(later * start_state, 2))
+        grad_tail = jnp.sum(end_terms, axis=0, keepdims=True) + head_sum(held)[0:1, :] * keep
+        final = iota((BLOCK, 1), 0) == BLOCK - 1
+        grad_cum = grad_cum - end_terms + jnp.where(final, grad_tail, 0.0)
+        upper = (iota((BLOCK, BLOCK), 0) <= iota((BLOCK, BLOCK), 1)).astype(BF)
+        grad_log = sum(dot(upper, part) for part in pieces(grad_cum, 3))
+        grad_step += grad_log * rate
+        grad_rate = jnp.sum(grad_log * step, axis=0, keepdims=True)
+        grad_heads = ght[...].T + grad_weighted * scaled_wide + grad_f * skip[...]
+        grad_skip = jnp.sum(grad_f * full, axis=0, keepdims=True)
+        yield
+        grad_act = jnp.concatenate([grad_heads, grad_keys, grad_query], axis=1)
+        grad_pre = grad_act * (sig * (1.0 + pre * (1.0 - sig)))
+        gext[BLOCK:, :] = gexts[0, 0:8, :] if u == PAIR - 1 else gexts[u + 1, 0:8, :]
+        conv_low = conv_backward(grad_pre, gext, cext, masks, taps, bounds, start, small_o).astype(BF)
+        grad_raw = grad_step * sigmoid(z)
+        small_o[0:1, width : width + 128] += jnp.sum(grad_raw, axis=0, keepdims=True)
+        small_o[1:2, width : width + 128] += grad_rate * rate
+        small_o[2:3, width : width + 128] += head_sum(jnp.broadcast_to(grad_skip, (8, lanes)))[0:1, :]
+        raw_low = grad_raw.astype(BF)
+        small_o[:, width + 128 :] += dot_nt(raw_low.T[0:16, :], normed_t[:, here])[0:8, :]
+        conv_of[u] = conv_low
+        proj_o[here, :width] = conv_low
+        proj_o[here, width:] = pltpu.roll(grad_raw, scal[0] * own_heads, 1).astype(BF)
+
+    running = [one(u) for u in reversed(range(PAIR))]
+    while running:
+        running = [block for block in running if next(block, True) is None]
+    end_grad[...] = later_of[0]
+    acc[...] += dot(normed_t[...], jnp.concatenate([conv_of[u] for u in range(PAIR)], axis=0))
 
     @pl.when(i == pl.num_programs(0) - 1)
     def _():
@@ -442,7 +456,6 @@
         term = taps[k : k + 1, :] * after
         total = term if total is None else total + term
     small_o[4:5, 0:count] += jnp.sum(grad_pre, axis=0, keepdims=True)
-    gext[BLOCK:, :] = gext[0:8, :]
     return total
 
 
@@ -873,17 +886,15 @@
         )
 
     order = gather_order(ndp) if nd > 1 else [0]
-    back = lambda b: nb - 1 - b
-
-    def tokens_back(cols, at=0):
-        return pl.BlockSpec((BLOCK, cols), lambda b, s: (back(b), at))
-
-    def halo_back(cols, at=0):
+
+    def step_rows_back(cols):
+        return pl.BlockSpec((PAIR * BLOCK, cols), lambda b, s: (nb // PAIR - 1 - b, 0))
+
+    def step_halo_back(cols):
+        strips = PAIR * BLOCK // 16
         return pl.BlockSpec(
-            (16, cols), lambda b, s: (jnp.maximum(back(b) * (BLOCK // 16) - 1, 0), at)
+            (16, cols), lambda b, s: (jnp.maximum((nb // PAIR - 1 - b) * strips - 1, 0), 0)
         )
-
-    normed_back = pl.BlockSpec((model, BLOCK), lambda b, s: (0, back(b)))
 
     if nd > 1:
         early = Shares(early, 0)
@@ -893,17 +904,17 @@
     proj_low, dw, small_grads = call(
         functools.partial(scan_kernel, n, nd, heads, own_heads),
         "scan_back",
-        (nb,),
+        (nb // PAIR,),
         scal,
         [
-            normed_back,
-            tokens_back(lanes),
-            halo_back(lanes),
-            tokens_back(2 * N),
-            halo_back(2 * N),
-            tokens_back(128),
-            pl.BlockSpec((1, lanes, N), lambda b, s: (back(b), 0, 0)),
-            tokens_back(lanes),
+            pl.BlockSpec((model, PAIR * BLOCK), lambda b, s: (0, nb // PAIR - 1 - b)),
+            step_rows_back(lanes),
+            step_halo_back(lanes),
+            step_rows_back(2 * N),
+            step_halo_back(2 * N),
+            step_rows_back(128),
+            pl.BlockSpec((PAIR, lanes, N), lambda b, s: (nb // PAIR - 1 - b, 0, 0)),
+            step_rows_back(lanes),
             whole(8, width),
             whole(8, 128),
             whole(1, lanes),
@@ -922,7 +933,7 @@
             skip,
         ),
         [
-            tokens_back(width + 128),
+            step_rows_back(width + 128),
             whole(n, nd, rows // nd, width),
             whole(8, width + 128 + model),
         ],
@@ -932,12 +943,12 @@
             shape((8, width + 128 + model), F32),
         ],
         [
-            pltpu.VMEM((8 + BLOCK, width), F32),
-            pltpu.VMEM((BLOCK + 8, width), F32),
+            pltpu.VMEM((PAIR, 8 + BLOCK, width), F32),
+            pltpu.VMEM((PAIR, BLOCK + 8, width), F32),
             pltpu.VMEM((lanes, N), F32),
             pltpu.VMEM((model, width), F32),
-            pltpu.VMEM((BLOCK, BLOCK), F32),
-            pltpu.VMEM((lanes, BLOCK), F32),
+            pltpu.VMEM((PAIR, BLOCK, BLOCK), F32),
+            pltpu.VMEM((PAIR, lanes, BLOCK), F32),
         ],
         20 * 10**9,
         10**7,
@@ -951,6 +962,7 @@
         for low in early.low[1:]:
             early.reduce(low)
         bits = [1 << bit for bit in range(ndp.bit_length() - 1)]
+        hops = bits[1:][::-1]
         small_grads = small_grads + xor(small_grads, "dp", bits[0])
     (gn_part,) = call(
         normed_kernel,
@@ -973,10 +985,9 @@
         wo, gates = early.value[:own_rows], early.value[own_rows:]
         for low in late.low[1:]:
             late.reduce(low)
-        gn_mine, gn_recv = chip_exchange(core_sum(gn_part))
-        hops = bits[1:][::-1]
+        gn_sum = core_sum(gn_part)
         wo = pair_step(wo[None], hops[0])
-        late.value, wo, small_grads = tie(late.value, wo, small_grads)
+        late.value, wo, small_grads, gn_sum = tie(late.value, wo, small_grads, gn_sum)
         owned = to_owners(
             [
                 jnp.concatenate(
@@ -991,23 +1002,23 @@
         )
         for hop in hops[1:]:
             wo = pair_step(wo, hop)
-        small_grads = small_grads + xor(small_grads, "dp", hops[0])
+        gn_mine, gn_recv = chip_exchange(gn_sum)
         late = late_rows(owned)
-        late, wo, small_grads = tie(late, wo, small_grads)
+        late, wo, small_grads, out_sum = tie(late, wo, small_grads, out_sum)
         gather = list(reversed(stages(ndp)))
         late = gather_step(late[None], *gather[0])
         wo = pair_step(wo, bits[0])
-        for hop in hops[1:]:
-            small_grads = small_grads + xor(small_grads, "dp", hop)
-        late, wo, small_grads, out_sum, *gn_recv = tie(late, wo, small_grads, out_sum, *gn_recv)
+        out_mine, out_recv = chip_exchange(out_sum)
+        late, wo, small_grads, *gn_recv = tie(late, wo, small_grads, *gn_recv)
         for low, take in gather[1:]:
             late = gather_step(late, low, take)
+        for hop in hops:
+            small_grads = small_grads + xor(small_grads, "dp", hop)
         small_other = xor(small_grads, "fsdp", 1)
         small_parts = [small_grads, small_other]
         for k in range(2, n, 2):
             pair = xor(jnp.concatenate([small_grads, small_other], axis=1), "fsdp", k)
             small_parts += [pair[:, : small_grads.shape[1]], pair[:, small_grads.shape[1] :]]
-        out_mine, out_recv = chip_exchange(out_sum)
     else:
         out_mine, out_recv = chip_exchange(out_sum)
         gn_mine, gn_recv = chip_exchange(core_sum(gn_part))

time: 177 us -> 174 us (0.983)
  waiting for transfers between devices: 56.4 us -> 52 us
  starting transfers between devices: 45.1 us -> 49.1 us
  other arithmetic: 9 us -> 5.76 us
    ppermute x45, waiting for transfers between devices: 56.4 us -> 52 us  [xor(): lax.ppermute(value, axis, [(s, s ^ k) for s in range(lax.axis_size(axis))])]
    ppermute x45, starting transfers between devices: 45.1 us -> 49.1 us  [xor(): lax.ppermute(value, axis, [(s, s ^ k) for s in range(lax.axis_size(axis))])]
    unnamed x18 -> x48, local copies, waits for them, and re-layouts: 3.59 us -> 6.04 us
  transfers between devices with their start and end apart: 45 -> 45, of which waited for: 16 -> 17; matrix products, arithmetic and copies ran while one was open for 8% -> 6% of each run, Pallas kernels for 22% -> 21%
where the time goes in v4:
time: 174 us
  Pallas kernels  53.4 us (31%)
  waiting for transfers between devices  52 us (30%)
  starting transfers between devices  49.1 us (28%)
  local copies, waits for them, and re-layouts  12.2 us (7%)
  other arithmetic  5.76 us (3%)
    pallas_call x10, Pallas kernels, call(): pl.pallas_call(kernel, grid_spec=pltpu.PrefetchScalarGridSpec(num_scalar_...  53.4 us
    ppermute x45, waiting for transfers between devices, xor(): lax.ppermute(value, axis, [(s, s ^ k) for s in range(lax.axis_size(axis))])  52 us
    ppermute x45, starting transfers between devices, xor(): lax.ppermute(value, axis, [(s, s ^ k) for s in range(lax.axis_size(axis))])  49.1 us
    unnamed x48, local copies, waits for them, and re-layouts  6.04 us
  transfers between devices with their start and end apart: 45, of which 17 were waited for; matrix products, arithmetic and copies ran while one was open for 6% of the time, Pallas kernels for 21%

profile of v4, /device:TPU:0, one launch (start us, length us, event | category | flops | bytes accessed | tf_op | source)
XLA Modules:
  0.0 173.7 jit_solution(14257946596572776366)
XLA Ops:
  1.2 2.6 %collective-permute-start = (bf16[256,768]{1,0:T(8,128)(2,1)}, bf16[256,768]{1,0:T(8,128)(2,1)S(1)}, u32[]{:S(2)}, u32[]{:S(2)}) collective-permute-start(bf16[256,768]{1,0:T(8,128)(2,1)} %bitcast.116), channel_id=1, source_target_pairs={{0,16},{8,24},{16,0},{24,8},{1,17},{9,25},{17,1},{25,9},{2,18},{10... | collective-permute-start | bytes 1179656 | tf_op jit(solution)/shard_map/ppermute | solution.py:562
  3.7 0.8 reduce-window.4
  4.6 0.7 fusion.38.refs_14_.refs_9_
  5.2 0.7 reshape_convert_fusion.refs_3_
  5.9 0.7 reshape.88
  6.6 0.7 broadcast_in_dim.25
  7.3 0.8 fusion.30.refs_0_
  8.5 1.4 collective-permute-start.4
  10.0 0.7 broadcast_in_dim.24
  10.8 0.7 reshape.96.refs_8_.refs_12_.gain
  11.5 1.3 copy-done
  12.8 0.7 packets.1
  14.4 1.8 %collective-permute-start.7 = (bf16[192,768]{1,0:T(8,128)(2,1)S(1)}, bf16[192,768]{1,0:T(8,128)(2,1)S(1)}, u32[]{:S(2)}, u32[]{:S(2)}) collective-permute-start(bf16[192,768]{1,0:T(8,128)(2,1)S(1)} %get-tuple-element.96), channel_id=1, source_target_pairs={{0,16},{8,24},{16,0},{24,8},{1,17},{9,25},{17,1},{25,9},{2,18},{10... | collective-permute-start | bytes 884744 | tf_op jit(solution)/shard_map/ppermute | solution.py:562
  16.2 1.5 collective-permute-start.10
  17.6 15.3 %collective-permute-done.10.refs_10_ = bf16[192,384]{1,0:T(8,128)(2,1)S(1)} collective-permute-done((bf16[192,384]{1,0:T(8,128)(2,1)S(1)}, bf16[192,384]{1,0:T(8,128)(2,1)S(1)}, u32[]{:S(2)}, u32[]{:S(2)}) %collective-permute-start.10) | collective-permute-done | bytes 147488 | tf_op jit(solution)/shard_map/ppermute | solution.py:562
  33.5 0.6 params.1
  34.1 1.8 %collective-permute-start.13 = (bf16[256,768]{1,0:T(8,128)(2,1)}, bf16[256,768]{1,0:T(8,128)(2,1)S(1)}, u32[]{:S(2)}, u32[]{:S(2)}) collective-permute-start(bf16[256,768]{1,0:T(8,128)(2,1)} %bitcast.121), channel_id=1, source_target_pairs={{0,16},{8,24},{16,0},{24,8},{1,17},{9,25},{17,1},{25,9},{2,18},{10... | collective-permute-start | bytes 1179656 | tf_op jit(solution)/shard_map/ppermute | solution.py:562
  36.0 1.0 copy-done.2
  37.0 10.9 %forward.1 = (bf16[1024,768]{1,0:T(8,128)(2,1)S(1)}, bf16[768,1024]{1,0:T(8,128)(2,1)S(1)}, bf16[1024,384]{1,0:T(8,128)(2,1)S(1)}, bf16[1024,256]{1,0:T(8,128)(2...) custom-call(s32[5]{0:T(128)S(1)} %pad_add_fusion.scal, ...), custom_call_target="tpu_custom_call" | custom-call | flops 8999999488 | bytes 10000000 | tf_op jit(solution)/shard_map/forward/pallas_call | solution.py:637
  47.9 0.8 copy-done.20
  49.3 1.3 collective-permute-done.14.refs_3_
  50.7 5.1 %gate.1 = (bf16[1024,384]{1,0:T(8,128)(2,1)S(1)}, f32[8,1024]{1,0:T(8,128)S(1)}) custom-call(s32[5]{0:T(128)S(1)} %pad_add_fusion.scal, bf16[256,768]{1,0:T(8,128)(2,1)S(1)} %bitcast.123, bf16[256,768]{1,0:T(8,128)(2,1)S(1)} %collective-permute-done.12.refs_1_, bf16[256,768]{1,0:T(8,128)(2,1)S(1)} %collective-permute-done.13.refs_2_, ...), custom_call_target="tpu_custom_call" | custom-call | flops 2000000000 | bytes 10000000 | tf_op jit(solution)/shard_map/gate/pallas_call | solution.py:637
  56.6 1.2 collective-permute-start.17
  57.8 2.5 %collective-permute-done.16.refs_6_ = f32[8,1024]{1,0:T(8,128)S(1)} collective-permute-done((f32[8,1024]{1,0:T(8,128)S(1)}, f32[8,1024]{1,0:T(8,128)S(1)}, u32[]{:S(2)}, u32[]{:S(2)}) %collective-permute-start.16) | collective-permute-done | bytes 32800 | tf_op jit(solution)/shard_map/ppermute | solution.py:562
  60.3 1.4 copy-done.7
  61.7 1.4 copy-done.11
  63.1 8.2 %output.1 = (bf16[4,256,768]{2,1,0:T(8,128)(2,1)S(1)}, bf16[1024,384]{1,0:T(8,128)(2,1)S(1)}, bf16[1024,384]{1,0:T(8,128)(2,1)S(1)}, bf16[8,96,768]{2,1,0:T(8,128)(2,1)S(1)}) custom-call(s32[5]{0:T(128)S(1)} %pad_add_fusion.scal, bf16[256,768]{1,0:T(8,128)(2,1)S(1)} %bitcast.124, bf16[256,768]{1,0:T(8,128)(2,1)S(1)} %collective-permute-done.12.refs_1_, ...), custom_call_target="tpu_custom_call" | custom-call | flops 3000000000 | bytes 10000000 | tf_op jit(solution)/shard_map/output/pallas_call | solution.py:637
  71.7 1.8 %collective-permute-start.18 = (bf16[4,96,768]{2,1,0:T(8,128)(2,1)S(1)}, bf16[4,96,768]{2,1,0:T(8,128)(2,1)S(1)}, u32[]{:S(2)}, u32[]{:S(2)}) collective-permute-start(bf16[4,96,768]{2,1,0:T(8,128)(2,1)S(1)} %slice_bitcast_fusion.4), channel_id=1, source_target_pairs={{0,1},{1,0},{2,3},{3,2},{4,5},{5,4},{6,7},{7,6},{8,9},{9,8},{10,11... | collective-permute-start | bytes 1769480 | tf_op jit(solution)/shard_map/ppermute | solution.py:562
  73.5 19.1 %scan_back.1 = (bf16[1024,768]{1,0:T(8,128)(2,1)S(1)}, bf16[4,8,24,640]{3,2,1,0:T(8,128)(2,1)S(1)}, f32[8,1536]{1,0:T(8,128)S(1)}) custom-call(s32[5]{0:T(128)S(1)} %pad_add_fusion.scal, bf16[768,1024]{1,0:T(8,128)(2,1)S(1)} %copy-done.11, bf16[1024,384]{1,0:T(8,128)(2,1)S(1)} %copy-done.15, bf16[1024,384]{1,0:T(8,128)(2,1)S(1)} %copy-done.15, ...), custom_call_target="tpu_custom_call" | custom-call | flops 20000000000 | bytes 10000000 | tf_op jit(solution)/shard_map/scan_back/pallas_call | solution.py:637
  93.0 1.3 collective-permute-start.24
  94.4 1.7 collective-permute-start.21
  96.0 2.6 %collective-permute-start.22 = (bf16[96,768]{1,0:T(8,128)(2,1)S(1)}, bf16[96,768]{1,0:T(8,128)(2,1)S(1)}, u32[]{:S(2)}, u32[]{:S(2)}) collective-permute-start(bf16[96,768]{1,0:T(8,128)(2,1)S(1)} %get-tuple-element.163), channel_id=1, source_target_pairs={{0,4},{1,5},{2,6},{3,7},{4,0},{5,1},{6,2},{7,3},{8,12},{9,13},{10,... | collective-permute-start | bytes 442376 | tf_op jit(solution)/shard_map/ppermute | solution.py:562
  99.0 0.9 collective-permute-start.20
  99.8 3.5 %normed_grad.1 = bf16[4,256,768]{2,1,0:T(8,128)(2,1)S(1)} custom-call(s32[5]{0:T(128)S(1)} %pad_add_fusion.scal, bf16[1024,768]{1,0:T(8,128)(2,1)S(1)} %get-tuple-element.126.proj, bf16[1024,384]{1,0:T(8,128)(2,1)S(1)} %get-tuple-element.127.ggr, bf16[768,768]{1,0:T(8,128)(2,1)S(1)} %copy-done.13, bf16[768,384]{1,0:T(8,128)(2,1)S(1)} %copy-done.9), custom_call_target="tpu_custom_call" | custom-call | flops 5000000000 | bytes 10000000 | tf_op jit(solution)/shard_map/normed_grad/pallas_call | solution.py:637
  103.4 6.6 %collective-permute-done.22 = bf16[96,768]{1,0:T(8,128)(2,1)S(1)} collective-permute-done((bf16[96,768]{1,0:T(8,128)(2,1)S(1)}, bf16[96,768]{1,0:T(8,128)(2,1)S(1)}, u32[]{:S(2)}, u32[]{:S(2)}) %collective-permute-start.22) | collective-permute-done | bytes 147488 | tf_op jit(solution)/shard_map/ppermute | solution.py:562
  110.1 1.2 collective-permute-done.20
  111.5 2.3 %collective-permute-start.28 = (bf16[1,48,768]{2,1,0:T(8,128)(2,1)S(1)}, bf16[1,48,768]{2,1,0:T(8,128)(2,1)S(1)}, u32[]{:S(2)}, u32[]{:S(2)}) collective-permute-start(bf16[1,48,768]{2,1,0:T(8,128)(2,1)S(1)} %slice_bitcast_fusion.14), channel_id=1, source_target_pairs={{0,4},{1,5},{2,6},{3,7},{4,0},{5,1},{6,2},{7,3},{8,12},{9,13},{10,... | collective-permute-start | bytes 221192 | tf_op jit(solution)/shard_map/ppermute | solution.py:562
  113.8 2.0 %collective-permute-start.25 = (bf16[4,24,640]{2,1,0:T(8,128)(2,1)S(1)}, bf16[4,24,640]{2,1,0:T(8,128)(2,1)S(1)}, u32[]{:S(2)}, u32[]{:S(2)}) collective-permute-start(bf16[4,24,640]{2,1,0:T(8,128)(2,1)S(1)} %get-tuple-element.164), channel_id=1, source_target_pairs={{0,2},{1,3},{2,0},{3,1},{4,6},{5,7},{6,4},{7,5},{8,10},{9,11},{10,... | collective-permute-start | bytes 368648 | tf_op jit(solution)/shard_map/ppermute | solution.py:562
  115.8 2.5 %collective-permute-start.27 = (bf16[4,24,640]{2,1,0:T(8,128)(2,1)S(1)}, bf16[4,24,640]{2,1,0:T(8,128)(2,1)S(1)}, u32[]{:S(2)}, u32[]{:S(2)}) collective-permute-start(bf16[4,24,640]{2,1,0:T(8,128)(2,1)S(1)} %get-tuple-element.165), channel_id=1, source_target_pairs={{0,6},{1,7},{2,4},{3,5},{4,2},{5,3},{6,0},{7,1},{8,14},{9,15},{10,... | collective-permute-start | bytes 368648 | tf_op jit(solution)/shard_map/ppermute | solution.py:562
  118.8 2.8 %collective-permute-done.25 = bf16[4,24,640]{2,1,0:T(8,128)(2,1)S(1)} collective-permute-done((bf16[4,24,640]{2,1,0:T(8,128)(2,1)S(1)}, bf16[4,24,640]{2,1,0:T(8,128)(2,1)S(1)}, u32[]{:S(2)}, u32[]{:S(2)}) %collective-permute-start.25) | collective-permute-done | bytes 122912 | tf_op jit(solution)/shard_map/ppermute | solution.py:562
  121.6 6.6 %collective-permute-done.26 = bf16[4,24,640]{2,1,0:T(8,128)(2,1)S(1)} collective-permute-done((bf16[4,24,640]{2,1,0:T(8,128)(2,1)S(1)}, bf16[4,24,640]{2,1,0:T(8,128)(2,1)S(1)}, u32[]{:S(2)}, u32[]{:S(2)}) %collective-permute-start.26) | collective-permute-done | bytes 122912 | tf_op jit(solution)/shard_map/ppermute | solution.py:562
  128.5 2.2 %collective-permute-start.33 = (bf16[2,48,768]{2,1,0:T(8,128)(2,1)S(1)}, bf16[2,48,768]{2,1,0:T(8,128)(2,1)S(1)}, u32[]{:S(2)}, u32[]{:S(2)}) collective-permute-start(bf16[2,48,768]{2,1,0:T(8,128)(2,1)S(1)} %pad_maximum_fusion.4), channel_id=1, source_target_pairs={{0,2},{1,3},{2,0},{3,1},{4,6},{5,7},{6,4},{7,5},{8,10},{9,11},{10,... | collective-permute-start | bytes 442376 | tf_op jit(solution)/shard_map/ppermute | solution.py:562
  130.8 1.4 collective-permute-start.31
  132.6 1.5 collective-permute-start.39
  134.1 1.5 collective-permute-done.31
  135.9 3.7 %collective-permute-start.36 = (bf16[1,24,3328]{2,1,0:T(8,128)(2,1)S(1)}, bf16[1,24,3328]{2,1,0:T(8,128)(2,1)S(1)}, u32[]{:S(2)}, u32[]{:S(2)}) collective-permute-start(bf16[1,24,3328]{2,1,0:T(8,128)(2,1)S(1)} %bitcast.127), channel_id=1, source_target_pairs={{0,4},{1,5},{2,6},{3,7},{4,0},{5,1},{6,2},{7,3},{8,12},{9,13},{10,... | collective-permute-start | bytes 479240 | tf_op jit(solution)/shard_map/ppermute | solution.py:562
  139.6 0.7 collective-permute-start.37
  140.2 0.7 collective-permute-start.38
  140.9 3.7 %collective-permute-done.35 = bf16[1,24,3328]{2,1,0:T(8,128)(2,1)S(1)} collective-permute-done((bf16[1,24,3328]{2,1,0:T(8,128)(2,1)S(1)}, bf16[1,24,3328]{2,1,0:T(8,128)(2,1)S(1)}, u32[]{:S(2)}, u32[]{:S(2)}) %collective-permute-start.35) | collective-permute-done | bytes 159776 | tf_op jit(solution)/shard_map/ppermute | solution.py:562
  144.6 1.2 collective-permute-start.34
  145.8 5.6 %collective-permute-done.36 = bf16[1,24,3328]{2,1,0:T(8,128)(2,1)S(1)} collective-permute-done((bf16[1,24,3328]{2,1,0:T(8,128)(2,1)S(1)}, bf16[1,24,3328]{2,1,0:T(8,128)(2,1)S(1)}, u32[]{:S(2)}, u32[]{:S(2)}) %collective-permute-start.36) | collective-permute-done | bytes 159776 | tf_op jit(solution)/shard_map/ppermute | solution.py:562
  151.6 3.7 %collective-permute-start.41 = (f32[8,1536]{1,0:T(8,128)S(1)}, f32[8,1536]{1,0:T(8,128)S(1)}, u32[]{:S(2)}, u32[]{:S(2)}) collective-permute-start(f32[8,1536]{1,0:T(8,128)S(1)} %add.85), channel_id=1, source_target_pairs={{0,4},{1,5},{2,6},{3,7},{4,0},{5,1},{6,2},{7,3},{8,12},{9,13},{10,... | collective-permute-start | bytes 147464 | tf_op jit(solution)/shard_map/ppermute | solution.py:562
  155.3 0.8 collective-permute-start.40
  156.3 1.0 collective-permute-done.41
  157.3 2.0 %collective-permute-start.42 = (f32[8,1536]{1,0:T(8,128)S(1)}, f32[8,1536]{1,0:T(8,128)S(1)}, u32[]{:S(2)}, u32[]{:S(2)}) collective-permute-start(f32[8,1536]{1,0:T(8,128)S(1)} %add.99), channel_id=1, source_target_pairs={{0,2},{1,3},{2,0},{3,1},{4,6},{5,7},{6,4},{7,5},{8,10},{9,11},{10,... | collective-permute-start | bytes 147464 | tf_op jit(solution)/shard_map/ppermute | solution.py:562
  159.3 1.6 out_weight_grad.1
  161.6 0.6 slice_reduce_fusion
  162.2 0.6 collective-permute-done.43.refs_1_
  162.8 1.8 %collective-permute-start.44 = (f32[8,3072]{1,0:T(8,128)S(1)}, f32[8,3072]{1,0:T(8,128)S(1)}, u32[]{:S(2)}, u32[]{:S(2)}) collective-permute-start(f32[8,3072]{1,0:T(8,128)S(1)} %pad_maximum_fusion.5), channel_id=1, source_target_pairs={{0,16},{8,24},{16,0},{24,8},{1,17},{9,25},{17,1},{25,9},{2,18},{10... | collective-permute-start | bytes 294920 | tf_op jit(solution)/shard_map/ppermute | solution.py:562
  164.6 1.3 fusion.14
  165.9 1.8 %collective-permute-done.44 = f32[8,3072]{1,0:T(8,128)S(1)} collective-permute-done((f32[8,3072]{1,0:T(8,128)S(1)}, f32[8,3072]{1,0:T(8,128)S(1)}, u32[]{:S(2)}, u32[]{:S(2)}) %collective-permute-start.44) | collective-permute-done | bytes 98336 | tf_op jit(solution)/shard_map/ppermute | solution.py:562
  167.7 0.7 small_grads.1
  168.3 0.6 slice.199
  170.2 2.9 %in_weight_grad.1 = (f32[192,3352]{1,0:T(8,128)}, f32[8,192]{1,0:T(8,128)S(1)}) custom-call(s32[5]{0:T(128)S(1)} %pad_add_fusion.scal, bf16[8,24,3328]{2,1,0:T(8,128)(2,1)S(1)} %pad_maximum_fusion.refs_0_, f32[192,128]{1,0:T(8,128)S(1)} %get-tuple-element.148.refs_1_, bf16[192,3352]{1,0:T(8,128)(2,1)S(1)} %copy-done.1, f32[1,192]{1,0:T(1,128)S(1)} %reshape_convert_fusion.refs_3_), custom_call_target="tpu_custom_call" | custom-call | flops 100000000 | bytes 6000000 | tf_op jit(solution)/shard_map/in_weight_grad/pallas_call | solution.py:637
  (138 shorter events, 9.9 us)
Async XLA Ops:
  0.6 7.4 %collective-permute-start.1 = (bf16[256,768]{1,0:T(8,128)(2,1)}, bf16[256,768]{1,0:T(8,128)(2,1)S(1)}, u32[]{:S(2)}, u32[]{:S(2)}) collective-permute-start(bf16[256,768]{1,0:T(8,128)(2,1)} %bitcast.115), channel_id=1, source_target_pairs={{0,8},{8,0},{16,24},{24,16},{1,9},{9,1},{17,25},{25,17},{2,10},{10... | collective-permute-start | bytes 1179656 | tf_op jit(solution)/shard_map/ppermute | solution.py:562
  1.2 12.7 %collective-permute-start = (bf16[256,768]{1,0:T(8,128)(2,1)}, bf16[256,768]{1,0:T(8,128)(2,1)S(1)}, u32[]{:S(2)}, u32[]{:S(2)}) collective-permute-start(bf16[256,768]{1,0:T(8,128)(2,1)} %bitcast.116), channel_id=1, source_target_pairs={{0,16},{8,24},{16,0},{24,8},{1,17},{9,25},{17,1},{25,9},{2,18},{10... | collective-permute-start | bytes 1179656 | tf_op jit(solution)/shard_map/ppermute | solution.py:562
  8.1 5.7 %collective-permute-start.2 = (bf16[8,512]{1,0:T(8,128)(2,1)S(1)}, bf16[8,512]{1,0:T(8,128)(2,1)S(1)}, u32[]{:S(2)}, u32[]{:S(2)}) collective-permute-start(bf16[8,512]{1,0:T(8,128)(2,1)S(1)} %fusion.30.refs_0_), channel_id=1, source_target_pairs={{0,8},{8,0},{16,24},{24,16},{1,9},{9,1},{17,25},{25,17},{2,10},{10... | collective-permute-start | bytes 24584 | tf_op jit(solution)/shard_map/ppermute | solution.py:562
  8.3 5.6 %collective-permute-start.3 = (bf16[8,512]{1,0:T(8,128)(2,1)S(1)}, bf16[8,512]{1,0:T(8,128)(2,1)S(1)}, u32[]{:S(2)}, u32[]{:S(2)}) collective-permute-start(bf16[8,512]{1,0:T(8,128)(2,1)S(1)} %fusion.30.refs_0_), channel_id=1, source_target_pairs={{0,16},{8,24},{16,0},{24,8},{1,17},{9,25},{17,1},{25,9},{2,18},{10... | collective-permute-start | bytes 24584 | tf_op jit(solution)/shard_map/ppermute | solution.py:562
  8.5 5.4 %collective-permute-start.4 = (bf16[8,512]{1,0:T(8,128)(2,1)S(1)}, bf16[8,512]{1,0:T(8,128)(2,1)S(1)}, u32[]{:S(2)}, u32[]{:S(2)}) collective-permute-start(bf16[8,512]{1,0:T(8,128)(2,1)S(1)} %fusion.30.refs_0_), channel_id=1, source_target_pairs={{0,24},{8,16},{16,8},{24,0},{1,25},{9,17},{17,9},{25,1},{2,26},{10... | collective-permute-start | bytes 24584 | tf_op jit(solution)/shard_map/ppermute | solution.py:562
  13.9 19.1 %collective-permute-start.6 = (bf16[192,768]{1,0:T(8,128)(2,1)S(1)}, bf16[192,768]{1,0:T(8,128)(2,1)S(1)}, u32[]{:S(2)}, u32[]{:S(2)}) collective-permute-start(bf16[192,768]{1,0:T(8,128)(2,1)S(1)} %get-tuple-element.95), channel_id=1, source_target_pairs={{0,8},{8,0},{16,24},{24,16},{1,9},{9,1},{17,25},{25,17},{2,10},{10... | collective-permute-start | bytes 884744 | tf_op jit(solution)/shard_map/ppermute | solution.py:562
  14.1 21.9 %collective-permute-start.5 = (bf16[256,768]{1,0:T(8,128)(2,1)S(1)}, bf16[256,768]{1,0:T(8,128)(2,1)S(1)}, u32[]{:S(2)}, u32[]{:S(2)}) collective-permute-start(bf16[256,768]{1,0:T(8,128)(2,1)S(1)} %collective-permute-done.refs_2_), channel_id=1, source_target_pairs={{0,8},{8,0},{16,24},{24,16},{1,9},{9,1},{17,25},{25,17},{2,10},{10... | collective-permute-start | bytes 1179656 | tf_op jit(solution)/shard_map/ppermute | solution.py:562
  14.4 19.7 %collective-permute-start.7 = (bf16[192,768]{1,0:T(8,128)(2,1)S(1)}, bf16[192,768]{1,0:T(8,128)(2,1)S(1)}, u32[]{:S(2)}, u32[]{:S(2)}) collective-permute-start(bf16[192,768]{1,0:T(8,128)(2,1)S(1)} %get-tuple-element.96), channel_id=1, source_target_pairs={{0,16},{8,24},{16,0},{24,8},{1,17},{9,25},{17,1},{25,9},{2,18},{10... | collective-permute-start | bytes 884744 | tf_op jit(solution)/shard_map/ppermute | solution.py:562
  16.2 18.0 %collective-permute-start.8 = (bf16[192,768]{1,0:T(8,128)(2,1)S(1)}, bf16[192,768]{1,0:T(8,128)(2,1)S(1)}, u32[]{:S(2)}, u32[]{:S(2)}) collective-permute-start(bf16[192,768]{1,0:T(8,128)(2,1)S(1)} %get-tuple-element.97), channel_id=1, source_target_pairs={{0,24},{8,16},{16,8},{24,0},{1,25},{9,17},{17,9},{25,1},{2,26},{10... | collective-permute-start | bytes 884744 | tf_op jit(solution)/shard_map/ppermute | solution.py:562
  16.2 16.8 %collective-permute-start.10 = (bf16[192,384]{1,0:T(8,128)(2,1)S(1)}, bf16[192,384]{1,0:T(8,128)(2,1)S(1)}, u32[]{:S(2)}, u32[]{:S(2)}) collective-permute-start(bf16[192,384]{1,0:T(8,128)(2,1)S(1)} %get-tuple-element.98.refs_8_), channel_id=1, source_target_pairs={{0,16},{8,24},{16,0},{24,8},{1,17},{9,25},{17,1},{25,9},{2,18},{10... | collective-permute-start | bytes 442376 | tf_op jit(solution)/shard_map/ppermute | solution.py:562
  33.0 2.9 %collective-permute-start.9 = (bf16[192,384]{1,0:T(8,128)(2,1)S(1)}, bf16[192,384]{1,0:T(8,128)(2,1)S(1)}, u32[]{:S(2)}, u32[]{:S(2)}) collective-permute-start(bf16[192,384]{1,0:T(8,128)(2,1)S(1)} %get-tuple-element.98.refs_8_), channel_id=1, source_target_pairs={{0,8},{8,0},{16,24},{24,16},{1,9},{9,1},{17,25},{25,17},{2,10},{10... | collective-permute-start | bytes 442376 | tf_op jit(solution)/shard_map/ppermute | solution.py:562
  33.0 2.9 %collective-permute-start.11 = (bf16[192,384]{1,0:T(8,128)(2,1)S(1)}, bf16[192,384]{1,0:T(8,128)(2,1)S(1)}, u32[]{:S(2)}, u32[]{:S(2)}) collective-permute-start(bf16[192,384]{1,0:T(8,128)(2,1)S(1)} %collective-permute-done.10.refs_10_), channel_id=1, source_target_pairs={{0,8},{8,0},{16,24},{24,16},{1,9},{9,1},{17,25},{25,17},{2,10},{10... | collective-permute-start | bytes 442376 | tf_op jit(solution)/shard_map/ppermute | solution.py:562
  34.1 14.6 %collective-permute-start.13 = (bf16[256,768]{1,0:T(8,128)(2,1)}, bf16[256,768]{1,0:T(8,128)(2,1)S(1)}, u32[]{:S(2)}, u32[]{:S(2)}) collective-permute-start(bf16[256,768]{1,0:T(8,128)(2,1)} %bitcast.121), channel_id=1, source_target_pairs={{0,16},{8,24},{16,0},{24,8},{1,17},{9,25},{17,1},{25,9},{2,18},{10... | collective-permute-start | bytes 1179656 | tf_op jit(solution)/shard_map/ppermute | solution.py:562
  35.9 13.4 %collective-permute-start.12 = (bf16[256,768]{1,0:T(8,128)(2,1)}, bf16[256,768]{1,0:T(8,128)(2,1)S(1)}, u32[]{:S(2)}, u32[]{:S(2)}) collective-permute-start(bf16[256,768]{1,0:T(8,128)(2,1)} %bitcast.122), channel_id=1, source_target_pairs={{0,8},{8,0},{16,24},{24,16},{1,9},{9,1},{17,25},{25,17},{2,10},{10... | collective-permute-start | bytes 1179656 | tf_op jit(solution)/shard_map/ppermute | solution.py:562
  37.0 13.7 %copy-start.4 = (bf16[384,768]{1,0:T(8,128)(2,1)S(1)}, bf16[384,768]{1,0:T(8,128)(2,1)}, u32[]{:S(2)}) copy-start(bf16[384,768]{1,0:T(8,128)(2,1)} %weight.2) | copy-start | bytes 1769476
  37.0 13.7 %copy-start.5 = (bf16[1,256,768]{2,1,0:T(8,128)(2,1)S(1)}, bf16[1,256,768]{2,1,0:T(8,128)(2,1)}, u32[]{:S(2)}) copy-start(bf16[1,256,768]{2,1,0:T(8,128)(2,1)} %param.13) | copy-start | bytes 1179652
  48.7 7.1 %copy-start.6 = (f32[1024,384]{1,0:T(8,128)}, f32[1024,384]{1,0:T(8,128)S(1)}, u32[]{:S(2)}) copy-start(f32[1024,384]{1,0:T(8,128)S(1)} %get-tuple-element.116.refs_6_.refs_9_) | copy-start | bytes 4718596
  48.7 7.1 %copy-start.8 = (bf16[768,384]{1,0:T(8,128)(2,1)}, bf16[768,384]{1,0:T(8,128)(2,1)S(1)}, u32[]{:S(2)}) copy-start(bf16[768,384]{1,0:T(8,128)(2,1)S(1)} %get-tuple-element.114.refs_4_.wgv) | copy-start | bytes 1769476
  48.7 7.1 %copy-start.10 = (bf16[768,1024]{1,0:T(8,128)(2,1)}, bf16[768,1024]{1,0:T(8,128)(2,1)S(1)}, u32[]{:S(2)}) copy-start(bf16[768,1024]{1,0:T(8,128)(2,1)S(1)} %get-tuple-element.106.refs_8_.refs_0_) | copy-start | bytes 4718596
  48.7 7.1 %copy-start.12 = (bf16[768,768]{1,0:T(8,128)(2,1)}, bf16[768,768]{1,0:T(8,128)(2,1)S(1)}, u32[]{:S(2)}) copy-start(bf16[768,768]{1,0:T(8,128)(2,1)S(1)} %get-tuple-element.128.wv) | copy-start | bytes 3538948
  48.7 7.1 %copy-start.14 = (bf16[1024,384]{1,0:T(8,128)(2,1)}, bf16[1024,384]{1,0:T(8,128)(2,1)S(1)}, u32[]{:S(2)}) copy-start(bf16[1024,384]{1,0:T(8,128)(2,1)S(1)} %get-tuple-element.107.refs_1_.refs_2_) | copy-start | bytes 2359300
  48.7 7.1 %copy-start.16 = (f32[4,384,128]{2,1,0:T(8,128)}, f32[4,384,128]{2,1,0:T(8,128)S(1)}, u32[]{:S(2)}) copy-start(f32[4,384,128]{2,1,0:T(8,128)S(1)} %get-tuple-element.110.refs_6_) | copy-start | bytes 2359300
  48.7 7.1 %copy-start.18 = (bf16[1024,256]{1,0:T(8,128)(2,1)}, bf16[1024,256]{1,0:T(8,128)(2,1)S(1)}, u32[]{:S(2)}) copy-start(bf16[1024,256]{1,0:T(8,128)(2,1)S(1)} %get-tuple-element.108.refs_3_.refs_4_) | copy-start | bytes 1572868
  48.8 1.9 %collective-permute-start.14 = (bf16[256,768]{1,0:T(8,128)(2,1)S(1)}, bf16[256,768]{1,0:T(8,128)(2,1)S(1)}, u32[]{:S(2)}, u32[]{:S(2)}) collective-permute-start(bf16[256,768]{1,0:T(8,128)(2,1)S(1)} %collective-permute-done.13.refs_2_), channel_id=1, source_target_pairs={{0,8},{8,0},{16,24},{24,16},{1,9},{9,1},{17,25},{25,17},{2,10},{10... | collective-permute-start | bytes 1179656 | tf_op jit(solution)/shard_map/ppermute | solution.py:562
  55.9 1.9 %collective-permute-start.15 = (f32[8,1024]{1,0:T(8,128)S(1)}, f32[8,1024]{1,0:T(8,128)S(1)}, u32[]{:S(2)}, u32[]{:S(2)}) collective-permute-start(f32[8,1024]{1,0:T(8,128)S(1)} %get-tuple-element.118.refs_4_), channel_id=1, source_target_pairs={{0,8},{8,0},{16,24},{24,16},{1,9},{9,1},{17,25},{25,17},{2,10},{10... | collective-permute-start | bytes 98312 | tf_op jit(solution)/shard_map/ppermute | solution.py:562
  56.3 4.0 %collective-permute-start.16 = (f32[8,1024]{1,0:T(8,128)S(1)}, f32[8,1024]{1,0:T(8,128)S(1)}, u32[]{:S(2)}, u32[]{:S(2)}) collective-permute-start(f32[8,1024]{1,0:T(8,128)S(1)} %get-tuple-element.118.refs_4_), channel_id=1, source_target_pairs={{0,16},{8,24},{16,0},{24,8},{1,17},{9,25},{17,1},{25,9},{2,18},{10... | collective-permute-start | bytes 98312 | tf_op jit(solution)/shard_map/ppermute | solution.py:562
  56.6 3.7 %collective-permute-start.17 = (f32[8,1024]{1,0:T(8,128)S(1)}, f32[8,1024]{1,0:T(8,128)S(1)}, u32[]{:S(2)}, u32[]{:S(2)}) collective-permute-start(f32[8,1024]{1,0:T(8,128)S(1)} %get-tuple-element.118.refs_4_), channel_id=1, source_target_pairs={{0,24},{8,16},{16,8},{24,0},{1,25},{9,17},{17,9},{25,1},{2,26},{10... | collective-permute-start | bytes 98312 | tf_op jit(solution)/shard_map/ppermute | solution.py:562
  60.3 1.4 copy-start.7
  61.7 1.4 copy-start.11
  71.3 2.2 %copy-start.15 = (bf16[1024,384]{1,0:T(8,128)(2,1)S(1)}, bf16[1024,384]{1,0:T(8,128)(2,1)}, u32[]{:S(2)}) copy-start(bf16[1024,384]{1,0:T(8,128)(2,1)} %copy-done.14) | copy-start | bytes 2359300
  71.4 2.2 %copy-start.17 = (f32[4,384,128]{2,1,0:T(8,128)S(1)}, f32[4,384,128]{2,1,0:T(8,128)}, u32[]{:S(2)}) copy-start(f32[4,384,128]{2,1,0:T(8,128)} %copy-done.16) | copy-start | bytes 2359300
  71.4 2.2 %copy-start.19 = (bf16[1024,256]{1,0:T(8,128)(2,1)S(1)}, bf16[1024,256]{1,0:T(8,128)(2,1)}, u32[]{:S(2)}) copy-start(bf16[1024,256]{1,0:T(8,128)(2,1)} %copy-done.18) | copy-start | bytes 1572868
  71.4 2.1 %copy-start.21 = (f32[1024,128]{1,0:T(8,128)S(1)}, f32[1024,128]{1,0:T(8,128)}, u32[]{:S(2)}) copy-start(f32[1024,128]{1,0:T(8,128)} %copy-done.20) | copy-start | bytes 1572868
  71.4 21.4 %collective-permute-start.19 = (bf16[2,256,768]{2,1,0:T(8,128)(2,1)S(1)}, bf16[2,256,768]{2,1,0:T(8,128)(2,1)S(1)}, u32[]{:S(2)}, u32[]{:S(2)}) collective-permute-start(bf16[2,256,768]{2,1,0:T(8,128)(2,1)S(1)} %slice_bitcast_fusion.2), channel_id=1, source_target_pairs={{0,8},{8,0},{16,24},{24,16},{1,9},{9,1},{17,25},{25,17},{2,10},{10... | collective-permute-start | bytes 2359304 | tf_op jit(solution)/shard_map/ppermute | solution.py:562
  71.7 20.9 %collective-permute-start.18 = (bf16[4,96,768]{2,1,0:T(8,128)(2,1)S(1)}, bf16[4,96,768]{2,1,0:T(8,128)(2,1)S(1)}, u32[]{:S(2)}, u32[]{:S(2)}) collective-permute-start(bf16[4,96,768]{2,1,0:T(8,128)(2,1)S(1)} %slice_bitcast_fusion.4), channel_id=1, source_target_pairs={{0,1},{1,0},{2,3},{3,2},{4,5},{5,4},{6,7},{7,6},{8,9},{9,8},{10,11... | collective-permute-start | bytes 1769480 | tf_op jit(solution)/shard_map/ppermute | solution.py:562
  93.0 10.4 %collective-permute-start.24 = (f32[8,1536]{1,0:T(8,128)S(1)}, f32[8,1536]{1,0:T(8,128)S(1)}, u32[]{:S(2)}, u32[]{:S(2)}) collective-permute-start(f32[8,1536]{1,0:T(8,128)S(1)} %get-tuple-element.131), channel_id=1, source_target_pairs={{0,1},{1,0},{2,3},{3,2},{4,5},{5,4},{6,7},{7,6},{8,9},{9,8},{10,11... | collective-permute-start | bytes 147464 | tf_op jit(solution)/shard_map/ppermute | solution.py:562
  94.3 5.5 %copy-start.9 = (bf16[768,384]{1,0:T(8,128)(2,1)S(1)}, bf16[768,384]{1,0:T(8,128)(2,1)}, u32[]{:S(2)}) copy-start(bf16[768,384]{1,0:T(8,128)(2,1)} %copy-done.8) | copy-start | bytes 1769476
  94.3 5.5 %copy-start.13 = (bf16[768,768]{1,0:T(8,128)(2,1)S(1)}, bf16[768,768]{1,0:T(8,128)(2,1)}, u32[]{:S(2)}) copy-start(bf16[768,768]{1,0:T(8,128)(2,1)} %copy-done.12) | copy-start | bytes 3538948
  94.4 9.1 %collective-permute-start.21 = (bf16[96,768]{1,0:T(8,128)(2,1)S(1)}, bf16[96,768]{1,0:T(8,128)(2,1)S(1)}, u32[]{:S(2)}, u32[]{:S(2)}) collective-permute-start(bf16[96,768]{1,0:T(8,128)(2,1)S(1)} %get-tuple-element.161), channel_id=1, source_target_pairs={{0,2},{1,3},{2,0},{3,1},{4,6},{5,7},{6,4},{7,5},{8,10},{9,11},{10,... | collective-permute-start | bytes 442376 | tf_op jit(solution)/shard_map/ppermute | solution.py:562
  96.0 14.0 %collective-permute-start.22 = (bf16[96,768]{1,0:T(8,128)(2,1)S(1)}, bf16[96,768]{1,0:T(8,128)(2,1)S(1)}, u32[]{:S(2)}, u32[]{:S(2)}) collective-permute-start(bf16[96,768]{1,0:T(8,128)(2,1)S(1)} %get-tuple-element.163), channel_id=1, source_target_pairs={{0,4},{1,5},{2,6},{3,7},{4,0},{5,1},{6,2},{7,3},{8,12},{9,13},{10,... | collective-permute-start | bytes 442376 | tf_op jit(solution)/shard_map/ppermute | solution.py:562
  98.6 11.4 %collective-permute-start.23 = (bf16[96,768]{1,0:T(8,128)(2,1)S(1)}, bf16[96,768]{1,0:T(8,128)(2,1)S(1)}, u32[]{:S(2)}, u32[]{:S(2)}) collective-permute-start(bf16[96,768]{1,0:T(8,128)(2,1)S(1)} %get-tuple-element.162), channel_id=1, source_target_pairs={{0,6},{1,7},{2,4},{3,5},{4,2},{5,3},{6,0},{7,1},{8,14},{9,15},{10,... | collective-permute-start | bytes 442376 | tf_op jit(solution)/shard_map/ppermute | solution.py:562
  99.0 12.3 %collective-permute-start.20 = (bf16[4,4,24,640]{3,2,0,1:T(8,128)(2,1)S(1)}, bf16[4,4,24,640]{3,2,0,1:T(8,128)(2,1)S(1)}, u32[]{:S(2)}, u32[]{:S(2)}) collective-permute-start(bf16[4,4,24,640]{3,2,0,1:T(8,128)(2,1)S(1)} %bitcast.125), channel_id=1, source_target_pairs={{0,1},{1,0},{2,3},{3,2},{4,5},{5,4},{6,7},{7,6},{8,9},{9,8},{10,11... | collective-permute-start | bytes 1474568 | tf_op jit(solution)/shard_map/ppermute | solution.py:562
  111.4 16.8 %collective-permute-start.29 = (bf16[2,256,768]{2,1,0:T(8,128)(2,1)S(1)}, bf16[2,256,768]{2,1,0:T(8,128)(2,1)S(1)}, u32[]{:S(2)}, u32[]{:S(2)}) collective-permute-start(bf16[2,256,768]{2,1,0:T(8,128)(2,1)S(1)} %slice_bitcast_fusion), channel_id=1, source_target_pairs={{0,8},{8,0},{16,24},{24,16},{1,9},{9,1},{17,25},{25,17},{2,10},{10... | collective-permute-start | bytes 2359304 | tf_op jit(solution)/shard_map/ppermute | solution.py:562
  111.5 7.3 %collective-permute-start.28 = (bf16[1,48,768]{2,1,0:T(8,128)(2,1)S(1)}, bf16[1,48,768]{2,1,0:T(8,128)(2,1)S(1)}, u32[]{:S(2)}, u32[]{:S(2)}) collective-permute-start(bf16[1,48,768]{2,1,0:T(8,128)(2,1)S(1)} %slice_bitcast_fusion.14), channel_id=1, source_target_pairs={{0,4},{1,5},{2,6},{3,7},{4,0},{5,1},{6,2},{7,3},{8,12},{9,13},{10,... | collective-permute-start | bytes 221192 | tf_op jit(solution)/shard_map/ppermute | solution.py:562
  113.8 7.8 %collective-permute-start.25 = (bf16[4,24,640]{2,1,0:T(8,128)(2,1)S(1)}, bf16[4,24,640]{2,1,0:T(8,128)(2,1)S(1)}, u32[]{:S(2)}, u32[]{:S(2)}) collective-permute-start(bf16[4,24,640]{2,1,0:T(8,128)(2,1)S(1)} %get-tuple-element.164), channel_id=1, source_target_pairs={{0,2},{1,3},{2,0},{3,1},{4,6},{5,7},{6,4},{7,5},{8,10},{9,11},{10,... | collective-permute-start | bytes 368648 | tf_op jit(solution)/shard_map/ppermute | solution.py:562
  115.8 12.4 %collective-permute-start.26 = (bf16[4,24,640]{2,1,0:T(8,128)(2,1)S(1)}, bf16[4,24,640]{2,1,0:T(8,128)(2,1)S(1)}, u32[]{:S(2)}, u32[]{:S(2)}) collective-permute-start(bf16[4,24,640]{2,1,0:T(8,128)(2,1)S(1)} %get-tuple-element.166), channel_id=1, source_target_pairs={{0,4},{1,5},{2,6},{3,7},{4,0},{5,1},{6,2},{7,3},{8,12},{9,13},{10,... | collective-permute-start | bytes 368648 | tf_op jit(solution)/shard_map/ppermute | solution.py:562
  115.8 12.4 %collective-permute-start.27 = (bf16[4,24,640]{2,1,0:T(8,128)(2,1)S(1)}, bf16[4,24,640]{2,1,0:T(8,128)(2,1)S(1)}, u32[]{:S(2)}, u32[]{:S(2)}) collective-permute-start(bf16[4,24,640]{2,1,0:T(8,128)(2,1)S(1)} %get-tuple-element.165), channel_id=1, source_target_pairs={{0,6},{1,7},{2,4},{3,5},{4,2},{5,3},{6,0},{7,1},{8,14},{9,15},{10,... | collective-permute-start | bytes 368648 | tf_op jit(solution)/shard_map/ppermute | solution.py:562
  128.5 7.2 %collective-permute-start.33 = (bf16[2,48,768]{2,1,0:T(8,128)(2,1)S(1)}, bf16[2,48,768]{2,1,0:T(8,128)(2,1)S(1)}, u32[]{:S(2)}, u32[]{:S(2)}) collective-permute-start(bf16[2,48,768]{2,1,0:T(8,128)(2,1)S(1)} %pad_maximum_fusion.4), channel_id=1, source_target_pairs={{0,2},{1,3},{2,0},{3,1},{4,6},{5,7},{6,4},{7,5},{8,10},{9,11},{10,... | collective-permute-start | bytes 442376 | tf_op jit(solution)/shard_map/ppermute | solution.py:562
  130.6 5.0 %collective-permute-start.32 = (bf16[24,1024]{1,0:T(8,128)(2,1)S(1)}, bf16[24,1024]{1,0:T(8,128)(2,1)S(1)}, u32[]{:S(2)}, u32[]{:S(2)}) collective-permute-start(bf16[24,1024]{1,0:T(8,128)(2,1)S(1)} %pad_maximum_fusion.8), channel_id=1, source_target_pairs={{0,24},{8,16},{16,8},{24,0},{1,25},{9,17},{17,9},{25,1},{2,26},{10... | collective-permute-start | bytes 147464 | tf_op jit(solution)/shard_map/ppermute | solution.py:562
  130.8 4.8 %collective-permute-start.31 = (bf16[24,1024]{1,0:T(8,128)(2,1)S(1)}, bf16[24,1024]{1,0:T(8,128)(2,1)S(1)}, u32[]{:S(2)}, u32[]{:S(2)}) collective-permute-start(bf16[24,1024]{1,0:T(8,128)(2,1)S(1)} %pad_maximum_fusion.7), channel_id=1, source_target_pairs={{0,16},{8,24},{16,0},{24,8},{1,17},{9,25},{17,1},{25,9},{2,18},{10... | collective-permute-start | bytes 147464 | tf_op jit(solution)/shard_map/ppermute | solution.py:562
  132.3 1.9 %collective-permute-start.30 = (bf16[24,1024]{1,0:T(8,128)(2,1)S(1)}, bf16[24,1024]{1,0:T(8,128)(2,1)S(1)}, u32[]{:S(2)}, u32[]{:S(2)}) collective-permute-start(bf16[24,1024]{1,0:T(8,128)(2,1)S(1)} %pad_maximum_fusion.6), channel_id=1, source_target_pairs={{0,8},{8,0},{16,24},{24,16},{1,9},{9,1},{17,25},{25,17},{2,10},{10... | collective-permute-start | bytes 147464 | tf_op jit(solution)/shard_map/ppermute | solution.py:562
  132.6 18.9 %collective-permute-start.39 = (bf16[256,768]{1,0:T(8,128)(2,1)S(1)}, bf16[256,768]{1,0:T(8,128)(2,1)S(1)}, u32[]{:S(2)}, u32[]{:S(2)}) collective-permute-start(bf16[256,768]{1,0:T(8,128)(2,1)S(1)} %slice_bitcast_fusion.6), channel_id=1, source_target_pairs={{0,16},{8,24},{16,0},{24,8},{1,17},{9,25},{17,1},{25,9},{2,18},{10... | collective-permute-start | bytes 1179656 | tf_op jit(solution)/shard_map/ppermute | solution.py:562
  135.7 20.3 %copy-start.3 = (bf16[1,256,768]{2,1,0:T(8,128)(2,1)S(1)}, bf16[1,256,768]{2,1,0:T(8,128)(2,1)}, u32[]{:S(2)}) copy-start(bf16[1,256,768]{2,1,0:T(8,128)(2,1)} %param.12) | copy-start | bytes 1179652
  135.8 8.8 %collective-permute-start.35 = (bf16[1,24,3328]{2,1,0:T(8,128)(2,1)S(1)}, bf16[1,24,3328]{2,1,0:T(8,128)(2,1)S(1)}, u32[]{:S(2)}, u32[]{:S(2)}) collective-permute-start(bf16[1,24,3328]{2,1,0:T(8,128)(2,1)S(1)} %bitcast.126), channel_id=1, source_target_pairs={{0,2},{1,3},{2,0},{3,1},{4,6},{5,7},{6,4},{7,5},{8,10},{9,11},{10,... | collective-permute-start | bytes 479240 | tf_op jit(solution)/shard_map/ppermute | solution.py:562
  135.9 15.5 %collective-permute-start.36 = (bf16[1,24,3328]{2,1,0:T(8,128)(2,1)S(1)}, bf16[1,24,3328]{2,1,0:T(8,128)(2,1)S(1)}, u32[]{:S(2)}, u32[]{:S(2)}) collective-permute-start(bf16[1,24,3328]{2,1,0:T(8,128)(2,1)S(1)} %bitcast.127), channel_id=1, source_target_pairs={{0,4},{1,5},{2,6},{3,7},{4,0},{5,1},{6,2},{7,3},{8,12},{9,13},{10,... | collective-permute-start | bytes 479240 | tf_op jit(solution)/shard_map/ppermute | solution.py:562
  139.6 11.9 %collective-permute-start.37 = (bf16[1,24,3328]{2,1,0:T(8,128)(2,1)S(1)}, bf16[1,24,3328]{2,1,0:T(8,128)(2,1)S(1)}, u32[]{:S(2)}, u32[]{:S(2)}) collective-permute-start(bf16[1,24,3328]{2,1,0:T(8,128)(2,1)S(1)} %bitcast.128), channel_id=1, source_target_pairs={{0,6},{1,7},{2,4},{3,5},{4,2},{5,3},{6,0},{7,1},{8,14},{9,15},{10,... | collective-permute-start | bytes 479240 | tf_op jit(solution)/shard_map/ppermute | solution.py:562
  140.2 11.3 %collective-permute-start.38 = (bf16[4,48,768]{2,1,0:T(8,128)(2,1)S(1)}, bf16[4,48,768]{2,1,0:T(8,128)(2,1)S(1)}, u32[]{:S(2)}, u32[]{:S(2)}) collective-permute-start(bf16[4,48,768]{2,1,0:T(8,128)(2,1)S(1)} %pad_maximum_fusion.3), channel_id=1, source_target_pairs={{0,1},{1,0},{2,3},{3,2},{4,5},{5,4},{6,7},{7,6},{8,9},{9,8},{10,11... | collective-permute-start | bytes 884744 | tf_op jit(solution)/shard_map/ppermute | solution.py:562
  144.6 20.0 %collective-permute-start.34 = (bf16[256,768]{1,0:T(8,128)(2,1)S(1)}, bf16[256,768]{1,0:T(8,128)(2,1)S(1)}, u32[]{:S(2)}, u32[]{:S(2)}) collective-permute-start(bf16[256,768]{1,0:T(8,128)(2,1)S(1)} %slice_bitcast_fusion.7), channel_id=1, source_target_pairs={{0,16},{8,24},{16,0},{24,8},{1,17},{9,25},{17,1},{25,9},{2,18},{10... | collective-permute-start | bytes 1179656 | tf_op jit(solution)/shard_map/ppermute | solution.py:562
  151.6 5.8 %collective-permute-start.41 = (f32[8,1536]{1,0:T(8,128)S(1)}, f32[8,1536]{1,0:T(8,128)S(1)}, u32[]{:S(2)}, u32[]{:S(2)}) collective-permute-start(f32[8,1536]{1,0:T(8,128)S(1)} %add.85), channel_id=1, source_target_pairs={{0,4},{1,5},{2,6},{3,7},{4,0},{5,1},{6,2},{7,3},{8,12},{9,13},{10,... | collective-permute-start | bytes 147464 | tf_op jit(solution)/shard_map/ppermute | solution.py:562
  155.3 14.8 %collective-permute-start.40 = (bf16[4,24,3328]{2,1,0:T(8,128)(2,1)S(1)}, bf16[4,24,3328]{2,1,0:T(8,128)(2,1)S(1)}, u32[]{:S(2)}, u32[]{:S(2)}) collective-permute-start(bf16[4,24,3328]{2,1,0:T(8,128)(2,1)S(1)} %pad_maximum_fusion.1), channel_id=1, source_target_pairs={{0,1},{1,0},{2,3},{3,2},{4,5},{5,4},{6,7},{7,6},{8,9},{9,8},{10,11... | collective-permute-start | bytes 1916936 | tf_op jit(solution)/shard_map/ppermute | solution.py:562
  157.3 4.2 %collective-permute-start.42 = (f32[8,1536]{1,0:T(8,128)S(1)}, f32[8,1536]{1,0:T(8,128)S(1)}, u32[]{:S(2)}, u32[]{:S(2)}) collective-permute-start(f32[8,1536]{1,0:T(8,128)S(1)} %add.99), channel_id=1, source_target_pairs={{0,2},{1,3},{2,0},{3,1},{4,6},{5,7},{6,4},{7,5},{8,10},{9,11},{10,... | collective-permute-start | bytes 147464 | tf_op jit(solution)/shard_map/ppermute | solution.py:562
  161.5 1.3 collective-permute-start.43
  162.8 4.9 %collective-permute-start.44 = (f32[8,3072]{1,0:T(8,128)S(1)}, f32[8,3072]{1,0:T(8,128)S(1)}, u32[]{:S(2)}, u32[]{:S(2)}) collective-permute-start(f32[8,3072]{1,0:T(8,128)S(1)} %pad_maximum_fusion.5), channel_id=1, source_target_pairs={{0,16},{8,24},{16,0},{24,8},{1,17},{9,25},{17,1},{25,9},{2,18},{10... | collective-permute-start | bytes 294920 | tf_op jit(solution)/shard_map/ppermute | solution.py:562
  165.9 4.3 %copy-start.1 = (bf16[192,3352]{1,0:T(8,128)(2,1)S(1)}, bf16[192,3352]{1,0:T(8,128)(2,1)}, u32[]{:S(2)}) copy-start(bf16[192,3352]{1,0:T(8,128)(2,1)} %refs_2_.1) | copy-start | bytes 3861508
  (3 other events, 3.1 us)
